TPU v7x, 32 devices: a whole 2x2x4 slice. The times are simulated.
32 devices in a mesh: mem: 2 (over core), tile: 16 (over z, y, x).
Axes of the slice: x: 2, y: 2, z: 4, core: 2. Of those that a mesh axis runs over, the one named last changes fastest.
Arguments:
- anomalies: bfloat16 [64, 256, 512], P('tile', 'mem'), may hold values from -6 to 6
- innovations: bfloat16 [128, 256, 512], P('tile', 'mem'), may hold values from -3 to 3
- obs_tile: int32 [128], P('tile'), may hold values from 0 to 63, as said below
- pair_tiles: int32 [128, 2], P('tile'), may hold values from 0 to 63, as said below
- loc_bin: int32 [128], P('tile'), may hold values from 0 to 4
Outputs:
- analysis: bfloat16 [64, 256, 512], P('tile', 'mem')
Inputs may be any that keep to these rules, and one draw needn't show every extreme that they name: Block o lies in a tile of its own index of tile: obs_tile[o] // 4 == o // 8. `pair_tiles`: slot k's first tile i has i // 4 == k // 8; its second tile j differs from i and j // 4 - i // 4 lies in 0 to 2, equal to 2 for some slot. Pairs may repeat. `loc_bin`: bin 4 marks an empty slot.
All inputs are finite; a program needn't handle non-finite values.
Results may differ from a plain program's by a relative error of at most 0.0051.
Values may be sent and summed in bfloat16 or wider, within the bound.
No kernel may reach another device: no remote copies, remote signals or barrier semaphores. Data moves between devices by JAX's collectives and lax.ppermute only.
A program may use at most 128 MiB of HBM per device.

v0:
```python
import jax
import jax.numpy as jnp
from jax import lax
from jax.sharding import PartitionSpec as P

MEMBERS = 256
HOPS = 2
NBIN = 4
RADIUS = 4


def from_behind(shard, axis, by):
    size = lax.axis_size(axis)
    pairs = [(i, i + by) for i in range(size) if 0 <= i + by < size]
    return lax.ppermute(shard, axis, pairs)


def weights_for(bins, points):
    positions = jnp.arange(points, dtype=jnp.int32)
    column = (positions % 32).astype(jnp.float32)
    levels = (positions // 32).astype(jnp.float32)
    along = (
        0.5 * RADIUS * bins.astype(jnp.float32)[:, None, None]
        + column[None, None, :]
        - column[None, :, None]
    )
    across = levels[None, None, :] - levels[None, :, None]
    weight = jnp.exp(-(along * along + across * across) / (2.0 * RADIUS * RADIUS))
    return jnp.where(bins[:, None, None] < NBIN, weight, 0.0)


def per_device(anomalies, innovations, obs_tile, pair_tiles, loc_bin):
    tile_count = anomalies.shape[0]
    points = anomalies.shape[2]
    tile_base = lax.axis_index("tile") * tile_count
    local_ids = jnp.arange(tile_count, dtype=jnp.int32)
    obs_onehot = (obs_tile[:, None] - tile_base == local_ids[None, :]).astype(jnp.bfloat16)
    forcing = jnp.einsum(
        "ot,omp->tmp", obs_onehot, innovations, preferred_element_type=jnp.float32
    ).astype(jnp.bfloat16)
    window_a = [anomalies]
    window_g = [forcing]
    for distance in range(1, HOPS + 1):
        fetched_a, fetched_g = from_behind((anomalies, forcing), "tile", -distance)
        window_a.append(fetched_a)
        window_g.append(fetched_g)
    window_a = jnp.concatenate(window_a, axis=0)
    window_g = jnp.concatenate(window_g, axis=0)
    first_local = pair_tiles[:, 0] - tile_base
    second_local = pair_tiles[:, 1] - tile_base
    whole_window = lax.all_gather(window_a, "mem", axis=1, tiled=True)
    first_a = jnp.take(whole_window, first_local, axis=0)
    second_a = jnp.take(whole_window, second_local, axis=0)
    cross = jnp.einsum("kmp,kmq->kpq", first_a, second_a, preferred_element_type=jnp.float32)
    own_whole = whole_window[:tile_count]
    self_cross = jnp.einsum(
        "tmp,tmq->tpq", own_whole, own_whole, preferred_element_type=jnp.float32
    )
    covar = (weights_for(loc_bin, points) * cross / (MEMBERS - 1)).astype(jnp.bfloat16)
    zero_bins = jnp.zeros((tile_count,), jnp.int32)
    own_covar = (weights_for(zero_bins, points) * self_cross / (MEMBERS - 1)).astype(jnp.bfloat16)
    first_g = jnp.take(forcing, first_local, axis=0)
    second_g = jnp.take(window_g, second_local, axis=0)
    to_first = jnp.einsum("kmq,kpq->kmp", second_g, covar, preferred_element_type=jnp.float32)
    to_second = jnp.einsum("kmp,kpq->kmq", first_g, covar, preferred_element_type=jnp.float32)
    first_onehot = (first_local[:, None] == local_ids[None, :]).astype(jnp.float32)
    window_ids = jnp.arange(window_a.shape[0], dtype=jnp.int32)
    second_onehot = (second_local[:, None] == window_ids[None, :]).astype(jnp.float32)
    own_total = jnp.einsum("tmq,tpq->tmp", forcing, own_covar, preferred_element_type=jnp.float32)
    own_total = own_total + jnp.einsum(
        "kt,kmp->tmp", first_onehot, to_first, precision=lax.Precision.HIGHEST
    )
    window_total = jnp.einsum(
        "kw,kmp->wmp", second_onehot, to_second, precision=lax.Precision.HIGHEST
    )
    own_total = own_total + window_total[:tile_count]
    for distance in range(1, HOPS + 1):
        block = window_total[distance * tile_count : (distance + 1) * tile_count]
        own_total = own_total + from_behind(block, "tile", distance)
    return (anomalies.astype(jnp.float32) + own_total).astype(jnp.bfloat16)


def solution(mesh):
    return jax.shard_map(
        per_device,
        mesh=mesh,
        in_specs=(
            P("tile", "mem", None),
            P("tile", "mem", None),
            P("tile"),
            P("tile", None),
            P("tile"),
        ),
        out_specs=P("tile", "mem", None),
        check_vma=False,
    )
```

profile of v0, /device:TPU:8, one launch (start us, length us, event | category | flops | bytes accessed | tf_op | source)
XLA Modules:
  0.0 150.4 jit_solution(5541628640274213207)
XLA Ops:
  6.5 0.0 copy-start
  6.5 0.0 all-gather.2.cloned.1.call-start
  6.5 4.4 %collective-permute-start = (bf16[4,128,512]{2,1,0:T(8,128)(2,1)}, bf16[4,128,512]{2,1,0:T(8,128)(2,1)S(1)}, u32[]{:S(2)}, u32[]{:S(2)}) collective-permute-start(bf16[4,128,512]{2,1,0:T(8,128)(2,1)} %param.7), channel_id=1, source_target_pairs={{1,0},{2,1},{3,2},{4,3},{5,4},{6,5},{7,6},{8,7},{9,8},{10,9},{11,1... | collective-permute-start | bytes 1572872 | tf_op jit(solution)/shard_map/ppermute | solution.py:15
  10.9 2.4 %collective-permute-start.1 = (bf16[4,128,512]{2,1,0:T(8,128)(2,1)}, bf16[4,128,512]{2,1,0:T(8,128)(2,1)S(1)}, u32[]{:S(2)}, u32[]{:S(2)}) collective-permute-start(bf16[4,128,512]{2,1,0:T(8,128)(2,1)} %param.7), channel_id=1, source_target_pairs={{2,0},{3,1},{4,2},{5,3},{6,4},{7,5},{8,6},{9,7},{10,8},{11,9},{12,... | collective-permute-start | bytes 1572872 | tf_op jit(solution)/shard_map/ppermute | solution.py:15
  13.3 0.7 broadcast_subtract_fusion
  14.0 0.0 copy-start.6
  14.0 0.0 copy-start.7
  14.0 15.1 %collective-permute-done = bf16[4,128,512]{2,1,0:T(8,128)(2,1)S(1)} collective-permute-done((bf16[4,128,512]{2,1,0:T(8,128)(2,1)}, bf16[4,128,512]{2,1,0:T(8,128)(2,1)S(1)}, u32[]{:S(2)}, u32[]{:S(2)}) %collective-permute-start) | collective-permute-done | bytes 524320 | tf_op jit(solution)/shard_map/ppermute | solution.py:15
  29.1 10.1 %collective-permute-done.1 = bf16[4,128,512]{2,1,0:T(8,128)(2,1)S(1)} collective-permute-done((bf16[4,128,512]{2,1,0:T(8,128)(2,1)}, bf16[4,128,512]{2,1,0:T(8,128)(2,1)S(1)}, u32[]{:S(2)}, u32[]{:S(2)}) %collective-permute-start.1) | collective-permute-done | bytes 524320 | tf_op jit(solution)/shard_map/ppermute | solution.py:15
  39.2 2.4 %pad_maximum_fusion.1 = bf16[12,128,512]{2,1,0:T(8,128)(2,1)} fusion(bf16[4,128,512]{2,1,0:T(8,128)(2,1)S(1)} %collective-permute-done.1, bf16[4,128,512]{2,1,0:T(8,128)(2,1)S(1)} %collective-permute-done, bf16[4,128,512]{2,1,0:T(8,128)(2,1)} %param.7), kind=kLoop, calls=%fused_computation.15 | loop fusion | flops 1572864 | bytes 3145728 | tf_op jit(solution)/shard_map/concatenate | solution.py:47
  41.6 0.0 all-gather.2.cloned.1.call-update
  41.6 0.0 copy-done
  41.6 0.7 convolution_convert_fusion
  42.4 5.2 %collective-permute-start.3 = (bf16[4,128,512]{2,0,1:T(4,128)(2,1)S(1)}, bf16[4,128,512]{2,0,1:T(4,128)(2,1)S(1)}, u32[]{:S(2)}, u32[]{:S(2)}) collective-permute-start(bf16[4,128,512]{2,0,1:T(4,128)(2,1)S(1)} %convolution_convert_fusion), channel_id=1, source_target_pairs={{2,0},{3,1},{4,2},{5,3},{6,4},{7,5},{8,6},{9,7},{10,8},{11,9},{12,... | collective-permute-start | bytes 1572872 | tf_op jit(solution)/shard_map/ppermute | solution.py:15
  47.6 1.9 %collective-permute-start.2 = (bf16[4,128,512]{2,0,1:T(4,128)(2,1)S(1)}, bf16[4,128,512]{2,0,1:T(4,128)(2,1)S(1)}, u32[]{:S(2)}, u32[]{:S(2)}) collective-permute-start(bf16[4,128,512]{2,0,1:T(4,128)(2,1)S(1)} %convolution_convert_fusion), channel_id=1, source_target_pairs={{1,0},{2,1},{3,2},{4,3},{5,4},{6,5},{7,6},{8,7},{9,8},{10,9},{11,1... | collective-permute-start | bytes 1572872 | tf_op jit(solution)/shard_map/ppermute | solution.py:15
  49.5 0.0 copy-done.6
  49.6 0.0 copy-done.7
  49.7 0.1 copy.14
  49.8 1.7 %gather_fusion.1 = bf16[8,128,512]{2,1,0:T(8,128)(2,1)} fusion(bf16[4,128,512]{2,1,0:T(8,128)(2,1)S(1)} %copy.14, s32[1024]{0:T(1024)S(1)} %pad_clamp_fusion), kind=kCustom, calls=%fused_computation.3 | custom fusion | bytes 2097184 | tf_op jit(solution)/shard_map/jit(_take)/gather | solution.py:62
  51.5 0.1 broadcast_add_fusion
  51.5 1.1 subtract_multiply_fusion
  52.7 7.3 %collective-permute-done.3 = bf16[4,128,512]{2,0,1:T(4,128)(2,1)S(1)} collective-permute-done((bf16[4,128,512]{2,0,1:T(4,128)(2,1)S(1)}, bf16[4,128,512]{2,0,1:T(4,128)(2,1)S(1)}, u32[]{:S(2)}, u32[]{:S(2)}) %collective-permute-start.3) | collective-permute-done | bytes 524320 | tf_op jit(solution)/shard_map/ppermute | solution.py:15
  59.9 9.2 %collective-permute-done.2 = bf16[4,128,512]{2,0,1:T(4,128)(2,1)S(1)} collective-permute-done((bf16[4,128,512]{2,0,1:T(4,128)(2,1)S(1)}, bf16[4,128,512]{2,0,1:T(4,128)(2,1)S(1)}, u32[]{:S(2)}, u32[]{:S(2)}) %collective-permute-start.2) | collective-permute-done | bytes 524320 | tf_op jit(solution)/shard_map/ppermute | solution.py:15
  69.1 1.1 pad_maximum_fusion
  70.2 0.9 copy.15
  71.1 1.7 %gather_fusion = bf16[8,128,512]{2,1,0:T(8,128)(2,1)} fusion(bf16[12,128,512]{2,1,0:T(8,128)(2,1)S(1)} %copy.15, s32[1024]{0:T(1024)S(1)} %pad_clamp_fusion.3), kind=kCustom, calls=%fused_computation.2 | custom fusion | bytes 2097184 | tf_op jit(solution)/shard_map/jit(_take)/gather | solution.py:63
  72.7 0.0 all-gather.2.cloned.1.call-done
  72.8 3.9 %gather_fusion.3 = bf16[8,256,512]{2,1,0:T(8,128)(2,1)} fusion(bf16[12,256,512]{2,1,0:T(8,128)(2,1)} %all-gather.2.cloned.1.call-done, s32[1024]{0:T(1024)S(1)} %pad_clamp_fusion.1), kind=kCustom, calls=%fused_computation.1.clone | custom fusion | bytes 4194336 | tf_op jit(solution)/shard_map/jit(_take)/gather | solution.py:53
  76.7 0.0 copy-start.5
  76.7 4.0 %gather_fusion.2 = bf16[8,256,512]{2,1,0:T(8,128)(2,1)} fusion(bf16[12,256,512]{2,1,0:T(8,128)(2,1)} %all-gather.2.cloned.1.call-done, s32[1024]{0:T(1024)S(1)} %pad_clamp_fusion.2), kind=kCustom, calls=%fused_computation.clone | custom fusion | bytes 4194336 | tf_op jit(solution)/shard_map/jit(_take)/gather | solution.py:52
  80.7 0.0 copy-done.5
  80.7 0.0 copy-start.3
  80.7 5.9 %multiply_convert_fusion = bf16[8,512,512]{2,1,0:T(8,128)(2,1)S(1)} fusion(f32[512,512]{1,0:T(8,128)S(1)} %copy-done.5, f32[512]{0:T(512)S(1)} %fusion.26, f32[8,512]{1,0:T(8,128)S(1)} %broadcast_add_fusion, pred[8]{0:T(512)(128)(4,1)S(1)} %broadcast_compare_fusion, bf16[8,256,512]{2,1,0:T(8,128)(2,1)} %gather_fusion.3, ...), kind=kOutput, calls=%fused_computation.4 | convolution fusion | flops 1094713344 | bytes 9455640 | tf_op jit(solution)/shard_map/kmp,kmq->kpq/dot_general | solution.py:54
  86.5 0.0 copy-done.3
  86.6 0.8 fusion.16
  87.3 2.8 %fusion = f32[12,128,512]{2,0,1:T(8,128)S(1)} fusion(f32[8,128,512]{2,1,0:T(8,128)S(1)} %fusion.16, s32[8]{0:T(128)S(1)} %bitcast.29), kind=kOutput, calls=%fused_computation.7 | convolution fusion | flops 75497568 | bytes 5242912 | tf_op jit(solution)/shard_map/kw,kmp->wmp/dot_general | solution.py:73
  90.2 0.6 fusion.46
  90.7 0.0 copy-start.2
  90.7 0.3 copy.26
  91.1 0.3 copy.27
  91.4 1.9 %collective-permute-start.5 = (f32[4,128,512]{2,1,0:T(8,128)S(1)}, f32[4,128,512]{2,1,0:T(8,128)S(1)}, u32[]{:S(2)}, u32[]{:S(2)}) collective-permute-start(f32[4,128,512]{2,1,0:T(8,128)S(1)} %copy.27), channel_id=1, source_target_pairs={{0,2},{1,3},{2,4},{3,5},{4,6},{5,7},{6,8},{7,9},{8,10},{9,11},{10,... | collective-permute-start | bytes 3145736 | tf_op jit(solution)/shard_map/ppermute | solution.py:15
  93.4 7.0 %collective-permute-start.4 = (f32[4,128,512]{2,1,0:T(8,128)S(1)}, f32[4,128,512]{2,1,0:T(8,128)S(1)}, u32[]{:S(2)}, u32[]{:S(2)}) collective-permute-start(f32[4,128,512]{2,1,0:T(8,128)S(1)} %copy.26), channel_id=1, source_target_pairs={{0,1},{1,2},{2,3},{3,4},{4,5},{5,6},{6,7},{7,8},{8,9},{9,10},{10,1... | collective-permute-start | bytes 3145736 | tf_op jit(solution)/shard_map/ppermute | solution.py:15
  100.4 0.0 copy-done.2
  100.4 1.5 fusion.18
  101.9 0.0 copy-start.1
  101.9 2.2 %fusion.2 = f32[4,128,512]{2,0,1:T(4,128)S(1)} fusion(f32[8,128,512]{2,1,0:T(8,128)S(1)} %fusion.18, s32[8]{0:T(128)S(1)} %bitcast.30), kind=kOutput, calls=%fused_computation.9 | convolution fusion | flops 25165856 | bytes 3145760 | tf_op jit(solution)/shard_map/kt,kmp->tmp/dot_general | solution.py:70
  104.1 0.0 copy-done.1
  104.1 0.0 copy-start.4
  104.2 1.2 multiply_convert_fusion.1
  105.4 31.3 %collective-permute-done.5 = f32[4,128,512]{2,1,0:T(8,128)S(1)} collective-permute-done((f32[4,128,512]{2,1,0:T(8,128)S(1)}, f32[4,128,512]{2,1,0:T(8,128)S(1)}, u32[]{:S(2)}, u32[]{:S(2)}) %collective-permute-start.5) | collective-permute-done | bytes 1048608 | tf_op jit(solution)/shard_map/ppermute | solution.py:15
  136.7 4.7 %collective-permute-done.4 = f32[4,128,512]{2,1,0:T(8,128)S(1)} collective-permute-done((f32[4,128,512]{2,1,0:T(8,128)S(1)}, f32[4,128,512]{2,1,0:T(8,128)S(1)}, u32[]{:S(2)}, u32[]{:S(2)}) %collective-permute-start.4) | collective-permute-done | bytes 1048608 | tf_op jit(solution)/shard_map/ppermute | solution.py:15
  141.4 0.0 copy-done.4
  141.4 2.1 %fusion.12 = bf16[4,128,512]{2,1,0:T(8,128)(2,1)} fusion(f32[4,128,512]{2,1,0:T(8,128)S(1)} %collective-permute-done.5, f32[4,128,512]{2,1,0:T(8,128)S(1)} %collective-permute-done.4, bf16[4,512,512]{2,1,0:T(8,128)(2,1)S(1)} %multiply_convert_fusion.1, f32[4,128,512]{2,0,1:T(4,128)S(1)} %get-tuple-element.10, f32[4,128,512]{2,0,1:T(4,128)S(1)} %fusion.2, ...), kind=kOutput, calls=%fused_computation.21 | convolution fusion | flops 270270464 | bytes 7864320 | tf_op jit(solution)/shard_map/tmq,tpq->tmp/dot_general | solution.py:69
  (13 shorter events, 0.1 us)
Async XLA Ops:
  6.5 35.1 %copy-start = (bf16[8,128,512]{2,1,0:T(8,128)(2,1)S(1)}, bf16[8,128,512]{2,1,0:T(8,128)(2,1)}, u32[]{:S(2)}) copy-start(bf16[8,128,512]{2,1,0:T(8,128)(2,1)} %param.8) | copy-start | bytes 3145732
  6.5 66.2 %all-gather.2.cloned.1.call-start = ((), (), s32[]{:S(2)}) async-start(), calls=%async_computation | async-start | bytes 4718592 | tf_op jit(solution)/shard_map/all_gather | solution.py:51
  6.5 22.6 %collective-permute-start = (bf16[4,128,512]{2,1,0:T(8,128)(2,1)}, bf16[4,128,512]{2,1,0:T(8,128)(2,1)S(1)}, u32[]{:S(2)}, u32[]{:S(2)}) collective-permute-start(bf16[4,128,512]{2,1,0:T(8,128)(2,1)} %param.7), channel_id=1, source_target_pairs={{1,0},{2,1},{3,2},{4,3},{5,4},{6,5},{7,6},{8,7},{9,8},{10,9},{11,1... | collective-permute-start | bytes 1572872 | tf_op jit(solution)/shard_map/ppermute | solution.py:15
  10.9 28.3 %collective-permute-start.1 = (bf16[4,128,512]{2,1,0:T(8,128)(2,1)}, bf16[4,128,512]{2,1,0:T(8,128)(2,1)S(1)}, u32[]{:S(2)}, u32[]{:S(2)}) collective-permute-start(bf16[4,128,512]{2,1,0:T(8,128)(2,1)} %param.7), channel_id=1, source_target_pairs={{2,0},{3,1},{4,2},{5,3},{6,4},{7,5},{8,6},{9,7},{10,8},{11,9},{12,... | collective-permute-start | bytes 1572872 | tf_op jit(solution)/shard_map/ppermute | solution.py:15
  14.0 35.5 %copy-start.6 = (s32[8,2]{0,1:T(2,128)S(1)}, s32[8,2]{0,1:T(2,128)}, u32[]{:S(2)}) copy-start(s32[8,2]{0,1:T(2,128)} %param.10) | copy-start | bytes 196
  14.0 35.6 %copy-start.7 = (s32[8]{0:T(128)S(1)}, s32[8]{0:T(128)}, u32[]{:S(2)}) copy-start(s32[8]{0:T(128)} %param.11) | copy-start | bytes 100
  42.4 17.5 %collective-permute-start.3 = (bf16[4,128,512]{2,0,1:T(4,128)(2,1)S(1)}, bf16[4,128,512]{2,0,1:T(4,128)(2,1)S(1)}, u32[]{:S(2)}, u32[]{:S(2)}) collective-permute-start(bf16[4,128,512]{2,0,1:T(4,128)(2,1)S(1)} %convolution_convert_fusion), channel_id=1, source_target_pairs={{2,0},{3,1},{4,2},{5,3},{6,4},{7,5},{8,6},{9,7},{10,8},{11,9},{12,... | collective-permute-start | bytes 1572872 | tf_op jit(solution)/shard_map/ppermute | solution.py:15
  47.6 21.5 %collective-permute-start.2 = (bf16[4,128,512]{2,0,1:T(4,128)(2,1)S(1)}, bf16[4,128,512]{2,0,1:T(4,128)(2,1)S(1)}, u32[]{:S(2)}, u32[]{:S(2)}) collective-permute-start(bf16[4,128,512]{2,0,1:T(4,128)(2,1)S(1)} %convolution_convert_fusion), channel_id=1, source_target_pairs={{1,0},{2,1},{3,2},{4,3},{5,4},{6,5},{7,6},{8,7},{9,8},{10,9},{11,1... | collective-permute-start | bytes 1572872 | tf_op jit(solution)/shard_map/ppermute | solution.py:15
  76.7 4.0 %copy-start.5 = (f32[512,512]{1,0:T(8,128)S(1)}, f32[512,512]{1,0:T(8,128)}, u32[]{:S(2)}) copy-start(f32[512,512]{1,0:T(8,128)} %subtract_multiply_fusion) | copy-start | bytes 3145732
  80.7 5.9 %copy-start.3 = (bf16[8,128,512]{2,1,0:T(8,128)(2,1)S(1)}, bf16[8,128,512]{2,1,0:T(8,128)(2,1)}, u32[]{:S(2)}) copy-start(bf16[8,128,512]{2,1,0:T(8,128)(2,1)} %gather_fusion.1) | copy-start | bytes 3145732
  90.7 9.7 %copy-start.2 = (bf16[8,128,512]{2,1,0:T(8,128)(2,1)S(1)}, bf16[8,128,512]{2,1,0:T(8,128)(2,1)}, u32[]{:S(2)}) copy-start(bf16[8,128,512]{2,1,0:T(8,128)(2,1)} %gather_fusion) | copy-start | bytes 3145732
  91.4 45.3 %collective-permute-start.5 = (f32[4,128,512]{2,1,0:T(8,128)S(1)}, f32[4,128,512]{2,1,0:T(8,128)S(1)}, u32[]{:S(2)}, u32[]{:S(2)}) collective-permute-start(f32[4,128,512]{2,1,0:T(8,128)S(1)} %copy.27), channel_id=1, source_target_pairs={{0,2},{1,3},{2,4},{3,5},{4,6},{5,7},{6,8},{7,9},{8,10},{9,11},{10,... | collective-permute-start | bytes 3145736 | tf_op jit(solution)/shard_map/ppermute | solution.py:15
  93.4 48.1 %collective-permute-start.4 = (f32[4,128,512]{2,1,0:T(8,128)S(1)}, f32[4,128,512]{2,1,0:T(8,128)S(1)}, u32[]{:S(2)}, u32[]{:S(2)}) collective-permute-start(f32[4,128,512]{2,1,0:T(8,128)S(1)} %copy.26), channel_id=1, source_target_pairs={{0,1},{1,2},{2,3},{3,4},{4,5},{5,6},{6,7},{7,8},{8,9},{9,10},{10,1... | collective-permute-start | bytes 3145736 | tf_op jit(solution)/shard_map/ppermute | solution.py:15
  101.9 2.2 %copy-start.1 = (bf16[12,256,512]{2,1,0:T(8,128)(2,1)S(1)}, bf16[12,256,512]{2,1,0:T(8,128)(2,1)}, u32[]{:S(2)}) copy-start(bf16[12,256,512]{2,1,0:T(8,128)(2,1)} %all-gather.2.cloned.1.call-done) | copy-start | bytes 9437188
  104.1 37.3 %copy-start.4 = (bf16[4,128,512]{2,1,0:T(8,128)(2,1)S(1)}, bf16[4,128,512]{2,1,0:T(8,128)(2,1)}, u32[]{:S(2)}) copy-start(bf16[4,128,512]{2,1,0:T(8,128)(2,1)} %param.7) | copy-start | bytes 1572868
Sparse Core Ops, SparseCore 0:
  41.7 13.4 all-gather.1
where the time goes:
time: 151 us; the launch traced here: 150 us
  waiting for transfers between devices  77.7 us (51%)
  starting transfers between devices  22.8 us (15%)
  matrix products  17.2 us (11%)
  between operations  13.7 us (9%)
  local copies, waits for them, and re-layouts  13.5 us (9%)
  other arithmetic  5.41 us (4%)
    ppermute x6, waiting for transfers between devices, from_behind(): return lax.ppermute(shard, axis, pairs)  77.7 us
    ppermute x6, starting transfers between devices, from_behind(): return lax.ppermute(shard, axis, pairs)  22.8 us
    dot_general x1, matrix products, per_device(): jnp.einsum('kmp,kmq->kpq', first_a, second_a, preferred_element_type=jnp....  5.86 us
    gather x1, local copies, waits for them, and re-layouts, per_device(): first_a = jnp.take(whole_window, first_local, axis=0)  4 us
    gather x1, local copies, waits for them, and re-layouts, per_device(): second_a = jnp.take(whole_window, second_local, axis=0)  3.92 us
  transfers between devices with their start and end apart: 7, of which 6 were waited for; matrix products, arithmetic and copies ran while one was open for 9% of the time, Pallas kernels for 0%

commit v1 on v0

v1 whole, which is shorter than its diff:
```python
import jax
import jax.numpy as jnp
from jax import lax
from jax.experimental import pallas as pl
from jax.experimental.pallas import tpu as pltpu
from jax.sharding import PartitionSpec as P

MEMBERS = 256
NBIN = 4
RADIUS = 4
WIDTH = 32
ROWS = 128
GROUPS = 3
F32 = jnp.float32
BF16 = jnp.bfloat16
VMEM_BYTES = 40 * 1024 * 1024


def routes(size):
    to_u, to_v = [], []
    for t in range(size):
        r = t % 4
        if r != 3:
            to_u.append((t, t + (1, 2, -2)[r]))
        if r != 1:
            to_v.append((t, t + {0: -4, 2: 1, 3: 2}[r]))
    inside = lambda pairs: [(a, b) for a, b in pairs if 0 <= a < size and 0 <= b < size]
    return inside(to_u), inside(to_v)


def back(pairs):
    return [(b, a) for a, b in pairs]


def entries_for(codes, place, tiles):
    r = place % 4
    out = []
    for group, code in enumerate(codes):
        left = code - 1
        bins = left % NBIN
        left = left // NBIN
        first = left % tiles
        left = left // tiles
        second = left % tiles
        dist = left // tiles
        if group == 0:
            other = jnp.where(dist == 0, 0, jnp.where((dist == 2) & (r == 0), 1, -1))
        elif group == 1:
            at_0 = jnp.where(dist == 2, 2, -1)
            at_1 = jnp.where(dist == 1, 0, -1)
            at_3 = jnp.where(dist == 1, 2, jnp.where(dist == 2, 0, -1))
            other = jnp.where(r == 0, at_0, jnp.where(r == 1, at_1, jnp.where(r == 3, at_3, -1)))
        else:
            at_1 = jnp.where(dist == 1, 1, jnp.where(dist == 2, 0, -1))
            at_3 = jnp.where(dist == 1, 0, -1)
            other = jnp.where(r == 1, at_1, jnp.where(r == 3, at_3, -1))
        entry = 1 + bins + NBIN * (group * tiles + first + GROUPS * tiles * (other * tiles + second))
        out.append(jnp.where((code > 0) & (other >= 0), entry, 0))
    return jnp.concatenate(out)


def decode(entry, tiles):
    left = entry - 1
    bins = lax.rem(left, NBIN)
    left = lax.div(left, NBIN)
    return bins, lax.rem(left, GROUPS * tiles), lax.div(left, GROUPS * tiles)


def fill_weights(along, across, points):
    q = lax.broadcasted_iota(jnp.int32, (WIDTH, points), 1) % WIDTH
    p = lax.broadcasted_iota(jnp.int32, (WIDTH, points), 0)
    gap = (q - p).astype(F32)
    for b in range(NBIN):
        shift = gap + 0.5 * RADIUS * b
        along[b] = jnp.exp(-(shift * shift) / (2.0 * RADIUS * RADIUS))
    levels = points // WIDTH
    row = lax.broadcasted_iota(jnp.int32, (levels, points), 1) // WIDTH
    level = lax.broadcasted_iota(jnp.int32, (levels, points), 0)
    gap = (row - level).astype(F32)
    across[...] = jnp.exp(-(gap * gap) / (2.0 * RADIUS * RADIUS)) / (MEMBERS - 1)


def covariance(a, first, second, bins, along, across, put):
    points = a.shape[2]
    right = a[second]
    weight = along[bins]
    for p0 in range(0, points, ROWS):
        cross = lax.dot_general(
            a[first, :, pl.ds(p0, ROWS)], right, (((0,), (0,)), ((), ())), preferred_element_type=F32
        )
        for k in range(ROWS // WIDTH):
            level = (p0 // WIDTH) + k
            part = cross[k * WIDTH : (k + 1) * WIDTH]
            put(p0 + k * WIDTH, (part * (weight * across[pl.ds(level, 1), :])).astype(BF16))


def to_first(g, c):
    return lax.dot_general(g, c, (((1,), (1,)), ((), ())), preferred_element_type=F32)


def to_second(g, c):
    return lax.dot_general(g, c, (((1,), (0,)), ((), ())), preferred_element_type=F32)


def load_groups(halves, a, sems):
    tiles, members = halves[0].shape[0], halves[0].shape[1]
    copies = []
    for k, half in enumerate(halves):
        copy = pltpu.make_async_copy(
            half, a.at[pl.ds((k // 2) * tiles, tiles), pl.ds((k % 2) * members, members), :], sems.at[k]
        )
        copy.start()
        copies.append(copy)
    return copies


def put_in(ref):
    def put(row, value):
        ref[pl.ds(row, WIDTH), :] = value

    return put


def forcing_kernel(obs, innov, out, total):
    total[...] = jnp.zeros_like(total)

    def step(o, carry):
        t = obs[o]
        total[t] = total[t] + innov[o].astype(F32)
        return carry

    lax.fori_loop(0, innov.shape[0], step, 0)
    out[...] = total[...].astype(BF16)


def local_kernel(entries, mine, theirs, g, out, a, c, along, across, sems):
    tiles, points = mine.shape[0], mine.shape[2]
    copies = load_groups([mine, theirs], a, sems)
    fill_weights(along, across, points)
    for copy in copies:
        copy.wait()

    def own(t, carry):
        covariance(a, t, t, 0, along, across, put_in(c))
        out[t] = to_first(g[t], c[...])
        return carry

    lax.fori_loop(0, tiles, own, 0)

    def pair(k, carry):
        entry = entries[k]
        bins, first, second = decode(entry, tiles)

        @pl.when((entry > 0) & (second < tiles))
        def _():
            covariance(a, first, second, bins, along, across, put_in(c))
            out[first] = out[first] + to_first(g[second], c[...])
            out[second] = out[second] + to_second(g[first], c[...])

        return carry

    lax.fori_loop(0, entries.shape[0] // GROUPS, pair, 0)


def early_kernel(entries, lm, lt, um, ut, vm, vt, g, far, inc, a, c, along, across, sems):
    tiles, points = lm.shape[0], lm.shape[2]
    copies = load_groups([lm, lt, um, ut, vm, vt], a, sems)
    fill_weights(along, across, points)
    inc[...] = jnp.zeros_like(inc)
    for copy in copies:
        copy.wait()
    slots = entries.shape[0] // GROUPS

    def pair(k, carry):
        entry = entries[k]
        bins, first, second = decode(entry, tiles)
        local_first, local_second = first < tiles, second < tiles

        @pl.when((entry > 0) & jnp.logical_not(local_first) & jnp.logical_not(local_second))
        def _():
            covariance(a, first, second, bins, along, across, put_in(far.at[lax.rem(k, slots)]))

        @pl.when((entry > 0) & (local_first != local_second))
        def _():
            covariance(a, first, second, bins, along, across, put_in(c))

            @pl.when(local_first)
            def _():
                inc[second - tiles] = inc[second - tiles] + to_second(g[first], c[...])

            @pl.when(local_second)
            def _():
                inc[first - tiles] = inc[first - tiles] + to_first(g[second], c[...])

        return carry

    lax.fori_loop(0, entries.shape[0], pair, 0)


def far_kernel(entries, far, inc, gu, gv, to_u, to_v, total, g):
    tiles = gu.shape[0]
    slots = entries.shape[0] // GROUPS
    total[...] = inc[...]
    g[pl.ds(0, tiles)] = gu[...]
    g[pl.ds(tiles, tiles)] = gv[...]

    def pair(k, carry):
        entry = entries[slots + k]
        _, first, second = decode(entry, tiles)

        @pl.when((entry > 0) & (first >= tiles) & (second >= tiles))
        def _():
            c = far[lax.rem(k, slots)]
            i, j = first - tiles, second - tiles
            total[i] = total[i] + to_first(g[j], c)
            total[j] = total[j] + to_second(g[i], c)

        return carry

    lax.fori_loop(0, 2 * slots, pair, 0)
    to_u[...] = total[pl.ds(0, tiles)].astype(BF16)
    to_v[...] = total[pl.ds(tiles, tiles)].astype(BF16)


def late_kernel(entries, lm, lt, um, ut, vm, vt, gu, gv, base, out, a, g, c, along, across, sems):
    tiles, points = lm.shape[0], lm.shape[2]
    copies = load_groups([lm, lt, um, ut, vm, vt], a, sems)
    fill_weights(along, across, points)
    g[pl.ds(0, tiles)] = gu[...]
    g[pl.ds(tiles, tiles)] = gv[...]
    for copy in copies:
        copy.wait()
    out[...] = base[...] + a[pl.ds(0, tiles), pl.ds(0, lm.shape[1]), :].astype(F32)

    def pair(k, carry):
        entry = entries[k]
        bins, first, second = decode(entry, tiles)
        local_first, local_second = first < tiles, second < tiles

        @pl.when((entry > 0) & (local_first != local_second))
        def _():
            covariance(a, first, second, bins, along, across, put_in(c))

            @pl.when(local_first)
            def _():
                out[first] = out[first] + to_first(g[second - tiles], c[...])

            @pl.when(local_second)
            def _():
                out[second] = out[second] + to_second(g[first - tiles], c[...])

        return carry

    lax.fori_loop(0, entries.shape[0], pair, 0)


def final_kernel(total, from_u, from_v, out):
    out[...] = (total[...] + from_u[...].astype(F32) + from_v[...].astype(F32)).astype(BF16)


def call(kernel, outs, places, scratch, us, *args):
    spec = {"s": pl.BlockSpec(memory_space=pltpu.SMEM), "v": pl.BlockSpec(memory_space=pltpu.VMEM), "h": pl.BlockSpec(memory_space=pl.ANY)}
    return pl.pallas_call(
        kernel,
        out_shape=outs,
        in_specs=[spec[p] for p in places],
        out_specs=jax.tree.map(lambda _: spec["v"], outs),
        scratch_shapes=scratch,
        compiler_params=pltpu.CompilerParams(vmem_limit_bytes=VMEM_BYTES),
        cost_estimate=pl.CostEstimate(flops=int(us * 1e9), bytes_accessed=int(us * 3e6), transcendentals=0),
    )(*args)


def per_device(anomalies, innovations, obs_tile, pair_tiles, loc_bin):
    tiles, members, points = anomalies.shape
    slots = loc_bin.shape[0]
    size = lax.axis_size("tile")
    place = lax.axis_index("tile")
    base = place * tiles
    to_u, to_v = routes(size)
    send = lambda x, pairs: lax.ppermute(x, "tile", pairs)
    swap = lambda x: lax.ppermute(x, "mem", [(0, 1), (1, 0)])

    a_u = send(anomalies, to_u)
    a_v = send(anomalies, to_v)
    a_t = swap(anomalies)
    first = pair_tiles[:, 0] - base
    second = pair_tiles[:, 1] - base
    code = 1 + loc_bin + NBIN * (first + tiles * second)
    code = jnp.where(loc_bin < NBIN, code, 0)
    entries = entries_for((code, send(code, to_u), send(code, to_v)), place, tiles)

    sds = jax.ShapeDtypeStruct
    vm = pltpu.VMEM
    weights = [vm((NBIN, WIDTH, points), F32), vm((points // WIDTH, points), F32)]
    forcing = call(
        forcing_kernel, sds(anomalies.shape, BF16), "sv", [vm(anomalies.shape, F32)], 1, obs_tile - base, innovations
    )
    g_u = send(forcing, to_u)
    g_v = send(forcing, to_v)
    a_ut = swap(a_u)
    a_vt = swap(a_v)

    local = call(
        local_kernel,
        sds(anomalies.shape, F32),
        "shhv",
        [vm((tiles, 2 * members, points), BF16), vm((points, points), BF16), *weights, pltpu.SemaphoreType.DMA((2,))],
        5,
        entries,
        anomalies,
        a_t,
        forcing,
    )
    groups = vm((GROUPS * tiles, 2 * members, points), BF16)
    square = vm((points, points), BF16)
    far, inc = call(
        early_kernel,
        (sds((slots, points, points), BF16), sds((2 * tiles, members, points), F32)),
        "shhhhhhv",
        [groups, square, *weights, pltpu.SemaphoreType.DMA((6,))],
        6,
        entries,
        anomalies,
        a_t,
        a_u,
        a_ut,
        a_v,
        a_vt,
        forcing,
    )
    inc_u, inc_v = call(
        far_kernel,
        (sds(anomalies.shape, BF16), sds(anomalies.shape, BF16)),
        "svvvv",
        [vm((2 * tiles, members, points), F32), vm((2 * tiles, members, points), BF16)],
        2,
        entries,
        far,
        inc,
        g_u,
        g_v,
    )
    from_u = send(inc_u, back(to_u))
    from_v = send(inc_v, back(to_v))
    total = call(
        late_kernel,
        sds(anomalies.shape, F32),
        "shhhhhhvvv",
        [groups, vm((2 * tiles, members, points), BF16), square, *weights, pltpu.SemaphoreType.DMA((6,))],
        6,
        entries,
        anomalies,
        a_t,
        a_u,
        a_ut,
        a_v,
        a_vt,
        g_u,
        g_v,
        local,
    )
    return call(final_kernel, sds(anomalies.shape, BF16), "vvv", [], 1, total, from_u, from_v)


def solution(mesh):
    return jax.shard_map(
        per_device,
        mesh=mesh,
        in_specs=(
            P("tile", "mem", None),
            P("tile", "mem", None),
            P("tile"),
            P("tile", None),
            P("tile"),
        ),
        out_specs=P("tile", "mem", None),
        check_vma=False,
    )
```

time: 151 us -> 62.1 us (0.41)
  the two profiles are of different devices: /device:TPU:8 before, /device:TPU:14 now
where the time goes in v1:
time: 62.1 us; the launch traced here: 61.3 us
  starting transfers between devices  19.6 us (32%)
  Pallas kernels  19.5 us (31%)
  waiting for transfers between devices  18.2 us (29%)
  local copies, waits for them, and re-layouts  2.28 us (4%)
  other arithmetic  1.61 us (3%)
    ppermute x8, starting transfers between devices, per_device(): send = lambda x, pairs: lax.ppermute(x, 'tile', pairs)  19.5 us
    pallas_call x6, Pallas kernels, call(): pl.pallas_call(kernel, out_shape=outs, in_specs=[spec[p] for p in places]...  19.5 us
    ppermute x8, waiting for transfers between devices, per_device(): send = lambda x, pairs: lax.ppermute(x, 'tile', pairs)  18.2 us
    unnamed x6, local copies, waits for them, and re-layouts  2.28 us
  transfers between devices with their start and end apart: 11, of which 4 were waited for; matrix products, arithmetic and copies ran while one was open for 1% of the time, Pallas kernels for 28%

profile of v1, /device:TPU:14, one launch (start us, length us, event | category | flops | bytes accessed | tf_op | source)
XLA Modules:
  0.0 61.3 jit_solution(5005074209224275878)
XLA Ops:
  0.0 0.8 %and_select_fusion.17 = (s32[8]{0:T(128)S(1)}, s32[8]{0:T(128)S(1)}) fusion(pred[]{:T(512)S(6)} %eq.47, s32[8,2]{0,1:T(2,128)} %param.8, s32[]{:T(128)S(6)} %mul.40, s32[8]{0:T(128)} %param.9), kind=kLoop, calls=%fused_computation.18 | loop fusion | flops 664 | bytes 165 | tf_op jit(solution)/shard_map/jit(_where)/select_n | solution.py:58
  0.8 3.4 %collective-permute-start.1 = (s32[8]{0:T(128)S(1)}, s32[8]{0:T(128)S(1)}, u32[]{:S(2)}, u32[]{:S(2)}) collective-permute-start(s32[8]{0:T(128)S(1)} %get-tuple-element.14), channel_id=1, source_target_pairs={{2,3},{3,5},{4,0},{6,7},{7,9},{8,4},{10,11},{11,13},{12,8},{14,15}... | collective-permute-start | bytes 104 | tf_op jit(solution)/shard_map/ppermute | solution.py:281
  4.2 1.3 %collective-permute-start = (s32[8]{0:T(128)S(1)}, s32[8]{0:T(128)S(1)}, u32[]{:S(2)}, u32[]{:S(2)}) collective-permute-start(s32[8]{0:T(128)S(1)} %get-tuple-element.14), channel_id=1, source_target_pairs={{0,1},{1,3},{2,0},{4,5},{5,7},{6,4},{8,9},{9,11},{10,8},{12,13},{1... | collective-permute-start | bytes 104 | tf_op jit(solution)/shard_map/ppermute | solution.py:281
  5.5 5.6 %collective-permute-start.5 = (bf16[4,128,512]{2,1,0:T(8,128)(2,1)}, bf16[4,128,512]{2,1,0:T(8,128)(2,1)S(1)}, u32[]{:S(2)}, u32[]{:S(2)}) collective-permute-start(bf16[4,128,512]{2,1,0:T(8,128)(2,1)} %lm.3), channel_id=1, source_target_pairs={{2,3},{3,5},{4,0},{6,7},{7,9},{8,4},{10,11},{11,13},{12,8},{14,15}... | collective-permute-start | bytes 1572872 | tf_op jit(solution)/shard_map/ppermute | solution.py:281
  11.1 1.3 %collective-permute-start.3 = (bf16[4,128,512]{2,1,0:T(8,128)(2,1)}, bf16[4,128,512]{2,1,0:T(8,128)(2,1)S(1)}, u32[]{:S(2)}, u32[]{:S(2)}) collective-permute-start(bf16[4,128,512]{2,1,0:T(8,128)(2,1)} %lm.3), channel_id=1, source_target_pairs={{0,1},{1,3},{2,0},{4,5},{5,7},{6,4},{8,9},{9,11},{10,8},{12,13},{1... | collective-permute-start | bytes 1572872 | tf_op jit(solution)/shard_map/ppermute | solution.py:281
  12.4 0.1 collective-permute-start.2
  12.5 0.7 %broadcast_subtract_fusion.obs = s32[8]{0:T(128)S(1)} fusion(s32[8]{0:T(128)} %param.7, s32[]{:T(128)S(6)} %mul.40), kind=kLoop, calls=%fused_computation.82 | loop fusion | flops 8 | bytes 68 | tf_op jit(solution)/shard_map/sub | solution.py:297
  13.2 0.0 copy-start
  13.2 1.2 %copy-done = bf16[8,128,512]{2,1,0:T(8,128)(2,1)S(1)} copy-done((bf16[8,128,512]{2,1,0:T(8,128)(2,1)S(1)}, bf16[8,128,512]{2,1,0:T(8,128)(2,1)}, u32[]{:S(2)}) %copy-start) | copy-done | bytes 1048600
  14.4 0.9 %shard_map.55.g = bf16[4,128,512]{2,1,0:T(8,128)(2,1)S(1)} custom-call(s32[8]{0:T(128)S(1)} %broadcast_subtract_fusion.obs, bf16[8,128,512]{2,1,0:T(8,128)(2,1)S(1)} %copy-done), custom_call_target="tpu_custom_call" | custom-call | flops 1000000000 | bytes 3000000 | tf_op jit(solution)/shard_map/pallas_call | solution.py:263
  15.3 0.0 collective-permute-done.1
  15.3 3.4 %collective-permute-start.8 = (bf16[4,128,512]{2,1,0:T(8,128)(2,1)S(1)}, bf16[4,128,512]{2,1,0:T(8,128)(2,1)S(1)}, u32[]{:S(2)}, u32[]{:S(2)}) collective-permute-start(bf16[4,128,512]{2,1,0:T(8,128)(2,1)S(1)} %shard_map.55.g), channel_id=1, source_target_pairs={{2,3},{3,5},{4,0},{6,7},{7,9},{8,4},{10,11},{11,13},{12,8},{14,15}... | collective-permute-start | bytes 1572872 | tf_op jit(solution)/shard_map/ppermute | solution.py:281
  18.7 0.0 collective-permute-done
  18.8 1.3 %collective-permute-start.7 = (bf16[4,128,512]{2,1,0:T(8,128)(2,1)S(1)}, bf16[4,128,512]{2,1,0:T(8,128)(2,1)S(1)}, u32[]{:S(2)}, u32[]{:S(2)}) collective-permute-start(bf16[4,128,512]{2,1,0:T(8,128)(2,1)S(1)} %shard_map.55.g), channel_id=1, source_target_pairs={{0,1},{1,3},{2,0},{4,5},{5,7},{6,4},{8,9},{9,11},{10,8},{12,13},{1... | collective-permute-start | bytes 1572872 | tf_op jit(solution)/shard_map/ppermute | solution.py:281
  20.1 3.7 %collective-permute-done.5.vm = bf16[4,128,512]{2,1,0:T(8,128)(2,1)S(1)} collective-permute-done((bf16[4,128,512]{2,1,0:T(8,128)(2,1)}, bf16[4,128,512]{2,1,0:T(8,128)(2,1)S(1)}, u32[]{:S(2)}, u32[]{:S(2)}) %collective-permute-start.5) | collective-permute-done | bytes 524320 | tf_op jit(solution)/shard_map/ppermute | solution.py:281
  23.8 0.0 collective-permute-start.6
  23.8 4.3 %collective-permute-done.3.um = bf16[4,128,512]{2,1,0:T(8,128)(2,1)S(1)} collective-permute-done((bf16[4,128,512]{2,1,0:T(8,128)(2,1)}, bf16[4,128,512]{2,1,0:T(8,128)(2,1)S(1)}, u32[]{:S(2)}, u32[]{:S(2)}) %collective-permute-start.3) | collective-permute-done | bytes 524320 | tf_op jit(solution)/shard_map/ppermute | solution.py:281
  28.1 0.0 collective-permute-start.4
  28.1 0.1 pad_add_fusion.entries
  28.2 0.0 collective-permute-done.2.theirs.lt
  28.2 0.0 copy-start.1
  28.2 1.0 %copy-done.1 = bf16[4,128,512]{2,1,0:T(8,128)(2,1)S(1)} copy-done((bf16[4,128,512]{2,1,0:T(8,128)(2,1)S(1)}, bf16[4,128,512]{2,1,0:T(8,128)(2,1)}, u32[]{:S(2)}) %copy-start.1) | copy-done | bytes 524312
  29.2 5.1 %shard_map.56.base = f32[4,128,512]{2,1,0:T(8,128)S(1)} custom-call(s32[24]{0:T(128)S(1)} %pad_add_fusion.entries, bf16[4,128,512]{2,1,0:T(8,128)(2,1)S(1)} %copy-done.1, bf16[4,128,512]{2,1,0:T(8,128)(2,1)S(1)} %collective-permute-done.2.theirs.lt, bf16[4,128,512]{2,1,0:T(8,128)(2,1)S(1)} %shard_map.55.g), custom_call_target="tpu_custom_call" | custom-call | flops 5000000000 | bytes 15000000 | tf_op jit(solution)/shard_map/pallas_call | solution.py:263
  34.3 0.0 collective-permute-done.6.vt
  34.3 0.0 collective-permute-done.4.ut
  34.3 5.9 %shard_map.58 = (bf16[8,512,512]{2,1,0:T(8,128)(2,1)S(1)}, f32[8,128,512]{2,1,0:T(8,128)S(1)}) custom-call(s32[24]{0:T(128)S(1)} %pad_add_fusion.entries, bf16[4,128,512]{2,1,0:T(8,128)(2,1)S(1)} %copy-done.1, bf16[4,128,512]{2,1,0:T(8,128)(2,1)S(1)} %collective-permute-done.2.theirs.lt, bf16[4,128,512]{2,1,0:T(8,128)(2,1)S(1)} %collective-permute-done.3.um, ...), custom_call_target="tpu_custom_call" | custom-call | flops 6000000000 | bytes 18000000 | tf_op jit(solution)/shard_map/pallas_call | solution.py:263
  40.2 0.0 copy-start.2
  40.3 0.0 collective-permute-done.8.gv
  40.3 0.0 collective-permute-done.7.gu
  40.3 1.6 %shard_map.59 = (bf16[4,128,512]{2,1,0:T(8,128)(2,1)S(1)}, bf16[4,128,512]{2,1,0:T(8,128)(2,1)S(1)}) custom-call(s32[24]{0:T(128)S(1)} %pad_add_fusion.entries, bf16[8,512,512]{2,1,0:T(8,128)(2,1)S(1)} %get-tuple-element.9.far, f32[8,128,512]{2,1,0:T(8,128)S(1)} %get-tuple-element.10.inc, bf16[4,128,512]{2,1,0:T(8,128)(2,1)S(1)} %collective-permute-done.7.gu, ...), custom_call_target="tpu_custom_call" | custom-call | flops 2000000000 | bytes 6000000 | tf_op jit(solution)/shard_map/pallas_call | solution.py:263
  41.9 1.3 %collective-permute-start.9 = (bf16[4,128,512]{2,1,0:T(8,128)(2,1)S(1)}, bf16[4,128,512]{2,1,0:T(8,128)(2,1)S(1)}, u32[]{:S(2)}, u32[]{:S(2)}) collective-permute-start(bf16[4,128,512]{2,1,0:T(8,128)(2,1)S(1)} %get-tuple-element.11), channel_id=1, source_target_pairs={{1,0},{3,1},{0,2},{5,4},{7,5},{4,6},{9,8},{11,9},{8,10},{13,12},{1... | collective-permute-start | bytes 1572872 | tf_op jit(solution)/shard_map/ppermute | solution.py:281
  43.3 1.9 %collective-permute-start.10 = (bf16[4,128,512]{2,1,0:T(8,128)(2,1)S(1)}, bf16[4,128,512]{2,1,0:T(8,128)(2,1)S(1)}, u32[]{:S(2)}, u32[]{:S(2)}) collective-permute-start(bf16[4,128,512]{2,1,0:T(8,128)(2,1)S(1)} %get-tuple-element.12), channel_id=1, source_target_pairs={{3,2},{5,3},{0,4},{7,6},{9,7},{4,8},{11,10},{13,11},{8,12},{15,14}... | collective-permute-start | bytes 1572872 | tf_op jit(solution)/shard_map/ppermute | solution.py:281
  45.2 0.0 copy-done.2
  45.2 5.0 %shard_map.57.total = f32[4,128,512]{2,1,0:T(8,128)S(1)} custom-call(s32[24]{0:T(128)S(1)} %pad_add_fusion.entries, bf16[4,128,512]{2,1,0:T(8,128)(2,1)S(1)} %copy-done.2, bf16[4,128,512]{2,1,0:T(8,128)(2,1)S(1)} %collective-permute-done.2.theirs.lt, bf16[4,128,512]{2,1,0:T(8,128)(2,1)S(1)} %collective-permute-done.3.um, ...), custom_call_target="tpu_custom_call" | custom-call | flops 6000000000 | bytes 18000000 | tf_op jit(solution)/shard_map/pallas_call | solution.py:263
  50.2 5.1 %collective-permute-done.9.from_u = bf16[4,128,512]{2,1,0:T(8,128)(2,1)S(1)} collective-permute-done((bf16[4,128,512]{2,1,0:T(8,128)(2,1)S(1)}, bf16[4,128,512]{2,1,0:T(8,128)(2,1)S(1)}, u32[]{:S(2)}, u32[]{:S(2)}) %collective-permute-start.9) | collective-permute-done | bytes 524320 | tf_op jit(solution)/shard_map/ppermute | solution.py:281
  55.3 5.0 %collective-permute-done.10.from_v = bf16[4,128,512]{2,1,0:T(8,128)(2,1)S(1)} collective-permute-done((bf16[4,128,512]{2,1,0:T(8,128)(2,1)S(1)}, bf16[4,128,512]{2,1,0:T(8,128)(2,1)S(1)}, u32[]{:S(2)}, u32[]{:S(2)}) %collective-permute-start.10) | collective-permute-done | bytes 524320 | tf_op jit(solution)/shard_map/ppermute | solution.py:281
  60.4 0.9 %shard_map.60 = bf16[4,128,512]{2,1,0:T(8,128)(2,1)} custom-call(f32[4,128,512]{2,1,0:T(8,128)S(1)} %shard_map.57.total, bf16[4,128,512]{2,1,0:T(8,128)(2,1)S(1)} %collective-permute-done.9.from_u, bf16[4,128,512]{2,1,0:T(8,128)(2,1)S(1)} %collective-permute-done.10.from_v), custom_call_target="tpu_custom_call" | custom-call | flops 1000000000 | bytes 3000000 | tf_op jit(solution)/shard_map/pallas_call | solution.py:263
  (2 shorter events, 0.1 us)
Async XLA Ops:
  0.8 14.5 %collective-permute-start.1 = (s32[8]{0:T(128)S(1)}, s32[8]{0:T(128)S(1)}, u32[]{:S(2)}, u32[]{:S(2)}) collective-permute-start(s32[8]{0:T(128)S(1)} %get-tuple-element.14), channel_id=1, source_target_pairs={{2,3},{3,5},{4,0},{6,7},{7,9},{8,4},{10,11},{11,13},{12,8},{14,15}... | collective-permute-start | bytes 104 | tf_op jit(solution)/shard_map/ppermute | solution.py:281
  4.2 14.5 %collective-permute-start = (s32[8]{0:T(128)S(1)}, s32[8]{0:T(128)S(1)}, u32[]{:S(2)}, u32[]{:S(2)}) collective-permute-start(s32[8]{0:T(128)S(1)} %get-tuple-element.14), channel_id=1, source_target_pairs={{0,1},{1,3},{2,0},{4,5},{5,7},{6,4},{8,9},{9,11},{10,8},{12,13},{1... | collective-permute-start | bytes 104 | tf_op jit(solution)/shard_map/ppermute | solution.py:281
  5.5 18.3 %collective-permute-start.5 = (bf16[4,128,512]{2,1,0:T(8,128)(2,1)}, bf16[4,128,512]{2,1,0:T(8,128)(2,1)S(1)}, u32[]{:S(2)}, u32[]{:S(2)}) collective-permute-start(bf16[4,128,512]{2,1,0:T(8,128)(2,1)} %lm.3), channel_id=1, source_target_pairs={{2,3},{3,5},{4,0},{6,7},{7,9},{8,4},{10,11},{11,13},{12,8},{14,15}... | collective-permute-start | bytes 1572872 | tf_op jit(solution)/shard_map/ppermute | solution.py:281
  11.1 17.0 %collective-permute-start.3 = (bf16[4,128,512]{2,1,0:T(8,128)(2,1)}, bf16[4,128,512]{2,1,0:T(8,128)(2,1)S(1)}, u32[]{:S(2)}, u32[]{:S(2)}) collective-permute-start(bf16[4,128,512]{2,1,0:T(8,128)(2,1)} %lm.3), channel_id=1, source_target_pairs={{0,1},{1,3},{2,0},{4,5},{5,7},{6,4},{8,9},{9,11},{10,8},{12,13},{1... | collective-permute-start | bytes 1572872 | tf_op jit(solution)/shard_map/ppermute | solution.py:281
  12.4 15.8 %collective-permute-start.2 = (bf16[4,128,512]{2,1,0:T(8,128)(2,1)}, bf16[4,128,512]{2,1,0:T(8,128)(2,1)S(1)}, u32[]{:S(2)}, u32[]{:S(2)}) collective-permute-start(bf16[4,128,512]{2,1,0:T(8,128)(2,1)} %lm.3), channel_id=1, source_target_pairs={{0,16},{16,0},{1,17},{17,1},{2,18},{18,2},{3,19},{19,3},{4,20},{20... | collective-permute-start | bytes 1572872 | tf_op jit(solution)/shard_map/ppermute | solution.py:282
  13.2 1.2 %copy-start = (bf16[8,128,512]{2,1,0:T(8,128)(2,1)S(1)}, bf16[8,128,512]{2,1,0:T(8,128)(2,1)}, u32[]{:S(2)}) copy-start(bf16[8,128,512]{2,1,0:T(8,128)(2,1)} %innov.1) | copy-start | bytes 3145732
  15.3 25.0 %collective-permute-start.8 = (bf16[4,128,512]{2,1,0:T(8,128)(2,1)S(1)}, bf16[4,128,512]{2,1,0:T(8,128)(2,1)S(1)}, u32[]{:S(2)}, u32[]{:S(2)}) collective-permute-start(bf16[4,128,512]{2,1,0:T(8,128)(2,1)S(1)} %shard_map.55.g), channel_id=1, source_target_pairs={{2,3},{3,5},{4,0},{6,7},{7,9},{8,4},{10,11},{11,13},{12,8},{14,15}... | collective-permute-start | bytes 1572872 | tf_op jit(solution)/shard_map/ppermute | solution.py:281
  18.8 21.5 %collective-permute-start.7 = (bf16[4,128,512]{2,1,0:T(8,128)(2,1)S(1)}, bf16[4,128,512]{2,1,0:T(8,128)(2,1)S(1)}, u32[]{:S(2)}, u32[]{:S(2)}) collective-permute-start(bf16[4,128,512]{2,1,0:T(8,128)(2,1)S(1)} %shard_map.55.g), channel_id=1, source_target_pairs={{0,1},{1,3},{2,0},{4,5},{5,7},{6,4},{8,9},{9,11},{10,8},{12,13},{1... | collective-permute-start | bytes 1572872 | tf_op jit(solution)/shard_map/ppermute | solution.py:281
  23.8 10.5 %collective-permute-start.6 = (bf16[4,128,512]{2,1,0:T(8,128)(2,1)S(1)}, bf16[4,128,512]{2,1,0:T(8,128)(2,1)S(1)}, u32[]{:S(2)}, u32[]{:S(2)}) collective-permute-start(bf16[4,128,512]{2,1,0:T(8,128)(2,1)S(1)} %collective-permute-done.5.vm), channel_id=1, source_target_pairs={{0,16},{16,0},{1,17},{17,1},{2,18},{18,2},{3,19},{19,3},{4,20},{20... | collective-permute-start | bytes 1572872 | tf_op jit(solution)/shard_map/ppermute | solution.py:282
  28.1 6.2 %collective-permute-start.4 = (bf16[4,128,512]{2,1,0:T(8,128)(2,1)S(1)}, bf16[4,128,512]{2,1,0:T(8,128)(2,1)S(1)}, u32[]{:S(2)}, u32[]{:S(2)}) collective-permute-start(bf16[4,128,512]{2,1,0:T(8,128)(2,1)S(1)} %collective-permute-done.3.um), channel_id=1, source_target_pairs={{0,16},{16,0},{1,17},{17,1},{2,18},{18,2},{3,19},{19,3},{4,20},{20... | collective-permute-start | bytes 1572872 | tf_op jit(solution)/shard_map/ppermute | solution.py:282
  28.2 1.0 %copy-start.1 = (bf16[4,128,512]{2,1,0:T(8,128)(2,1)S(1)}, bf16[4,128,512]{2,1,0:T(8,128)(2,1)}, u32[]{:S(2)}) copy-start(bf16[4,128,512]{2,1,0:T(8,128)(2,1)} %lm.3) | copy-start | bytes 1572868
  40.2 4.9 %copy-start.2 = (bf16[4,128,512]{2,1,0:T(8,128)(2,1)S(1)}, bf16[4,128,512]{2,1,0:T(8,128)(2,1)}, u32[]{:S(2)}) copy-start(bf16[4,128,512]{2,1,0:T(8,128)(2,1)} %lm.3) | copy-start | bytes 1572868
  41.9 13.4 %collective-permute-start.9 = (bf16[4,128,512]{2,1,0:T(8,128)(2,1)S(1)}, bf16[4,128,512]{2,1,0:T(8,128)(2,1)S(1)}, u32[]{:S(2)}, u32[]{:S(2)}) collective-permute-start(bf16[4,128,512]{2,1,0:T(8,128)(2,1)S(1)} %get-tuple-element.11), channel_id=1, source_target_pairs={{1,0},{3,1},{0,2},{5,4},{7,5},{4,6},{9,8},{11,9},{8,10},{13,12},{1... | collective-permute-start | bytes 1572872 | tf_op jit(solution)/shard_map/ppermute | solution.py:281
  43.3 17.1 %collective-permute-start.10 = (bf16[4,128,512]{2,1,0:T(8,128)(2,1)S(1)}, bf16[4,128,512]{2,1,0:T(8,128)(2,1)S(1)}, u32[]{:S(2)}, u32[]{:S(2)}) collective-permute-start(bf16[4,128,512]{2,1,0:T(8,128)(2,1)S(1)} %get-tuple-element.12), channel_id=1, source_target_pairs={{3,2},{5,3},{0,4},{7,6},{9,7},{4,8},{11,10},{13,11},{8,12},{15,14}... | collective-permute-start | bytes 1572872 | tf_op jit(solution)/shard_map/ppermute | solution.py:281

commit v2 on v1

v2 whole, which is shorter than its diff:
```python
import jax
import jax.numpy as jnp
from jax import lax
from jax.experimental import pallas as pl
from jax.experimental.pallas import tpu as pltpu
from jax.sharding import PartitionSpec as P

MEMBERS = 256
NBIN = 4
RADIUS = 4
WIDTH = 32
ROWS = 128
GROUPS = 3
F32 = jnp.float32
BF16 = jnp.bfloat16
VMEM_BYTES = 24 * 1024 * 1024
FULL_BYTES = 60 * 1024 * 1024

FROM_U = {0: 1, 1: 2, 2: 2}
FROM_V = {0: 2, 1: 4, 2: 1}


def routes(size, steps):
    return [(t + step, t) for t in range(size) for r, step in steps.items() if t % 4 == r and t + step < size]


def back(pairs):
    return [(b, a) for a, b in pairs]


def entries_for(lists, place, tiles):
    r = place % 4
    out = []
    for group, (code, second) in enumerate(lists):
        left = code - 1
        bins = left % NBIN
        first = left // NBIN
        dist = second // tiles
        second = second % tiles
        if group == 0:
            at_0 = dist
            at_1 = jnp.where(dist == 2, 1, -1)
            at_2 = 3 - dist
            other = jnp.where(r == 0, at_0, jnp.where(r == 1, at_1, jnp.where(r == 2, at_2, -1)))
            other = jnp.where(dist == 0, 0, other)
        elif group == 1:
            other = jnp.where(((r == 0) & (dist == 1)) | ((r == 1) & (dist == 2)), 2, -1)
        else:
            other = jnp.where((r == 2) & (dist == 1), 1, -1)
        entry = 1 + bins + NBIN * (group * tiles + first + GROUPS * tiles * (other * tiles + second))
        out.append(jnp.where((code > 0) & (other >= 0), entry, 0))
    return jnp.concatenate(out)


def decode(entry, tiles):
    left = entry - 1
    bins = lax.rem(left, NBIN)
    left = lax.div(left, NBIN)
    return bins, lax.rem(left, GROUPS * tiles), lax.div(left, GROUPS * tiles)


def fill_weights(along, across, points):
    q = lax.broadcasted_iota(jnp.int32, (WIDTH, points), 1) % WIDTH
    p = lax.broadcasted_iota(jnp.int32, (WIDTH, points), 0)
    gap = (q - p).astype(F32)
    for b in range(NBIN):
        shift = gap + 0.5 * RADIUS * b
        along[b] = jnp.exp(-(shift * shift) / (2.0 * RADIUS * RADIUS))
    levels = points // WIDTH
    row = lax.broadcasted_iota(jnp.int32, (levels, points), 1) // WIDTH
    level = lax.broadcasted_iota(jnp.int32, (levels, points), 0)
    gap = (row - level).astype(F32)
    across[...] = jnp.exp(-(gap * gap) / (2.0 * RADIUS * RADIUS)) / (MEMBERS - 1)


def both(a, tile, cols):
    tiles = a.shape[1]
    half, t = 2 * lax.div(tile, tiles), lax.rem(tile, tiles)
    return jnp.concatenate([a[half, t, :, cols], a[half + 1, t, :, cols]], axis=0)


def covariance(a, first, second, bins, along, across, put):
    points = a.shape[3]
    right = both(a, second, slice(None))
    weight = along[bins]
    for p0 in range(0, points, ROWS):
        cross = lax.dot_general(
            both(a, first, slice(p0, p0 + ROWS)), right, (((0,), (0,)), ((), ())), preferred_element_type=F32
        )
        for k in range(ROWS // WIDTH):
            level = (p0 // WIDTH) + k
            part = cross[k * WIDTH : (k + 1) * WIDTH]
            put(p0 + k * WIDTH, (part * (weight * across[pl.ds(level, 1), :])).astype(BF16))


def to_first(g, c):
    return lax.dot_general(g, c, (((1,), (1,)), ((), ())), preferred_element_type=F32)


def to_second(g, c):
    return lax.dot_general(g, c, (((1,), (0,)), ((), ())), preferred_element_type=F32)


def load_groups(messages, a, sems):
    copies = []
    for k, message in enumerate(messages):
        copy = pltpu.make_async_copy(message, a.at[k], sems.at[k])
        copy.start()
        copies.append(copy)
    return copies


def put_in(ref):
    def put(row, value):
        ref[pl.ds(row, WIDTH), :] = value

    return put


def forcing_kernel(obs, innov, out, total):
    tiles = out.shape[0]
    total[...] = jnp.zeros_like(total)

    def step(o, carry):
        t = lax.rem(obs[o], tiles)
        total[t] = total[t] + innov[o].astype(F32)
        return carry

    lax.fori_loop(0, innov.shape[0], step, 0)
    out[...] = total[...].astype(BF16)


def early_kernel(entries, lm, lt, um, ut, vm, vt, g, far, inc, a, c, along, across, sems):
    tiles, points = g.shape[0], g.shape[2]
    copies = load_groups([lm, lt, um, ut, vm, vt], a, sems)
    fill_weights(along, across, points)
    inc[...] = jnp.zeros_like(inc)
    for copy in copies:
        copy.wait()
    slots = entries.shape[0] // GROUPS

    def pair(k, carry):
        entry = entries[k]
        bins, first, second = decode(entry, tiles)
        local_first, local_second = first < tiles, second < tiles

        @pl.when((entry > 0) & jnp.logical_not(local_first))
        def _():
            covariance(a, first, second, bins, along, across, put_in(far.at[lax.rem(k, slots)]))

        @pl.when((entry > 0) & local_first & jnp.logical_not(local_second))
        def _():
            covariance(a, first, second, bins, along, across, put_in(c))
            inc[second - tiles] = inc[second - tiles] + to_second(g[first], c[...])

        return carry

    lax.fori_loop(0, entries.shape[0], pair, 0)


def far_kernel(entries, far, inc, gu, gv, to_u, to_v, total):
    del inc
    tiles = gu.shape[0]
    slots = entries.shape[0] // GROUPS

    def pair(k, carry):
        entry = entries[slots + k]
        _, first, second = decode(entry, tiles)
        far_pair = (entry > 0) & (first >= tiles) & (second >= tiles)

        def add(g_first, g_second):
            c = far.at[lax.rem(k, slots)]
            i, j = first - tiles, second - tiles
            total[i] = total[i] + to_first(g_second[lax.rem(j, tiles)], c[...])
            total[j] = total[j] + to_second(g_first[lax.rem(i, tiles)], c[...])

        @pl.when(far_pair & (first < second))
        def _():
            add(gu, gv)

        @pl.when(far_pair & (first > second))
        def _():
            add(gv, gu)

        return carry

    lax.fori_loop(0, 2 * slots, pair, 0)
    to_u[...] = total[pl.ds(0, tiles)].astype(BF16)
    to_v[...] = total[pl.ds(tiles, tiles)].astype(BF16)


def late_kernel(entries, lm, lt, um, ut, vm, vt, g_l, gu, gv, out, a, g, c, along, across, sems):
    tiles, members, points = g_l.shape
    copies = load_groups([lm, lt, um, ut, vm, vt], a, sems)
    fill_weights(along, across, points)
    g[pl.ds(0, tiles)] = g_l[...]
    g[pl.ds(tiles, tiles)] = gu[...]
    g[pl.ds(2 * tiles, tiles)] = gv[...]
    for copy in copies:
        copy.wait()

    def own(t, carry):
        covariance(a, t, t, 0, along, across, put_in(c))
        out[t] = a[0, t].astype(F32) + to_first(g[t], c[...])
        return carry

    lax.fori_loop(0, tiles, own, 0)

    def pair(k, carry):
        entry = entries[k]
        bins, first, second = decode(entry, tiles)

        @pl.when((entry > 0) & (first < tiles))
        def _():
            covariance(a, first, second, bins, along, across, put_in(c))
            out[first] = out[first] + to_first(g[second], c[...])

            @pl.when(second < tiles)
            def _():
                out[second] = out[second] + to_second(g[first], c[...])

        return carry

    lax.fori_loop(0, entries.shape[0] // GROUPS, pair, 0)


def final_kernel(total, from_u, from_v, out):
    out[...] = (total[...] + from_u[...].astype(F32) + from_v[...].astype(F32)).astype(BF16)


def call(kernel, outs, places, scratch, us, *args, aliases={}, grant=VMEM_BYTES):
    spec = {"s": pl.BlockSpec(memory_space=pltpu.SMEM), "v": pl.BlockSpec(memory_space=pltpu.VMEM), "h": pl.BlockSpec(memory_space=pl.ANY), "d": pl.BlockSpec(memory_space=pltpu.HBM)}
    return pl.pallas_call(
        kernel,
        out_shape=outs,
        in_specs=[spec[p] for p in places],
        out_specs=jax.tree.map(lambda _: spec["v"], outs),
        scratch_shapes=scratch,
        input_output_aliases=aliases,
        compiler_params=pltpu.CompilerParams(vmem_limit_bytes=grant),
        cost_estimate=pl.CostEstimate(flops=int(us * 1e7), bytes_accessed=int(us * 3e4), transcendentals=0),
    )(*args)


def per_device(anomalies, innovations, obs_tile, pair_tiles, loc_bin):
    tiles, members, points = anomalies.shape
    slots = loc_bin.shape[0]
    size = lax.axis_size("tile")
    place = lax.axis_index("tile")
    to_u, to_v = routes(size, FROM_U), routes(size, FROM_V)
    send = lambda x, pairs: lax.ppermute(x, "tile", pairs)
    swap = lambda x: lax.ppermute(x, "mem", [(0, 1), (1, 0)])

    sds = jax.ShapeDtypeStruct
    vm = pltpu.VMEM
    a_v = send(anomalies, to_v)
    a_u = send(anomalies, to_u)
    a_t = swap(anomalies)
    innovations, pair_tiles, a_t = lax.optimization_barrier((innovations, pair_tiles, a_t))
    first = pair_tiles[:, 0] % tiles
    second = pair_tiles[:, 1] - pair_tiles[:, 0] + first
    slot_list = jnp.stack([jnp.where(loc_bin < NBIN, 1 + loc_bin + NBIN * first, 0), second])
    lists = (slot_list, send(slot_list, to_u), send(slot_list, to_v))
    weights = [vm((NBIN, WIDTH, points), F32), vm((points // WIDTH, points), F32)]
    forcing = call(
        forcing_kernel, sds(anomalies.shape, BF16), "sv", [vm(anomalies.shape, F32)], 1, obs_tile, innovations
    )
    g_v = send(forcing, to_v)
    g_u = send(forcing, to_u)
    entries = entries_for(lists, place, tiles)
    a_ut = swap(a_u)
    a_vt = swap(a_v)

    groups = vm((2 * GROUPS, *anomalies.shape), BF16)
    square = vm((points, points), BF16)
    far, inc = call(
        early_kernel,
        (sds((slots, points, points), BF16), sds((2 * tiles, members, points), F32)),
        "shhhhhhv",
        [groups, square, *weights, pltpu.SemaphoreType.DMA((2 * GROUPS,))],
        6,
        entries,
        anomalies,
        a_t,
        a_u,
        a_ut,
        a_v,
        a_vt,
        forcing,
    )
    inc_u, inc_v, _ = call(
        far_kernel,
        (sds(anomalies.shape, BF16), sds(anomalies.shape, BF16), sds(inc.shape, F32)),
        "svvvv",
        [],
        2,
        entries,
        far,
        inc,
        g_u,
        g_v,
        aliases={2: 2},
    )
    from_v = send(inc_v, back(to_v))
    from_u = send(inc_u, back(to_u))
    total = call(
        late_kernel,
        sds(anomalies.shape, F32),
        "shhhhhhvvv",
        [groups, vm((GROUPS * tiles, members, points), BF16), square, *weights, pltpu.SemaphoreType.DMA((2 * GROUPS,))],
        10,
        entries,
        anomalies,
        a_t,
        a_u,
        a_ut,
        a_v,
        a_vt,
        forcing,
        g_u,
        g_v,
    )
    return call(final_kernel, sds(anomalies.shape, BF16), "vvv", [], 1, total, from_u, from_v)


def solution(mesh):
    return jax.shard_map(
        per_device,
        mesh=mesh,
        in_specs=(
            P("tile", "mem", None),
            P("tile", "mem", None),
            P("tile"),
            P("tile", None),
            P("tile"),
        ),
        out_specs=P("tile", "mem", None),
        check_vma=False,
    )
```

time: 62.1 us -> 54.1 us (0.87)
  the two profiles are of different devices: /device:TPU:14 before, /device:TPU:12 now
where the time goes in v2:
time: 54.1 us; the launch traced here: 53.7 us
  starting transfers between devices  17.6 us (33%)
  Pallas kernels  17.2 us (32%)
  waiting for transfers between devices  13.5 us (25%)
  local copies, waits for them, and re-layouts  2.92 us (5%)
  other arithmetic  2.34 us (4%)
    pallas_call x5, Pallas kernels, call(): pl.pallas_call(kernel, out_shape=outs, in_specs=[spec[p] for p in places]...  17.2 us
    ppermute x8, starting transfers between devices, per_device(): send = lambda x, pairs: lax.ppermute(x, 'tile', pairs)  17.1 us
    ppermute x8, waiting for transfers between devices, per_device(): send = lambda x, pairs: lax.ppermute(x, 'tile', pairs)  11.5 us
    unnamed x8, local copies, waits for them, and re-layouts  2.92 us
    ppermute x3, waiting for transfers between devices, per_device(): swap = lambda x: lax.ppermute(x, 'mem', [(0, 1), (1, 0)])  2.01 us
  transfers between devices with their start and end apart: 11, of which 8 were waited for; matrix products, arithmetic and copies ran while one was open for 4% of the time, Pallas kernels for 25%

profile of v2, /device:TPU:12, one launch (start us, length us, event | category | flops | bytes accessed | tf_op | source)
XLA Modules:
  0.0 53.7 jit_solution(6190561227068257388)
XLA Ops:
  0.0 0.0 collective-permute-start
  0.0 2.4 %collective-permute-start.5 = (bf16[4,128,512]{2,1,0:T(8,128)(2,1)}, bf16[4,128,512]{2,1,0:T(8,128)(2,1)S(1)}, u32[]{:S(2)}, u32[]{:S(2)}) collective-permute-start(bf16[4,128,512]{2,1,0:T(8,128)(2,1)} %lm.3), channel_id=1, source_target_pairs={{2,0},{5,1},{3,2},{6,4},{9,5},{7,6},{10,8},{13,9},{11,10},{14,12},... | collective-permute-start | bytes 1572872 | tf_op jit(solution)/shard_map/ppermute | solution.py:251
  2.4 1.3 %collective-permute-start.3 = (bf16[4,128,512]{2,1,0:T(8,128)(2,1)}, bf16[4,128,512]{2,1,0:T(8,128)(2,1)S(1)}, u32[]{:S(2)}, u32[]{:S(2)}) collective-permute-start(bf16[4,128,512]{2,1,0:T(8,128)(2,1)} %lm.3), channel_id=1, source_target_pairs={{1,0},{3,1},{4,2},{5,4},{7,5},{8,6},{9,8},{11,9},{12,10},{13,12},{... | collective-permute-start | bytes 1572872 | tf_op jit(solution)/shard_map/ppermute | solution.py:251
  3.7 0.0 collective-permute-done.lt
  3.7 0.8 %and_select_fusion.13 = (s32[8]{0:T(128)S(1)}, s32[8]{0:T(128)S(1)}) fusion(pred[]{:T(512)S(6)} %eq.41, pred[]{:T(512)S(6)} %eq.39, pred[]{:T(512)S(6)} %eq.38, s32[8,2]{0,1:T(2,128)} %param.8, s32[8]{0:T(128)} %param.9), kind=kLoop, calls=%fused_computation.22 | loop fusion | flops 608 | bytes 163 | tf_op jit(solution)/shard_map/jit(_where)/select_n | solution.py:51
  4.5 0.8 %fusion.3 = s32[1,8]{1,0:T(1,128)S(1)} fusion(s32[8,2]{0,1:T(2,128)} %param.8), kind=kLoop, calls=%fused_computation.51 | loop fusion | flops 104 | bytes 96 | tf_op jit(solution)/shard_map/add | solution.py:261
  5.3 0.7 %fusion.15 = s32[1,8]{1,0:T(1,128)S(1)} fusion(s32[8]{0:T(128)S(1)} %get-tuple-element.20, s32[8]{0:T(128)} %param.9), kind=kLoop, calls=%fused_computation.70 | loop fusion | flops 40 | bytes 96 | tf_op jit(solution)/shard_map/stack | solution.py:262
  6.0 3.9 %collective-permute-start.2 = (s32[2,8]{1,0:T(2,128)S(1)}, s32[2,8]{1,0:T(2,128)S(1)}, u32[]{:S(2)}, u32[]{:S(2)}) collective-permute-start(s32[2,8]{1,0:T(2,128)S(1)} %pad_add_fusion), channel_id=1, source_target_pairs={{2,0},{5,1},{3,2},{6,4},{9,5},{7,6},{10,8},{13,9},{11,10},{14,12},... | collective-permute-start | bytes 200 | tf_op jit(solution)/shard_map/ppermute | solution.py:251
  9.9 1.3 %collective-permute-start.1 = (s32[2,8]{1,0:T(2,128)S(1)}, s32[2,8]{1,0:T(2,128)S(1)}, u32[]{:S(2)}, u32[]{:S(2)}) collective-permute-start(s32[2,8]{1,0:T(2,128)S(1)} %pad_add_fusion), channel_id=1, source_target_pairs={{1,0},{3,1},{4,2},{5,4},{7,5},{8,6},{9,8},{11,9},{12,10},{13,12},{... | collective-permute-start | bytes 200 | tf_op jit(solution)/shard_map/ppermute | solution.py:251
  11.2 0.0 copy-start.2
  11.2 1.2 %copy-done.2 = bf16[8,128,512]{2,1,0:T(8,128)(2,1)S(1)} copy-done((bf16[8,128,512]{2,1,0:T(8,128)(2,1)S(1)}, bf16[8,128,512]{2,1,0:T(8,128)(2,1)}, u32[]{:S(2)}) %copy-start.2) | copy-done | bytes 1048600
  12.4 0.0 copy-start.3
  12.4 0.7 %copy-done.3 = s32[8]{0:T(128)S(1)} copy-done((s32[8]{0:T(128)S(1)}, s32[8]{0:T(128)}, u32[]{:S(2)}) %copy-start.3) | copy-done | bytes 56
  13.1 0.9 %shard_map.55.g_l.g = bf16[4,128,512]{2,1,0:T(8,128)(2,1)S(1)} custom-call(s32[8]{0:T(128)S(1)} %copy-done.3, bf16[8,128,512]{2,1,0:T(8,128)(2,1)S(1)} %copy-done.2), custom_call_target="tpu_custom_call" | custom-call | flops 10000000 | bytes 30000 | tf_op jit(solution)/shard_map/pallas_call | solution.py:233
  14.0 1.9 %collective-permute-start.8 = (bf16[4,128,512]{2,1,0:T(8,128)(2,1)S(1)}, bf16[4,128,512]{2,1,0:T(8,128)(2,1)S(1)}, u32[]{:S(2)}, u32[]{:S(2)}) collective-permute-start(bf16[4,128,512]{2,1,0:T(8,128)(2,1)S(1)} %shard_map.55.g_l.g), channel_id=1, source_target_pairs={{2,0},{5,1},{3,2},{6,4},{9,5},{7,6},{10,8},{13,9},{11,10},{14,12},... | collective-permute-start | bytes 1572872 | tf_op jit(solution)/shard_map/ppermute | solution.py:251
  15.9 0.5 collective-permute-done.5.vm
  16.4 1.3 %collective-permute-start.7 = (bf16[4,128,512]{2,1,0:T(8,128)(2,1)S(1)}, bf16[4,128,512]{2,1,0:T(8,128)(2,1)S(1)}, u32[]{:S(2)}, u32[]{:S(2)}) collective-permute-start(bf16[4,128,512]{2,1,0:T(8,128)(2,1)S(1)} %shard_map.55.g_l.g), channel_id=1, source_target_pairs={{1,0},{3,1},{4,2},{5,4},{7,5},{8,6},{9,8},{11,9},{12,10},{13,12},{... | collective-permute-start | bytes 1572872 | tf_op jit(solution)/shard_map/ppermute | solution.py:251
  17.7 1.8 %collective-permute-done.3.um = bf16[4,128,512]{2,1,0:T(8,128)(2,1)S(1)} collective-permute-done((bf16[4,128,512]{2,1,0:T(8,128)(2,1)}, bf16[4,128,512]{2,1,0:T(8,128)(2,1)S(1)}, u32[]{:S(2)}, u32[]{:S(2)}) %collective-permute-start.3) | collective-permute-done | bytes 524320 | tf_op jit(solution)/shard_map/ppermute | solution.py:251
  19.5 0.0 collective-permute-start.6
  19.5 0.0 collective-permute-done.2
  19.5 0.5 collective-permute-start.4
  20.0 0.0 collective-permute-done.1
  20.1 0.1 pad_add_fusion.1.entries
  20.1 1.3 %collective-permute-done.6.vt = bf16[4,128,512]{2,1,0:T(8,128)(2,1)S(1)} collective-permute-done((bf16[4,128,512]{2,1,0:T(8,128)(2,1)S(1)}, bf16[4,128,512]{2,1,0:T(8,128)(2,1)S(1)}, u32[]{:S(2)}, u32[]{:S(2)}) %collective-permute-start.6) | collective-permute-done | bytes 524320 | tf_op jit(solution)/shard_map/ppermute | solution.py:252
  21.4 0.7 %collective-permute-done.4.ut = bf16[4,128,512]{2,1,0:T(8,128)(2,1)S(1)} collective-permute-done((bf16[4,128,512]{2,1,0:T(8,128)(2,1)S(1)}, bf16[4,128,512]{2,1,0:T(8,128)(2,1)S(1)}, u32[]{:S(2)}, u32[]{:S(2)}) %collective-permute-start.4) | collective-permute-done | bytes 524320 | tf_op jit(solution)/shard_map/ppermute | solution.py:252
  22.2 0.0 copy-start
  22.2 1.0 %copy-done = bf16[4,128,512]{2,1,0:T(8,128)(2,1)S(1)} copy-done((bf16[4,128,512]{2,1,0:T(8,128)(2,1)S(1)}, bf16[4,128,512]{2,1,0:T(8,128)(2,1)}, u32[]{:S(2)}) %copy-start) | copy-done | bytes 524312
  23.2 5.6 %shard_map.57 = (bf16[8,512,512]{2,1,0:T(8,128)(2,1)S(1)}, f32[8,128,512]{2,1,0:T(8,128)S(1)}) custom-call(s32[24]{0:T(128)S(1)} %pad_add_fusion.1.entries, bf16[4,128,512]{2,1,0:T(8,128)(2,1)S(1)} %copy-done, bf16[4,128,512]{2,1,0:T(8,128)(2,1)S(1)} %collective-permute-done.lt, bf16[4,128,512]{2,1,0:T(8,128)(2,1)S(1)} %collective-permute-done.3.um, ...), custom_call_target="tpu_custom_call" | custom-call | flops 60000000 | bytes 180000 | tf_op jit(solution)/shard_map/pallas_call | solution.py:233
  28.8 0.9 %collective-permute-done.8.gv = bf16[4,128,512]{2,1,0:T(8,128)(2,1)S(1)} collective-permute-done((bf16[4,128,512]{2,1,0:T(8,128)(2,1)S(1)}, bf16[4,128,512]{2,1,0:T(8,128)(2,1)S(1)}, u32[]{:S(2)}, u32[]{:S(2)}) %collective-permute-start.8) | collective-permute-done | bytes 524320 | tf_op jit(solution)/shard_map/ppermute | solution.py:251
  29.7 3.1 %collective-permute-done.7.gu = bf16[4,128,512]{2,1,0:T(8,128)(2,1)S(1)} collective-permute-done((bf16[4,128,512]{2,1,0:T(8,128)(2,1)S(1)}, bf16[4,128,512]{2,1,0:T(8,128)(2,1)S(1)}, u32[]{:S(2)}, u32[]{:S(2)}) %collective-permute-start.7) | collective-permute-done | bytes 524320 | tf_op jit(solution)/shard_map/ppermute | solution.py:251
  32.8 0.0 copy-start.1
  32.8 2.7 %shard_map.58 = (bf16[4,128,512]{2,1,0:T(8,128)(2,1)S(1)}, bf16[4,128,512]{2,1,0:T(8,128)(2,1)S(1)}, f32[8,128,512]{2,1,0:T(8,128)S(1)}) custom-call(s32[24]{0:T(128)S(1)} %pad_add_fusion.1.entries, bf16[8,512,512]{2,1,0:T(8,128)(2,1)S(1)} %get-tuple-element.15.far, f32[8,128,512]{2,1,0:T(8,128)S(1)} %get-tuple-element.16.inc, ...), custom_call_target="tpu_custom_call", output_to_operand_aliasing={{2}: (2, {})} | custom-call | flops 20000000 | bytes 60000 | tf_op jit(solution)/shard_map/pallas_call | solution.py:233
  35.5 3.0 %collective-permute-start.9 = (bf16[4,128,512]{2,1,0:T(8,128)(2,1)S(1)}, bf16[4,128,512]{2,1,0:T(8,128)(2,1)S(1)}, u32[]{:S(2)}, u32[]{:S(2)}) collective-permute-start(bf16[4,128,512]{2,1,0:T(8,128)(2,1)S(1)} %get-tuple-element.17), channel_id=1, source_target_pairs={{0,1},{1,3},{2,4},{4,5},{5,7},{6,8},{8,9},{9,11},{10,12},{12,13},{... | collective-permute-start | bytes 1572872 | tf_op jit(solution)/shard_map/ppermute | solution.py:251
  38.5 1.9 %collective-permute-start.10 = (bf16[4,128,512]{2,1,0:T(8,128)(2,1)S(1)}, bf16[4,128,512]{2,1,0:T(8,128)(2,1)S(1)}, u32[]{:S(2)}, u32[]{:S(2)}) collective-permute-start(bf16[4,128,512]{2,1,0:T(8,128)(2,1)S(1)} %get-tuple-element.18), channel_id=1, source_target_pairs={{0,2},{1,5},{2,3},{4,6},{5,9},{6,7},{8,10},{9,13},{10,11},{12,14},... | collective-permute-start | bytes 1572872 | tf_op jit(solution)/shard_map/ppermute | solution.py:251
  40.4 0.0 copy-done.1
  40.5 7.0 %shard_map.56.total = f32[4,128,512]{2,1,0:T(8,128)S(1)} custom-call(s32[24]{0:T(128)S(1)} %pad_add_fusion.1.entries, bf16[4,128,512]{2,1,0:T(8,128)(2,1)S(1)} %copy-done.1, bf16[4,128,512]{2,1,0:T(8,128)(2,1)S(1)} %collective-permute-done.lt, bf16[4,128,512]{2,1,0:T(8,128)(2,1)S(1)} %collective-permute-done.3.um, ...), custom_call_target="tpu_custom_call" | custom-call | flops 100000000 | bytes 300000 | tf_op jit(solution)/shard_map/pallas_call | solution.py:233
  47.5 1.1 %collective-permute-done.9.from_u = bf16[4,128,512]{2,1,0:T(8,128)(2,1)S(1)} collective-permute-done((bf16[4,128,512]{2,1,0:T(8,128)(2,1)S(1)}, bf16[4,128,512]{2,1,0:T(8,128)(2,1)S(1)}, u32[]{:S(2)}, u32[]{:S(2)}) %collective-permute-start.9) | collective-permute-done | bytes 524320 | tf_op jit(solution)/shard_map/ppermute | solution.py:251
  48.6 4.1 %collective-permute-done.10.from_v = bf16[4,128,512]{2,1,0:T(8,128)(2,1)S(1)} collective-permute-done((bf16[4,128,512]{2,1,0:T(8,128)(2,1)S(1)}, bf16[4,128,512]{2,1,0:T(8,128)(2,1)S(1)}, u32[]{:S(2)}, u32[]{:S(2)}) %collective-permute-start.10) | collective-permute-done | bytes 524320 | tf_op jit(solution)/shard_map/ppermute | solution.py:251
  52.7 1.0 %shard_map.59 = bf16[4,128,512]{2,1,0:T(8,128)(2,1)} custom-call(f32[4,128,512]{2,1,0:T(8,128)S(1)} %shard_map.56.total, bf16[4,128,512]{2,1,0:T(8,128)(2,1)S(1)} %collective-permute-done.9.from_u, bf16[4,128,512]{2,1,0:T(8,128)(2,1)S(1)} %collective-permute-done.10.from_v), custom_call_target="tpu_custom_call" | custom-call | flops 10000000 | bytes 30000 | tf_op jit(solution)/shard_map/pallas_call | solution.py:233
  (3 shorter events, 0.1 us)
Async XLA Ops:
  0.0 3.7 %collective-permute-start = (bf16[4,128,512]{2,1,0:T(8,128)(2,1)}, bf16[4,128,512]{2,1,0:T(8,128)(2,1)S(1)}, u32[]{:S(2)}, u32[]{:S(2)}) collective-permute-start(bf16[4,128,512]{2,1,0:T(8,128)(2,1)} %lm.3), channel_id=1, source_target_pairs={{0,16},{16,0},{1,17},{17,1},{2,18},{18,2},{3,19},{19,3},{4,20},{20... | collective-permute-start | bytes 1572872 | tf_op jit(solution)/shard_map/ppermute | solution.py:252
  0.0 16.4 %collective-permute-start.5 = (bf16[4,128,512]{2,1,0:T(8,128)(2,1)}, bf16[4,128,512]{2,1,0:T(8,128)(2,1)S(1)}, u32[]{:S(2)}, u32[]{:S(2)}) collective-permute-start(bf16[4,128,512]{2,1,0:T(8,128)(2,1)} %lm.3), channel_id=1, source_target_pairs={{2,0},{5,1},{3,2},{6,4},{9,5},{7,6},{10,8},{13,9},{11,10},{14,12},... | collective-permute-start | bytes 1572872 | tf_op jit(solution)/shard_map/ppermute | solution.py:251
  2.4 17.1 %collective-permute-start.3 = (bf16[4,128,512]{2,1,0:T(8,128)(2,1)}, bf16[4,128,512]{2,1,0:T(8,128)(2,1)S(1)}, u32[]{:S(2)}, u32[]{:S(2)}) collective-permute-start(bf16[4,128,512]{2,1,0:T(8,128)(2,1)} %lm.3), channel_id=1, source_target_pairs={{1,0},{3,1},{4,2},{5,4},{7,5},{8,6},{9,8},{11,9},{12,10},{13,12},{... | collective-permute-start | bytes 1572872 | tf_op jit(solution)/shard_map/ppermute | solution.py:251
  6.0 13.5 %collective-permute-start.2 = (s32[2,8]{1,0:T(2,128)S(1)}, s32[2,8]{1,0:T(2,128)S(1)}, u32[]{:S(2)}, u32[]{:S(2)}) collective-permute-start(s32[2,8]{1,0:T(2,128)S(1)} %pad_add_fusion), channel_id=1, source_target_pairs={{2,0},{5,1},{3,2},{6,4},{9,5},{7,6},{10,8},{13,9},{11,10},{14,12},... | collective-permute-start | bytes 200 | tf_op jit(solution)/shard_map/ppermute | solution.py:251
  9.9 10.1 %collective-permute-start.1 = (s32[2,8]{1,0:T(2,128)S(1)}, s32[2,8]{1,0:T(2,128)S(1)}, u32[]{:S(2)}, u32[]{:S(2)}) collective-permute-start(s32[2,8]{1,0:T(2,128)S(1)} %pad_add_fusion), channel_id=1, source_target_pairs={{1,0},{3,1},{4,2},{5,4},{7,5},{8,6},{9,8},{11,9},{12,10},{13,12},{... | collective-permute-start | bytes 200 | tf_op jit(solution)/shard_map/ppermute | solution.py:251
  11.2 1.2 %copy-start.2 = (bf16[8,128,512]{2,1,0:T(8,128)(2,1)S(1)}, bf16[8,128,512]{2,1,0:T(8,128)(2,1)}, u32[]{:S(2)}) copy-start(bf16[8,128,512]{2,1,0:T(8,128)(2,1)} %innov) | copy-start | bytes 3145732
  12.4 0.7 %copy-start.3 = (s32[8]{0:T(128)S(1)}, s32[8]{0:T(128)}, u32[]{:S(2)}) copy-start(s32[8]{0:T(128)} %obs.1) | copy-start | bytes 100
  14.0 15.7 %collective-permute-start.8 = (bf16[4,128,512]{2,1,0:T(8,128)(2,1)S(1)}, bf16[4,128,512]{2,1,0:T(8,128)(2,1)S(1)}, u32[]{:S(2)}, u32[]{:S(2)}) collective-permute-start(bf16[4,128,512]{2,1,0:T(8,128)(2,1)S(1)} %shard_map.55.g_l.g), channel_id=1, source_target_pairs={{2,0},{5,1},{3,2},{6,4},{9,5},{7,6},{10,8},{13,9},{11,10},{14,12},... | collective-permute-start | bytes 1572872 | tf_op jit(solution)/shard_map/ppermute | solution.py:251
  16.4 16.3 %collective-permute-start.7 = (bf16[4,128,512]{2,1,0:T(8,128)(2,1)S(1)}, bf16[4,128,512]{2,1,0:T(8,128)(2,1)S(1)}, u32[]{:S(2)}, u32[]{:S(2)}) collective-permute-start(bf16[4,128,512]{2,1,0:T(8,128)(2,1)S(1)} %shard_map.55.g_l.g), channel_id=1, source_target_pairs={{1,0},{3,1},{4,2},{5,4},{7,5},{8,6},{9,8},{11,9},{12,10},{13,12},{... | collective-permute-start | bytes 1572872 | tf_op jit(solution)/shard_map/ppermute | solution.py:251
  19.5 1.9 %collective-permute-start.6 = (bf16[4,128,512]{2,1,0:T(8,128)(2,1)S(1)}, bf16[4,128,512]{2,1,0:T(8,128)(2,1)S(1)}, u32[]{:S(2)}, u32[]{:S(2)}) collective-permute-start(bf16[4,128,512]{2,1,0:T(8,128)(2,1)S(1)} %collective-permute-done.5.vm), channel_id=1, source_target_pairs={{0,16},{16,0},{1,17},{17,1},{2,18},{18,2},{3,19},{19,3},{4,20},{20... | collective-permute-start | bytes 1572872 | tf_op jit(solution)/shard_map/ppermute | solution.py:252
  19.5 2.7 %collective-permute-start.4 = (bf16[4,128,512]{2,1,0:T(8,128)(2,1)S(1)}, bf16[4,128,512]{2,1,0:T(8,128)(2,1)S(1)}, u32[]{:S(2)}, u32[]{:S(2)}) collective-permute-start(bf16[4,128,512]{2,1,0:T(8,128)(2,1)S(1)} %collective-permute-done.3.um), channel_id=1, source_target_pairs={{0,16},{16,0},{1,17},{17,1},{2,18},{18,2},{3,19},{19,3},{4,20},{20... | collective-permute-start | bytes 1572872 | tf_op jit(solution)/shard_map/ppermute | solution.py:252
  22.2 1.0 %copy-start = (bf16[4,128,512]{2,1,0:T(8,128)(2,1)S(1)}, bf16[4,128,512]{2,1,0:T(8,128)(2,1)}, u32[]{:S(2)}) copy-start(bf16[4,128,512]{2,1,0:T(8,128)(2,1)} %lm.3) | copy-start | bytes 1572868
  32.8 7.7 %copy-start.1 = (bf16[4,128,512]{2,1,0:T(8,128)(2,1)S(1)}, bf16[4,128,512]{2,1,0:T(8,128)(2,1)}, u32[]{:S(2)}) copy-start(bf16[4,128,512]{2,1,0:T(8,128)(2,1)} %lm.3) | copy-start | bytes 1572868
  35.5 13.1 %collective-permute-start.9 = (bf16[4,128,512]{2,1,0:T(8,128)(2,1)S(1)}, bf16[4,128,512]{2,1,0:T(8,128)(2,1)S(1)}, u32[]{:S(2)}, u32[]{:S(2)}) collective-permute-start(bf16[4,128,512]{2,1,0:T(8,128)(2,1)S(1)} %get-tuple-element.17), channel_id=1, source_target_pairs={{0,1},{1,3},{2,4},{4,5},{5,7},{6,8},{8,9},{9,11},{10,12},{12,13},{... | collective-permute-start | bytes 1572872 | tf_op jit(solution)/shard_map/ppermute | solution.py:251
  38.5 14.2 %collective-permute-start.10 = (bf16[4,128,512]{2,1,0:T(8,128)(2,1)S(1)}, bf16[4,128,512]{2,1,0:T(8,128)(2,1)S(1)}, u32[]{:S(2)}, u32[]{:S(2)}) collective-permute-start(bf16[4,128,512]{2,1,0:T(8,128)(2,1)S(1)} %get-tuple-element.18), channel_id=1, source_target_pairs={{0,2},{1,5},{2,3},{4,6},{5,9},{6,7},{8,10},{9,13},{10,11},{12,14},... | collective-permute-start | bytes 1572872 | tf_op jit(solution)/shard_map/ppermute | solution.py:251

commit v3 on v2

v3 whole, which is shorter than its diff:
```python
import functools

import jax
import jax.numpy as jnp
from jax import lax
from jax.experimental import pallas as pl
from jax.experimental.pallas import tpu as pltpu
from jax.sharding import PartitionSpec as P

MEMBERS = 256
NBIN = 4
RADIUS = 4
WIDTH = 32
ROWS = 128
SLOT_ROWS = 16
GROUPS = 3
F32 = jnp.float32
BF16 = jnp.bfloat16
VMEM_BYTES = 24 * 1024 * 1024
FULL_BYTES = 60 * 1024 * 1024

FROM_U = {0: 1, 1: 2, 2: 2}
FROM_V = {0: 2, 1: 4, 2: 1}


def routes(size, steps):
    return [(t + step, t) for t in range(size) for r, step in steps.items() if t % 4 == r and t + step < size]


def back(pairs):
    return [(b, a) for a, b in pairs]


def slot_codes(message, slots):
    rows = message.shape[0] - SLOT_ROWS
    parts = message[rows : rows + slots, :3].astype(jnp.int32)
    return parts[:, 0] + (parts[:, 1] << 8) + (parts[:, 2] << 16)


def entries_for(own, other, place, tiles):
    r = place % 4
    out = []
    for foreign, code in enumerate((own, other)):
        first, second = (code >> 8) & 255, code >> 16
        dist = second // tiles
        if foreign:
            first_group = jnp.where(r == 2, 2, 1)
            second_group = jnp.where(dist == jnp.where(r == 1, 2, 1), 3 - first_group, -1)
            second_group = jnp.where(r == 3, -1, second_group)
        else:
            first_group = 0
            second_group = jnp.where(r == 0, dist, jnp.where(r == 2, 3 - dist, jnp.where((r == 1) & (dist == 2), 1, -1)))
            second_group = jnp.where(dist == 0, 0, second_group)
        entry = (code & 255) + ((first + tiles * first_group) << 8) + ((second % tiles + tiles * second_group) << 16)
        out.append(jnp.where((code > 0) & (second_group >= 0), entry, 0))
    return jnp.concatenate(out)


def decode(entry):
    return lax.shift_right_logical(entry, 1) & 127, lax.shift_right_logical(entry, 8) & 255, lax.shift_right_logical(entry, 16)


def fill_weights(along, across, points):
    q = lax.broadcasted_iota(jnp.int32, (WIDTH, points), 1) % WIDTH
    p = lax.broadcasted_iota(jnp.int32, (WIDTH, points), 0)
    gap = (q - p).astype(F32)
    for b in range(NBIN):
        shift = gap + 0.5 * RADIUS * b
        along[b] = jnp.exp(-(shift * shift) / (2.0 * RADIUS * RADIUS))
    levels = points // WIDTH
    row = lax.broadcasted_iota(jnp.int32, (levels, points), 1) // WIDTH
    level = lax.broadcasted_iota(jnp.int32, (levels, points), 0)
    gap = (row - level).astype(F32)
    across[...] = jnp.exp(-(gap * gap) / (2.0 * RADIUS * RADIUS)) / (MEMBERS - 1)


def both(a, tile, cols):
    tiles = (a.shape[1] - SLOT_ROWS) // ROWS
    half = 2 * lax.div(tile, tiles)
    rows = pl.ds(pl.multiple_of(lax.rem(tile, tiles) * ROWS, ROWS), ROWS)
    return jnp.concatenate([a[half, rows, cols], a[half + 1, rows, cols]], axis=0)


def covariance(a, first, second, bins, along, across, put):
    points = a.shape[2]
    right = both(a, second, slice(None))
    weight = along[bins]
    for p0 in range(0, points, ROWS):
        cross = lax.dot_general(
            both(a, first, slice(p0, p0 + ROWS)), right, (((0,), (0,)), ((), ())), preferred_element_type=F32
        )
        for k in range(ROWS // WIDTH):
            level = (p0 // WIDTH) + k
            part = cross[k * WIDTH : (k + 1) * WIDTH]
            put(p0 + k * WIDTH, (part * (weight * across[pl.ds(level, 1), :])).astype(BF16))


def to_first(g, c):
    return lax.dot_general(g, c, (((1,), (1,)), ((), ())), preferred_element_type=F32)


def to_second(g, c):
    return lax.dot_general(g, c, (((1,), (0,)), ((), ())), preferred_element_type=F32)


def load_groups(messages, a, sems):
    copies = []
    for k, message in enumerate(messages):
        copy = pltpu.make_async_copy(message, a.at[k], sems.at[k])
        copy.start()
        copies.append(copy)
    return copies


def put_in(ref):
    def put(row, value):
        ref[pl.ds(row, WIDTH), :] = value

    return put


def pack_kernel(pairs, bins, anomalies, out, pairs_s, bins_s, sems):
    tiles, members = anomalies.shape[0], anomalies.shape[1]
    slots = bins.shape[0]
    copies = [pltpu.make_async_copy(pairs, pairs_s, sems.at[tiles]), pltpu.make_async_copy(bins, bins_s, sems.at[tiles + 1])]
    for t in range(tiles):
        copies.append(pltpu.make_async_copy(anomalies.at[t], out.at[pl.ds(t * members, members), :], sems.at[t]))
    for copy in copies:
        copy.start()
    copies[0].wait()
    copies[1].wait()
    row = lax.broadcasted_iota(jnp.int32, (SLOT_ROWS, 128), 0)
    lane = lax.broadcasted_iota(jnp.int32, (SLOT_ROWS, 128), 1)
    value = jnp.zeros(lane.shape, jnp.int32)
    for k in range(slots):
        first = lax.rem(pairs_s[0, k], tiles)
        second = pairs_s[1, k] - pairs_s[0, k] + first
        parts = jnp.where(lane == 0, 1 + 2 * bins_s[k], jnp.where(lane == 1, first, jnp.where(lane == 2, second, 0)))
        value = jnp.where((row == k) & (bins_s[k] < NBIN), parts, value)
    out[pl.ds(tiles * members, SLOT_ROWS), :] = jnp.zeros((SLOT_ROWS, out.shape[1]), BF16)
    out[pl.ds(tiles * members, SLOT_ROWS), pl.ds(0, 128)] = value.astype(F32).astype(BF16)
    for copy in copies[2:]:
        copy.wait()


def forcing_kernel(obs, innov, out, total):
    tiles = out.shape[0]
    total[...] = jnp.zeros_like(total)

    def step(o, carry):
        t = lax.rem(obs[o], tiles)
        total[t] = total[t] + innov[o].astype(F32)
        return carry

    lax.fori_loop(0, innov.shape[0], step, 0)
    out[...] = total[...].astype(BF16)


def early_kernel(entries, lm, lt, um, ut, vm, vt, g, far, inc_u, inc_v, a, c, along, across, sems):
    tiles, points = g.shape[0], g.shape[2]
    copies = load_groups([lm, lt, um, ut, vm, vt], a, sems)
    fill_weights(along, across, points)
    inc_u[...] = jnp.zeros_like(inc_u)
    inc_v[...] = jnp.zeros_like(inc_v)
    for copy in copies:
        copy.wait()
    slots = entries.shape[0] // 2

    def pair(k, carry):
        entry = entries[k]
        bins, first, second = decode(entry)
        local_first, local_second = first < tiles, second < tiles

        @pl.when((entry > 0) & jnp.logical_not(local_first))
        def _():
            covariance(a, first, second, bins, along, across, put_in(far.at[lax.rem(k, slots)]))

        @pl.when((entry > 0) & local_first & jnp.logical_not(local_second))
        def _():
            covariance(a, first, second, bins, along, across, put_in(c))
            part = to_second(g[first], c[...])

            @pl.when(second < 2 * tiles)
            def _():
                inc_u[second - tiles] = inc_u[second - tiles] + part

            @pl.when(second >= 2 * tiles)
            def _():
                inc_v[second - 2 * tiles] = inc_v[second - 2 * tiles] + part


        return carry

    lax.fori_loop(0, entries.shape[0], pair, 0)


def far_kernel(group, entries, far, inc, g, out, total):
    tiles = g.shape[0]
    slots = entries.shape[0] // 2
    total[...] = inc[...]

    def pair(k, carry):
        entry = entries[slots + k]
        _, first, second = decode(entry)
        here, there = group * tiles, (3 - group) * tiles
        first_here = (first >= here) & (first < here + tiles)

        @pl.when((entry > 0) & first_here)
        def _():
            total[first - here] = total[first - here] + to_first(g[second - there], far[k])

        @pl.when((entry > 0) & jnp.logical_not(first_here))
        def _():
            total[second - here] = total[second - here] + to_second(g[first - there], far[k])

        return carry

    lax.fori_loop(0, slots, pair, 0)
    out[...] = total[...].astype(BF16)


def late_kernel(entries, lm, lt, um, ut, vm, vt, g_l, gu, gv, out, a, g, c, along, across, sems):
    tiles, members, points = g_l.shape
    copies = load_groups([lm, lt, um, ut, vm, vt], a, sems)
    fill_weights(along, across, points)
    g[pl.ds(0, tiles)] = g_l[...]
    g[pl.ds(tiles, tiles)] = gu[...]
    g[pl.ds(2 * tiles, tiles)] = gv[...]
    for copy in copies:
        copy.wait()

    def own(t, carry):
        covariance(a, t, t, 0, along, across, put_in(c))
        out[t] = a[0, pl.ds(pl.multiple_of(t * members, members), members), :].astype(F32) + to_first(g[t], c[...])
        return carry

    lax.fori_loop(0, tiles, own, 0)

    def pair(k, carry):
        entry = entries[k]
        bins, first, second = decode(entry)

        @pl.when((entry > 0) & (first < tiles))
        def _():
            covariance(a, first, second, bins, along, across, put_in(c))
            out[first] = out[first] + to_first(g[second], c[...])

            @pl.when(second < tiles)
            def _():
                out[second] = out[second] + to_second(g[first], c[...])

        return carry

    lax.fori_loop(0, entries.shape[0] // 2, pair, 0)


def final_kernel(total, from_u, from_v, out):
    out[...] = (total[...] + from_u[...].astype(F32) + from_v[...].astype(F32)).astype(BF16)


def call(kernel, outs, places, scratch, us, *args, grant=VMEM_BYTES):
    spec = {"s": pl.BlockSpec(memory_space=pltpu.SMEM), "v": pl.BlockSpec(memory_space=pltpu.VMEM), "h": pl.BlockSpec(memory_space=pl.ANY), "d": pl.BlockSpec(memory_space=pltpu.HBM)}
    return pl.pallas_call(
        kernel,
        out_shape=outs,
        in_specs=[spec[p] for p in places],
        out_specs=jax.tree.map(lambda _: spec["v"], outs),
        scratch_shapes=scratch,
        compiler_params=pltpu.CompilerParams(vmem_limit_bytes=grant),
        cost_estimate=pl.CostEstimate(flops=int(us * 1e7), bytes_accessed=int(us * 3e4), transcendentals=0),
    )(*args)


def per_device(anomalies, innovations, obs_tile, pair_tiles, loc_bin):
    tiles, members, points = anomalies.shape
    slots = loc_bin.shape[0]
    size = lax.axis_size("tile")
    place = lax.axis_index("tile")
    to_u, to_v = routes(size, FROM_U), routes(size, FROM_V)
    send = lambda x, pairs: lax.ppermute(x, "tile", pairs)
    stay = lambda x: pltpu.with_memory_space_constraint(x, pltpu.HBM)
    swap = lambda x: lax.ppermute(x, "mem", [(0, 1), (1, 0)])

    sds = jax.ShapeDtypeStruct
    vm = pltpu.VMEM
    a_l = call(
        pack_kernel,
        sds((tiles * members + SLOT_ROWS, points), BF16),
        "hhh",
        [
            pltpu.SMEM((2, slots), jnp.int32),
            pltpu.SMEM((slots,), jnp.int32),
            pltpu.SemaphoreType.DMA((tiles + 2,)),
        ],
        1,
        stay(pair_tiles.T),
        stay(loc_bin),
        stay(anomalies),
    )
    a_v = send(a_l, to_v)
    a_u = send(a_l, to_u)
    a_t = swap(a_l)
    obs_tile, a_t = lax.optimization_barrier((obs_tile, a_t))
    weights = [vm((NBIN, WIDTH, points), F32), vm((points // WIDTH, points), F32)]
    forcing = call(
        forcing_kernel, sds(anomalies.shape, BF16), "sv", [vm(anomalies.shape, F32)], 1, obs_tile, stay(innovations)
    )
    g_v = send(forcing, to_v)
    g_u = send(forcing, to_u)
    other_list = jnp.where(place % 4 != 2, slot_codes(a_u, slots), slot_codes(a_v, slots))
    entries = entries_for(slot_codes(a_l, slots), other_list, place, tiles)
    a_ut = swap(a_u)
    a_vt = swap(a_v)

    groups = vm((2 * GROUPS, *a_l.shape), BF16)
    square = vm((points, points), BF16)
    far, inc_u, inc_v = call(
        early_kernel,
        (sds((slots, points, points), BF16), sds(anomalies.shape, F32), sds(anomalies.shape, F32)),
        "shhhhhhv",
        [groups, square, *weights, pltpu.SemaphoreType.DMA((2 * GROUPS,))],
        6,
        entries,
        a_l,
        a_t,
        a_u,
        a_ut,
        a_v,
        a_vt,
        forcing,
    )
    finish = lambda group, inc, g: call(
        functools.partial(far_kernel, group),
        sds(anomalies.shape, BF16),
        "svvv",
        [vm(anomalies.shape, F32)],
        1,
        entries,
        far,
        inc,
        g,
    )
    from_u = send(finish(1, inc_u, g_v), back(to_u))
    from_v = send(finish(2, inc_v, g_u), back(to_v))
    total = call(
        late_kernel,
        sds(anomalies.shape, F32),
        "shhhhhhvvv",
        [groups, vm((GROUPS * tiles, members, points), BF16), square, *weights, pltpu.SemaphoreType.DMA((2 * GROUPS,))],
        10,
        entries,
        a_l,
        a_t,
        a_u,
        a_ut,
        a_v,
        a_vt,
        forcing,
        g_u,
        g_v,
    )
    return call(final_kernel, sds(anomalies.shape, BF16), "vvv", [], 1, total, from_v, from_u)


def solution(mesh):
    return jax.shard_map(
        per_device,
        mesh=mesh,
        in_specs=(
            P("tile", "mem", None),
            P("tile", "mem", None),
            P("tile"),
            P("tile", None),
            P("tile"),
        ),
        out_specs=P("tile", "mem", None),
        check_vma=False,
    )
```

time: 54.1 us -> 51.2 us (0.946)
  the two profiles are of different devices: /device:TPU:12 before, /device:TPU:20 now
where the time goes in v3:
time: 51.2 us; the launch traced here: 50.7 us
  Pallas kernels  18 us (35%)
  waiting for transfers between devices  16.3 us (32%)
  starting transfers between devices  14.7 us (29%)
  other arithmetic  0.78 us (2%)
  local copies, waits for them, and re-layouts  0.66 us (1%)
    pallas_call x7, Pallas kernels, call(): pl.pallas_call(kernel, out_shape=outs, in_specs=[spec[p] for p in places]...  18 us
    ppermute x6, starting transfers between devices, per_device(): send = lambda x, pairs: lax.ppermute(x, 'tile', pairs)  14.1 us
    ppermute x6, waiting for transfers between devices, per_device(): send = lambda x, pairs: lax.ppermute(x, 'tile', pairs)  13.1 us
    ppermute x3, waiting for transfers between devices, per_device(): swap = lambda x: lax.ppermute(x, 'mem', [(0, 1), (1, 0)])  3.2 us
  transfers between devices with their start and end apart: 9, of which 6 were waited for; matrix products, arithmetic and copies ran while one was open for 2% of the time, Pallas kernels for 31%

profile of v3, /device:TPU:20, one launch (start us, length us, event | category | flops | bytes accessed | tf_op | source)
XLA Modules:
  0.0 50.7 jit_solution(9129230695789562725)
XLA Ops:
  0.0 1.1 %shard_map.55.lm = bf16[528,512]{1,0:T(8,128)(2,1)S(1)} custom-call(s32[2,8]{1,0:T(2,128)} %bitcast.1, s32[8]{0:T(128)} %bins.1, bf16[4,128,512]{2,1,0:T(8,128)(2,1)} %anomalies.1), custom_call_target="tpu_custom_call" | custom-call | flops 10000000 | bytes 30000 | tf_op jit(solution)/shard_map/pallas_call | solution.py:263
  1.2 2.4 %collective-permute-start.1 = (bf16[528,512]{1,0:T(8,128)(2,1)S(1)}, bf16[528,512]{1,0:T(8,128)(2,1)S(1)}, u32[]{:S(2)}, u32[]{:S(2)}) collective-permute-start(bf16[528,512]{1,0:T(8,128)(2,1)S(1)} %shard_map.55.lm), channel_id=1, source_target_pairs={{2,0},{5,1},{3,2},{6,4},{9,5},{7,6},{10,8},{13,9},{11,10},{14,12},... | collective-permute-start | bytes 1622024 | tf_op jit(solution)/shard_map/ppermute | solution.py:280
  3.6 1.3 %collective-permute-start = (bf16[528,512]{1,0:T(8,128)(2,1)S(1)}, bf16[528,512]{1,0:T(8,128)(2,1)S(1)}, u32[]{:S(2)}, u32[]{:S(2)}) collective-permute-start(bf16[528,512]{1,0:T(8,128)(2,1)S(1)} %shard_map.55.lm), channel_id=1, source_target_pairs={{1,0},{3,1},{4,2},{5,4},{7,5},{8,6},{9,8},{11,9},{12,10},{13,12},{... | collective-permute-start | bytes 1622024 | tf_op jit(solution)/shard_map/ppermute | solution.py:280
  4.9 0.1 collective-permute-start.2
  5.0 0.2 shift-right-arithmetic_reduce_fusion.1
  5.2 0.1 compare_reduce_fusion.1
  5.4 1.5 %collective-permute-done.2.lt = bf16[528,512]{1,0:T(8,128)(2,1)S(1)} collective-permute-done((bf16[528,512]{1,0:T(8,128)(2,1)S(1)}, bf16[528,512]{1,0:T(8,128)(2,1)S(1)}, u32[]{:S(2)}, u32[]{:S(2)}) %collective-permute-start.2) | collective-permute-done | bytes 540704 | tf_op jit(solution)/shard_map/ppermute | solution.py:282
  6.9 0.0 copy-start
  6.9 0.7 %copy-done = s32[8]{0:T(128)S(1)} copy-done((s32[8]{0:T(128)S(1)}, s32[8]{0:T(128)}, u32[]{:S(2)}) %copy-start) | copy-done | bytes 56
  7.5 1.6 %shard_map.56.g_l.g = bf16[4,128,512]{2,1,0:T(8,128)(2,1)S(1)} custom-call(s32[8]{0:T(128)S(1)} %copy-done, bf16[8,128,512]{2,1,0:T(8,128)(2,1)} %innov.1), custom_call_target="tpu_custom_call" | custom-call | flops 10000000 | bytes 30000 | tf_op jit(solution)/shard_map/pallas_call | solution.py:263
  9.1 4.4 %collective-permute-start.6 = (bf16[4,128,512]{2,1,0:T(8,128)(2,1)S(1)}, bf16[4,128,512]{2,1,0:T(8,128)(2,1)S(1)}, u32[]{:S(2)}, u32[]{:S(2)}) collective-permute-start(bf16[4,128,512]{2,1,0:T(8,128)(2,1)S(1)} %shard_map.56.g_l.g), channel_id=1, source_target_pairs={{2,0},{5,1},{3,2},{6,4},{9,5},{7,6},{10,8},{13,9},{11,10},{14,12},... | collective-permute-start | bytes 1572872 | tf_op jit(solution)/shard_map/ppermute | solution.py:280
  13.5 1.3 %collective-permute-start.5 = (bf16[4,128,512]{2,1,0:T(8,128)(2,1)S(1)}, bf16[4,128,512]{2,1,0:T(8,128)(2,1)S(1)}, u32[]{:S(2)}, u32[]{:S(2)}) collective-permute-start(bf16[4,128,512]{2,1,0:T(8,128)(2,1)S(1)} %shard_map.56.g_l.g), channel_id=1, source_target_pairs={{1,0},{3,1},{4,2},{5,4},{7,5},{8,6},{9,8},{11,9},{12,10},{13,12},{... | collective-permute-start | bytes 1572872 | tf_op jit(solution)/shard_map/ppermute | solution.py:280
  14.8 6.5 %collective-permute-done.um = bf16[528,512]{1,0:T(8,128)(2,1)S(1)} collective-permute-done((bf16[528,512]{1,0:T(8,128)(2,1)S(1)}, bf16[528,512]{1,0:T(8,128)(2,1)S(1)}, u32[]{:S(2)}, u32[]{:S(2)}) %collective-permute-start) | collective-permute-done | bytes 540704 | tf_op jit(solution)/shard_map/ppermute | solution.py:280
  21.3 0.0 collective-permute-start.3
  21.4 0.0 collective-permute-done.1.vm
  21.4 0.6 %collective-permute-start.4 = (bf16[528,512]{1,0:T(8,128)(2,1)S(1)}, bf16[528,512]{1,0:T(8,128)(2,1)S(1)}, u32[]{:S(2)}, u32[]{:S(2)}) collective-permute-start(bf16[528,512]{1,0:T(8,128)(2,1)S(1)} %collective-permute-done.1.vm), channel_id=1, source_target_pairs={{0,16},{16,0},{1,17},{17,1},{2,18},{18,2},{3,19},{19,3},{4,20},{20... | collective-permute-start | bytes 1622024 | tf_op jit(solution)/shard_map/ppermute | solution.py:282
  21.9 0.2 shift-right-arithmetic_reduce_fusion
  22.1 0.1 compare_reduce_fusion
  22.3 0.1 pad_add_fusion.entries
  22.4 0.9 %collective-permute-done.3.ut = bf16[528,512]{1,0:T(8,128)(2,1)S(1)} collective-permute-done((bf16[528,512]{1,0:T(8,128)(2,1)S(1)}, bf16[528,512]{1,0:T(8,128)(2,1)S(1)}, u32[]{:S(2)}, u32[]{:S(2)}) %collective-permute-start.3) | collective-permute-done | bytes 540704 | tf_op jit(solution)/shard_map/ppermute | solution.py:282
  23.3 0.8 %collective-permute-done.4.vt = bf16[528,512]{1,0:T(8,128)(2,1)S(1)} collective-permute-done((bf16[528,512]{1,0:T(8,128)(2,1)S(1)}, bf16[528,512]{1,0:T(8,128)(2,1)S(1)}, u32[]{:S(2)}, u32[]{:S(2)}) %collective-permute-start.4) | collective-permute-done | bytes 540704 | tf_op jit(solution)/shard_map/ppermute | solution.py:282
  24.1 4.6 %shard_map.58 = (bf16[8,512,512]{2,1,0:T(8,128)(2,1)S(1)}, f32[4,128,512]{2,1,0:T(8,128)S(1)}, f32[4,128,512]{2,1,0:T(8,128)S(1)}) custom-call(s32[16]{0:T(128)S(1)} %pad_add_fusion.entries, bf16[528,512]{1,0:T(8,128)(2,1)S(1)} %shard_map.55.lm, bf16[528,512]{1,0:T(8,128)(2,1)S(1)} %collective-permute-done.2.lt, ...), custom_call_target="tpu_custom_call" | custom-call | flops 60000000 | bytes 180000 | tf_op jit(solution)/shard_map/pallas_call | solution.py:263
  28.6 0.0 collective-permute-done.6.gv.g
  28.6 1.5 %shard_map.60 = bf16[4,128,512]{2,1,0:T(8,128)(2,1)S(1)} custom-call(s32[16]{0:T(128)S(1)} %pad_add_fusion.entries, bf16[8,512,512]{2,1,0:T(8,128)(2,1)S(1)} %get-tuple-element.12.far, f32[4,128,512]{2,1,0:T(8,128)S(1)} %get-tuple-element.14.inc, bf16[4,128,512]{2,1,0:T(8,128)(2,1)S(1)} %collective-permute-done.6.gv.g), custom_call_target="tpu_custom_call" | custom-call | flops 10000000 | bytes 30000 | tf_op jit(solution)/shard_map/pallas_call | solution.py:263
  30.1 2.7 %collective-permute-start.8 = (bf16[4,128,512]{2,1,0:T(8,128)(2,1)S(1)}, bf16[4,128,512]{2,1,0:T(8,128)(2,1)S(1)}, u32[]{:S(2)}, u32[]{:S(2)}) collective-permute-start(bf16[4,128,512]{2,1,0:T(8,128)(2,1)S(1)} %shard_map.60), channel_id=1, source_target_pairs={{0,1},{1,3},{2,4},{4,5},{5,7},{6,8},{8,9},{9,11},{10,12},{12,13},{... | collective-permute-start | bytes 1572872 | tf_op jit(solution)/shard_map/ppermute | solution.py:280
  32.9 0.0 collective-permute-done.5.gu.g
  32.9 1.7 %shard_map.59 = bf16[4,128,512]{2,1,0:T(8,128)(2,1)S(1)} custom-call(s32[16]{0:T(128)S(1)} %pad_add_fusion.entries, bf16[8,512,512]{2,1,0:T(8,128)(2,1)S(1)} %get-tuple-element.12.far, f32[4,128,512]{2,1,0:T(8,128)S(1)} %get-tuple-element.13.inc, bf16[4,128,512]{2,1,0:T(8,128)(2,1)S(1)} %collective-permute-done.5.gu.g), custom_call_target="tpu_custom_call" | custom-call | flops 10000000 | bytes 30000 | tf_op jit(solution)/shard_map/pallas_call | solution.py:263
  34.7 1.9 %collective-permute-start.7 = (bf16[4,128,512]{2,1,0:T(8,128)(2,1)S(1)}, bf16[4,128,512]{2,1,0:T(8,128)(2,1)S(1)}, u32[]{:S(2)}, u32[]{:S(2)}) collective-permute-start(bf16[4,128,512]{2,1,0:T(8,128)(2,1)S(1)} %shard_map.59), channel_id=1, source_target_pairs={{0,2},{1,5},{2,3},{4,6},{5,9},{6,7},{8,10},{9,13},{10,11},{12,14},... | collective-permute-start | bytes 1572872 | tf_op jit(solution)/shard_map/ppermute | solution.py:280
  36.6 6.5 %shard_map.57.total = f32[4,128,512]{2,1,0:T(8,128)S(1)} custom-call(s32[16]{0:T(128)S(1)} %pad_add_fusion.entries, bf16[528,512]{1,0:T(8,128)(2,1)S(1)} %shard_map.55.lm, bf16[528,512]{1,0:T(8,128)(2,1)S(1)} %collective-permute-done.2.lt, bf16[528,512]{1,0:T(8,128)(2,1)S(1)} %collective-permute-done.um, bf16[528,512]{1,0:T(8,128)(2,1)S(1)} %collective-permute-done.3.ut, ...), custom_call_target="tpu_custom_call" | custom-call | flops 100000000 | bytes 300000 | tf_op jit(solution)/shard_map/pallas_call | solution.py:263
  43.1 0.7 %collective-permute-done.8.from_v = bf16[4,128,512]{2,1,0:T(8,128)(2,1)S(1)} collective-permute-done((bf16[4,128,512]{2,1,0:T(8,128)(2,1)S(1)}, bf16[4,128,512]{2,1,0:T(8,128)(2,1)S(1)}, u32[]{:S(2)}, u32[]{:S(2)}) %collective-permute-start.8) | collective-permute-done | bytes 524320 | tf_op jit(solution)/shard_map/ppermute | solution.py:280
  43.8 5.9 %collective-permute-done.7.from_u = bf16[4,128,512]{2,1,0:T(8,128)(2,1)S(1)} collective-permute-done((bf16[4,128,512]{2,1,0:T(8,128)(2,1)S(1)}, bf16[4,128,512]{2,1,0:T(8,128)(2,1)S(1)}, u32[]{:S(2)}, u32[]{:S(2)}) %collective-permute-start.7) | collective-permute-done | bytes 524320 | tf_op jit(solution)/shard_map/ppermute | solution.py:280
  49.7 1.0 %shard_map.61 = bf16[4,128,512]{2,1,0:T(8,128)(2,1)} custom-call(f32[4,128,512]{2,1,0:T(8,128)S(1)} %shard_map.57.total, bf16[4,128,512]{2,1,0:T(8,128)(2,1)S(1)} %collective-permute-done.7.from_u, bf16[4,128,512]{2,1,0:T(8,128)(2,1)S(1)} %collective-permute-done.8.from_v), custom_call_target="tpu_custom_call" | custom-call | flops 10000000 | bytes 30000 | tf_op jit(solution)/shard_map/pallas_call | solution.py:263
  (5 shorter events, 0.1 us)
Async XLA Ops:
  1.2 20.2 %collective-permute-start.1 = (bf16[528,512]{1,0:T(8,128)(2,1)S(1)}, bf16[528,512]{1,0:T(8,128)(2,1)S(1)}, u32[]{:S(2)}, u32[]{:S(2)}) collective-permute-start(bf16[528,512]{1,0:T(8,128)(2,1)S(1)} %shard_map.55.lm), channel_id=1, source_target_pairs={{2,0},{5,1},{3,2},{6,4},{9,5},{7,6},{10,8},{13,9},{11,10},{14,12},... | collective-permute-start | bytes 1622024 | tf_op jit(solution)/shard_map/ppermute | solution.py:280
  3.6 17.8 %collective-permute-start = (bf16[528,512]{1,0:T(8,128)(2,1)S(1)}, bf16[528,512]{1,0:T(8,128)(2,1)S(1)}, u32[]{:S(2)}, u32[]{:S(2)}) collective-permute-start(bf16[528,512]{1,0:T(8,128)(2,1)S(1)} %shard_map.55.lm), channel_id=1, source_target_pairs={{1,0},{3,1},{4,2},{5,4},{7,5},{8,6},{9,8},{11,9},{12,10},{13,12},{... | collective-permute-start | bytes 1622024 | tf_op jit(solution)/shard_map/ppermute | solution.py:280
  4.9 2.0 %collective-permute-start.2 = (bf16[528,512]{1,0:T(8,128)(2,1)S(1)}, bf16[528,512]{1,0:T(8,128)(2,1)S(1)}, u32[]{:S(2)}, u32[]{:S(2)}) collective-permute-start(bf16[528,512]{1,0:T(8,128)(2,1)S(1)} %shard_map.55.lm), channel_id=1, source_target_pairs={{0,16},{16,0},{1,17},{17,1},{2,18},{18,2},{3,19},{19,3},{4,20},{20... | collective-permute-start | bytes 1622024 | tf_op jit(solution)/shard_map/ppermute | solution.py:282
  6.9 0.7 %copy-start = (s32[8]{0:T(128)S(1)}, s32[8]{0:T(128)}, u32[]{:S(2)}) copy-start(s32[8]{0:T(128)} %obs) | copy-start | bytes 100
  9.1 19.5 %collective-permute-start.6 = (bf16[4,128,512]{2,1,0:T(8,128)(2,1)S(1)}, bf16[4,128,512]{2,1,0:T(8,128)(2,1)S(1)}, u32[]{:S(2)}, u32[]{:S(2)}) collective-permute-start(bf16[4,128,512]{2,1,0:T(8,128)(2,1)S(1)} %shard_map.56.g_l.g), channel_id=1, source_target_pairs={{2,0},{5,1},{3,2},{6,4},{9,5},{7,6},{10,8},{13,9},{11,10},{14,12},... | collective-permute-start | bytes 1572872 | tf_op jit(solution)/shard_map/ppermute | solution.py:280
  13.5 19.4 %collective-permute-start.5 = (bf16[4,128,512]{2,1,0:T(8,128)(2,1)S(1)}, bf16[4,128,512]{2,1,0:T(8,128)(2,1)S(1)}, u32[]{:S(2)}, u32[]{:S(2)}) collective-permute-start(bf16[4,128,512]{2,1,0:T(8,128)(2,1)S(1)} %shard_map.56.g_l.g), channel_id=1, source_target_pairs={{1,0},{3,1},{4,2},{5,4},{7,5},{8,6},{9,8},{11,9},{12,10},{13,12},{... | collective-permute-start | bytes 1572872 | tf_op jit(solution)/shard_map/ppermute | solution.py:280
  21.3 1.9 %collective-permute-start.3 = (bf16[528,512]{1,0:T(8,128)(2,1)S(1)}, bf16[528,512]{1,0:T(8,128)(2,1)S(1)}, u32[]{:S(2)}, u32[]{:S(2)}) collective-permute-start(bf16[528,512]{1,0:T(8,128)(2,1)S(1)} %collective-permute-done.um), channel_id=1, source_target_pairs={{0,16},{16,0},{1,17},{17,1},{2,18},{18,2},{3,19},{19,3},{4,20},{20... | collective-permute-start | bytes 1622024 | tf_op jit(solution)/shard_map/ppermute | solution.py:282
  21.4 2.7 %collective-permute-start.4 = (bf16[528,512]{1,0:T(8,128)(2,1)S(1)}, bf16[528,512]{1,0:T(8,128)(2,1)S(1)}, u32[]{:S(2)}, u32[]{:S(2)}) collective-permute-start(bf16[528,512]{1,0:T(8,128)(2,1)S(1)} %collective-permute-done.1.vm), channel_id=1, source_target_pairs={{0,16},{16,0},{1,17},{17,1},{2,18},{18,2},{3,19},{19,3},{4,20},{20... | collective-permute-start | bytes 1622024 | tf_op jit(solution)/shard_map/ppermute | solution.py:282
  30.1 13.7 %collective-permute-start.8 = (bf16[4,128,512]{2,1,0:T(8,128)(2,1)S(1)}, bf16[4,128,512]{2,1,0:T(8,128)(2,1)S(1)}, u32[]{:S(2)}, u32[]{:S(2)}) collective-permute-start(bf16[4,128,512]{2,1,0:T(8,128)(2,1)S(1)} %shard_map.60), channel_id=1, source_target_pairs={{0,1},{1,3},{2,4},{4,5},{5,7},{6,8},{8,9},{9,11},{10,12},{12,13},{... | collective-permute-start | bytes 1572872 | tf_op jit(solution)/shard_map/ppermute | solution.py:280
  34.7 15.1 %collective-permute-start.7 = (bf16[4,128,512]{2,1,0:T(8,128)(2,1)S(1)}, bf16[4,128,512]{2,1,0:T(8,128)(2,1)S(1)}, u32[]{:S(2)}, u32[]{:S(2)}) collective-permute-start(bf16[4,128,512]{2,1,0:T(8,128)(2,1)S(1)} %shard_map.59), channel_id=1, source_target_pairs={{0,2},{1,5},{2,3},{4,6},{5,9},{6,7},{8,10},{9,13},{10,11},{12,14},... | collective-permute-start | bytes 1572872 | tf_op jit(solution)/shard_map/ppermute | solution.py:280

commit v4 on v3

v4 whole, which is shorter than its diff:
```python
import functools

import jax
import jax.numpy as jnp
from jax import lax
from jax.experimental import pallas as pl
from jax.experimental.pallas import tpu as pltpu
from jax.sharding import PartitionSpec as P

MEMBERS = 256
NBIN = 4
RADIUS = 4
WIDTH = 32
ROWS = 128
SLOT_ROWS = 16
F32 = jnp.float32
BF16 = jnp.bfloat16
VMEM_BYTES = 24 * 1024 * 1024
FULL_BYTES = 60 * 1024 * 1024

FROM_U = {0: 1, 1: 2, 2: 2}
FROM_V = {0: 2, 1: 4, 2: 1}


def routes(size, steps):
    return [(t + step, t) for t in range(size) for r, step in steps.items() if t % 4 == r and t + step < size]


def back(pairs):
    return [(b, a) for a, b in pairs]


def slot_codes(message, slots):
    rows = message.shape[0] - SLOT_ROWS
    parts = message[rows : rows + slots, :3].astype(jnp.int32)
    return parts[:, 0] + (parts[:, 1] << 8) + (parts[:, 2] << 16)


def entries_for(own, other, place, tiles):
    r = place % 4
    first, second = (own >> 8) & 255, own >> 16
    dist = second // tiles
    group = jnp.where(r == 0, dist, jnp.where(r == 2, 3 - dist, jnp.where((r == 1) & (dist == 2), 1, -1)))
    group = jnp.where(dist == 0, 0, group)
    entry = (own & 65535) + ((second % tiles + tiles * group) << 16)
    near = jnp.where((own > 0) & (group >= 0), entry, 0)
    first, second = (other >> 8) & 255, other >> 16
    dist = second // tiles
    second = second % tiles
    turned = r == 2
    entry = (other & 255) + jnp.where(turned, 2 * NBIN, 0)
    entry = entry + (jnp.where(turned, second, first) << 8) + (jnp.where(turned, first, second) << 16)
    far = jnp.where((other > 0) & (r != 3) & (dist == jnp.where(r == 1, 2, 1)), entry, 0)
    return jnp.concatenate([near, far])


def decode(entry):
    return lax.shift_right_logical(entry, 1) & 127, lax.shift_right_logical(entry, 8) & 255, lax.shift_right_logical(entry, 16)


def fill_weights(along, across, points):
    q = lax.broadcasted_iota(jnp.int32, (WIDTH, points), 1) % WIDTH
    p = lax.broadcasted_iota(jnp.int32, (WIDTH, points), 0)
    gap = (q - p).astype(F32)
    for k in range(along.shape[0]):
        shift = (gap if k < NBIN else -gap) + 0.5 * RADIUS * (k % NBIN)
        along[k] = jnp.exp(-(shift * shift) / (2.0 * RADIUS * RADIUS))
    levels = points // WIDTH
    row = lax.broadcasted_iota(jnp.int32, (levels, points), 1) // WIDTH
    level = lax.broadcasted_iota(jnp.int32, (levels, points), 0)
    gap = (row - level).astype(F32)
    across[...] = jnp.exp(-(gap * gap) / (2.0 * RADIUS * RADIUS)) / (MEMBERS - 1)


def both(halves, tile, cols):
    rows = pl.ds(pl.multiple_of(tile * ROWS, ROWS), ROWS)
    return jnp.concatenate([half[rows, cols] for half in halves], axis=0)


def covariance(left, right, first, second, weight, across, out):
    points = out.shape[1]
    values = both(right, second, slice(None))
    for p0 in range(0, points, ROWS):
        cross = lax.dot_general(
            both(left, first, slice(p0, p0 + ROWS)), values, (((0,), (0,)), ((), ())), preferred_element_type=F32
        )
        for row in range(0, ROWS, WIDTH):
            level = (p0 + row) // WIDTH
            part = cross[row : row + WIDTH] * (weight * across[pl.ds(level, 1), :])
            out[pl.ds(p0 + row, WIDTH), :] = part.astype(BF16)


def to_first(g, c):
    return lax.dot_general(g, c, (((1,), (1,)), ((), ())), preferred_element_type=F32)


def to_second(g, c):
    return lax.dot_general(g, c, (((1,), (0,)), ((), ())), preferred_element_type=F32)


def pack_kernel(pairs, bins, anomalies, out, pairs_s, bins_s, sems):
    tiles, members = anomalies.shape[0], anomalies.shape[1]
    slots = bins.shape[0]
    copies = [pltpu.make_async_copy(pairs, pairs_s, sems.at[tiles]), pltpu.make_async_copy(bins, bins_s, sems.at[tiles + 1])]
    for t in range(tiles):
        copies.append(pltpu.make_async_copy(anomalies.at[t], out.at[pl.ds(t * members, members), :], sems.at[t]))
    for copy in copies:
        copy.start()
    copies[0].wait()
    copies[1].wait()
    row = lax.broadcasted_iota(jnp.int32, (SLOT_ROWS, 128), 0)
    lane = lax.broadcasted_iota(jnp.int32, (SLOT_ROWS, 128), 1)
    value = jnp.zeros(lane.shape, jnp.int32)
    for k in range(slots):
        first = lax.rem(pairs_s[0, k], tiles)
        second = pairs_s[1, k] - pairs_s[0, k] + first
        parts = jnp.where(lane == 0, 1 + 2 * bins_s[k], jnp.where(lane == 1, first, jnp.where(lane == 2, second, 0)))
        value = jnp.where((row == k) & (bins_s[k] < NBIN), parts, value)
    out[pl.ds(tiles * members, SLOT_ROWS), :] = jnp.zeros((SLOT_ROWS, out.shape[1]), BF16)
    out[pl.ds(tiles * members, SLOT_ROWS), pl.ds(0, 128)] = value.astype(F32).astype(BF16)
    for copy in copies[2:]:
        copy.wait()


def forcing_kernel(obs, innov, out, total):
    tiles = out.shape[0]
    total[...] = jnp.zeros_like(total)

    def step(o, carry):
        t = lax.rem(obs[o], tiles)
        total[t] = total[t] + innov[o].astype(F32)
        return carry

    lax.fori_loop(0, innov.shape[0], step, 0)
    out[...] = total[...].astype(BF16)


def add_near(group, entries, left, right, g, inc, c, along, across):
    tiles = g.shape[0]

    def pair(k, carry):
        entry = entries[k]
        bins, first, second = decode(entry)
        here = second - group * tiles

        @pl.when((entry > 0) & (here >= 0) & (here < tiles))
        def _():
            covariance(left, right, first, here, along[bins], across, c)
            inc[here] = inc[here] + to_second(g[first], c[...])

        return carry

    lax.fori_loop(0, entries.shape[0] // 2, pair, 0)


def early_kernel(entries, lm, lt, um, ut, vm, vt, g, far, inc_u, inc_v, c, along, across):
    fill_weights(along, across, c.shape[1])
    inc_u[...] = jnp.zeros_like(inc_u)
    inc_v[...] = jnp.zeros_like(inc_v)
    add_near(1, entries, (lm, lt), (um, ut), g, inc_u, c, along, across)
    add_near(2, entries, (lm, lt), (vm, vt), g, inc_v, c, along, across)
    slots = entries.shape[0] // 2

    def pair(k, carry):
        entry = entries[slots + k]
        bins, first, second = decode(entry)

        @pl.when(entry > 0)
        def _():
            covariance((um, ut), (vm, vt), first, second, along[bins], across, far.at[k])

        return carry

    lax.fori_loop(0, slots, pair, 0)


def far_kernel(group, entries, far, inc, g, out, total):
    slots = entries.shape[0] // 2
    total[...] = inc[...]

    def pair(k, carry):
        entry = entries[slots + k]
        _, first, second = decode(entry)

        @pl.when(entry > 0)
        def _():
            if group == 1:
                total[first] = total[first] + to_first(g[second], far[k])
            else:
                total[second] = total[second] + to_second(g[first], far[k])

        return carry

    lax.fori_loop(0, slots, pair, 0)
    out[...] = total[...].astype(BF16)


def late_kernel(entries, lm, lt, um, ut, vm, vt, g_l, g_u, g_v, out, c, along, across):
    tiles, members, points = g_l.shape
    fill_weights(along, across, points)

    def own(t, carry):
        covariance((lm, lt), (lm, lt), t, t, along[0], across, c)
        rows = pl.ds(pl.multiple_of(t * members, members), members)
        out[t] = lm[rows, :].astype(F32) + to_first(g_l[t], c[...])
        return carry

    lax.fori_loop(0, tiles, own, 0)

    def pair(k, carry):
        entry = entries[k]
        bins, first, second = decode(entry)

        for group, (right, g) in enumerate((((lm, lt), g_l), ((um, ut), g_u), ((vm, vt), g_v))):
            here = second - group * tiles

            @pl.when((entry > 0) & (here >= 0) & (here < tiles))
            def _():
                covariance((lm, lt), right, first, here, along[bins], across, c)
                out[first] = out[first] + to_first(g[here], c[...])
                if group == 0:
                    out[here] = out[here] + to_second(g_l[first], c[...])

        return carry

    lax.fori_loop(0, entries.shape[0] // 2, pair, 0)


def final_kernel(total, from_u, from_v, out, done, sems):
    copies = []
    for t in range(total.shape[0]):
        done[t] = (total[t] + from_u[t].astype(F32) + from_v[t].astype(F32)).astype(BF16)
        copies.append(pltpu.make_async_copy(done.at[t], out.at[t], sems.at[t]))
        copies[-1].start()
    for copy in copies:
        copy.wait()


def call(kernel, outs, places, scratch, us, *args, grant=VMEM_BYTES, to="v"):
    spec = {"s": pl.BlockSpec(memory_space=pltpu.SMEM), "v": pl.BlockSpec(memory_space=pltpu.VMEM), "h": pl.BlockSpec(memory_space=pl.ANY), "d": pl.BlockSpec(memory_space=pltpu.HBM)}
    return pl.pallas_call(
        kernel,
        out_shape=outs,
        in_specs=[spec[p] for p in places],
        out_specs=jax.tree.map(lambda _: spec[to], outs),
        scratch_shapes=scratch,
        compiler_params=pltpu.CompilerParams(vmem_limit_bytes=grant),
        cost_estimate=pl.CostEstimate(flops=int(us * 1e7), bytes_accessed=int(us * 3e4), transcendentals=0),
    )(*args)


def per_device(anomalies, innovations, obs_tile, pair_tiles, loc_bin):
    tiles, members, points = anomalies.shape
    slots = loc_bin.shape[0]
    size = lax.axis_size("tile")
    place = lax.axis_index("tile")
    to_u, to_v = routes(size, FROM_U), routes(size, FROM_V)
    send = lambda x, pairs: lax.ppermute(x, "tile", pairs)
    stay = lambda x: pltpu.with_memory_space_constraint(x, pltpu.HBM)
    swap = lambda x: lax.ppermute(x, "mem", [(0, 1), (1, 0)])

    sds = jax.ShapeDtypeStruct
    vm = pltpu.VMEM
    a_l = call(
        pack_kernel,
        sds((tiles * members + SLOT_ROWS, points), BF16),
        "hhh",
        [
            pltpu.SMEM((2, slots), jnp.int32),
            pltpu.SMEM((slots,), jnp.int32),
            pltpu.SemaphoreType.DMA((tiles + 2,)),
        ],
        1,
        stay(pair_tiles.T),
        stay(loc_bin),
        stay(anomalies),
    )
    a_v = send(a_l, to_v)
    a_u = send(a_l, to_u)
    a_t = swap(a_l)
    obs_tile, a_t = lax.optimization_barrier((obs_tile, a_t))
    forcing = call(
        forcing_kernel, sds(anomalies.shape, BF16), "sv", [vm(anomalies.shape, F32)], 1, obs_tile, stay(innovations)
    )
    g_v = send(forcing, to_v)
    g_u = send(forcing, to_u)
    other_list = jnp.where(place % 4 != 2, slot_codes(a_u, slots), slot_codes(a_v, slots))
    entries = entries_for(slot_codes(a_l, slots), other_list, place, tiles)
    square = vm((points, points), BF16)
    across = vm((points // WIDTH, points), F32)
    weights = [square, vm((NBIN, WIDTH, points), F32), across]
    weights_far = [square, vm((2 * NBIN, WIDTH, points), F32), across]

    a_vt = swap(a_v)
    a_ut = swap(a_u)
    far, inc_u, inc_v = call(
        early_kernel,
        (sds((slots, points, points), BF16), sds(anomalies.shape, F32), sds(anomalies.shape, F32)),
        "svvvvvvv",
        weights_far,
        4,
        entries,
        a_l,
        a_t,
        a_u,
        a_ut,
        a_v,
        a_vt,
        forcing,
    )
    finish = lambda group, inc, g: call(
        functools.partial(far_kernel, group),
        sds(anomalies.shape, BF16),
        "svvv",
        [vm(anomalies.shape, F32)],
        1,
        entries,
        far,
        inc,
        g,
    )
    from_u = send(finish(1, inc_u, g_v), back(to_u))
    from_v = send(finish(2, inc_v, g_u), back(to_v))
    total = call(
        late_kernel,
        sds(anomalies.shape, F32),
        "svvvvvvvvv",
        weights,
        10,
        entries,
        a_l,
        a_t,
        a_u,
        a_ut,
        a_v,
        a_vt,
        forcing,
        g_u,
        g_v,
    )
    return call(
        final_kernel,
        sds(anomalies.shape, BF16),
        "vvv",
        [vm(anomalies.shape, BF16), pltpu.SemaphoreType.DMA((tiles,))],
        1,
        total,
        from_v,
        from_u,
        to="h",
    )


def solution(mesh):
    return jax.shard_map(
        per_device,
        mesh=mesh,
        in_specs=(
            P("tile", "mem", None),
            P("tile", "mem", None),
            P("tile"),
            P("tile", None),
            P("tile"),
        ),
        out_specs=P("tile", "mem", None),
        check_vma=False,
    )
```

time: 51.2 us -> 50.9 us (level)
  the two profiles are of different devices: /device:TPU:20 before, /device:TPU:0 now
where the time goes in v4:
time: 50.9 us; the launch traced here: 51 us
  waiting for transfers between devices  18.8 us (37%)
  Pallas kernels  16.7 us (33%)
  starting transfers between devices  13.9 us (27%)
  other arithmetic  0.81 us (2%)
  local copies, waits for them, and re-layouts  0.65 us (1%)
    pallas_call x7, Pallas kernels, call(): pl.pallas_call(kernel, out_shape=outs, in_specs=[spec[p] for p in places]...  16.7 us
    ppermute x6, waiting for transfers between devices, per_device(): send = lambda x, pairs: lax.ppermute(x, 'tile', pairs)  15.9 us
    ppermute x6, starting transfers between devices, per_device(): send = lambda x, pairs: lax.ppermute(x, 'tile', pairs)  12.8 us
    ppermute x3, waiting for transfers between devices, per_device(): swap = lambda x: lax.ppermute(x, 'mem', [(0, 1), (1, 0)])  2.86 us
    ppermute x3, starting transfers between devices, per_device(): swap = lambda x: lax.ppermute(x, 'mem', [(0, 1), (1, 0)])  1.08 us
  transfers between devices with their start and end apart: 9, of which 6 were waited for; matrix products, arithmetic and copies ran while one was open for 2% of the time, Pallas kernels for 29%

profile of v4, /device:TPU:0, one launch (start us, length us, event | category | flops | bytes accessed | tf_op | source)
XLA Modules:
  0.0 51.0 jit_solution(9569548552397754152)
XLA Ops:
  0.0 1.1 %shard_map.55.lm = bf16[528,512]{1,0:T(8,128)(2,1)S(1)} custom-call(s32[2,8]{1,0:T(2,128)} %bitcast.1, s32[8]{0:T(128)} %bins.1, bf16[4,128,512]{2,1,0:T(8,128)(2,1)} %anomalies.1), custom_call_target="tpu_custom_call" | custom-call | flops 10000000 | bytes 30000 | tf_op jit(solution)/shard_map/pallas_call | solution.py:241
  1.2 1.3 %collective-permute-start.1 = (bf16[528,512]{1,0:T(8,128)(2,1)S(1)}, bf16[528,512]{1,0:T(8,128)(2,1)S(1)}, u32[]{:S(2)}, u32[]{:S(2)}) collective-permute-start(bf16[528,512]{1,0:T(8,128)(2,1)S(1)} %shard_map.55.lm), channel_id=1, source_target_pairs={{2,0},{5,1},{3,2},{6,4},{9,5},{7,6},{10,8},{13,9},{11,10},{14,12},... | collective-permute-start | bytes 1622024 | tf_op jit(solution)/shard_map/ppermute | solution.py:258
  2.5 1.3 %collective-permute-start = (bf16[528,512]{1,0:T(8,128)(2,1)S(1)}, bf16[528,512]{1,0:T(8,128)(2,1)S(1)}, u32[]{:S(2)}, u32[]{:S(2)}) collective-permute-start(bf16[528,512]{1,0:T(8,128)(2,1)S(1)} %shard_map.55.lm), channel_id=1, source_target_pairs={{1,0},{3,1},{4,2},{5,4},{7,5},{8,6},{9,8},{11,9},{12,10},{13,12},{... | collective-permute-start | bytes 1622024 | tf_op jit(solution)/shard_map/ppermute | solution.py:258
  3.8 0.5 %collective-permute-start.2 = (bf16[528,512]{1,0:T(8,128)(2,1)S(1)}, bf16[528,512]{1,0:T(8,128)(2,1)S(1)}, u32[]{:S(2)}, u32[]{:S(2)}) collective-permute-start(bf16[528,512]{1,0:T(8,128)(2,1)S(1)} %shard_map.55.lm), channel_id=1, source_target_pairs={{0,16},{16,0},{1,17},{17,1},{2,18},{18,2},{3,19},{19,3},{4,20},{20... | collective-permute-start | bytes 1622024 | tf_op jit(solution)/shard_map/ppermute | solution.py:260
  4.3 0.2 shift-right-arithmetic_reduce_fusion.1
  4.5 0.1 compare_reduce_fusion
  4.6 1.2 %collective-permute-done.2.lt = bf16[528,512]{1,0:T(8,128)(2,1)S(1)} collective-permute-done((bf16[528,512]{1,0:T(8,128)(2,1)S(1)}, bf16[528,512]{1,0:T(8,128)(2,1)S(1)}, u32[]{:S(2)}, u32[]{:S(2)}) %collective-permute-start.2) | collective-permute-done | bytes 540704 | tf_op jit(solution)/shard_map/ppermute | solution.py:260
  5.8 0.0 copy-start
  5.8 0.7 %copy-done = s32[8]{0:T(128)S(1)} copy-done((s32[8]{0:T(128)S(1)}, s32[8]{0:T(128)}, u32[]{:S(2)}) %copy-start) | copy-done | bytes 56
  6.5 1.6 %shard_map.56.g_l.g = bf16[4,128,512]{2,1,0:T(8,128)(2,1)S(1)} custom-call(s32[8]{0:T(128)S(1)} %copy-done, bf16[8,128,512]{2,1,0:T(8,128)(2,1)} %innov.1), custom_call_target="tpu_custom_call" | custom-call | flops 10000000 | bytes 30000 | tf_op jit(solution)/shard_map/pallas_call | solution.py:241
  8.1 1.3 %collective-permute-start.6 = (bf16[4,128,512]{2,1,0:T(8,128)(2,1)S(1)}, bf16[4,128,512]{2,1,0:T(8,128)(2,1)S(1)}, u32[]{:S(2)}, u32[]{:S(2)}) collective-permute-start(bf16[4,128,512]{2,1,0:T(8,128)(2,1)S(1)} %shard_map.56.g_l.g), channel_id=1, source_target_pairs={{2,0},{5,1},{3,2},{6,4},{9,5},{7,6},{10,8},{13,9},{11,10},{14,12},... | collective-permute-start | bytes 1572872 | tf_op jit(solution)/shard_map/ppermute | solution.py:258
  9.4 1.3 %collective-permute-start.5 = (bf16[4,128,512]{2,1,0:T(8,128)(2,1)S(1)}, bf16[4,128,512]{2,1,0:T(8,128)(2,1)S(1)}, u32[]{:S(2)}, u32[]{:S(2)}) collective-permute-start(bf16[4,128,512]{2,1,0:T(8,128)(2,1)S(1)} %shard_map.56.g_l.g), channel_id=1, source_target_pairs={{1,0},{3,1},{4,2},{5,4},{7,5},{8,6},{9,8},{11,9},{12,10},{13,12},{... | collective-permute-start | bytes 1572872 | tf_op jit(solution)/shard_map/ppermute | solution.py:258
  10.7 9.7 %collective-permute-done.um = bf16[528,512]{1,0:T(8,128)(2,1)S(1)} collective-permute-done((bf16[528,512]{1,0:T(8,128)(2,1)S(1)}, bf16[528,512]{1,0:T(8,128)(2,1)S(1)}, u32[]{:S(2)}, u32[]{:S(2)}) %collective-permute-start) | collective-permute-done | bytes 540704 | tf_op jit(solution)/shard_map/ppermute | solution.py:258
  20.4 0.0 collective-permute-start.3
  20.4 0.0 collective-permute-done.1.vm
  20.4 0.6 %collective-permute-start.4 = (bf16[528,512]{1,0:T(8,128)(2,1)S(1)}, bf16[528,512]{1,0:T(8,128)(2,1)S(1)}, u32[]{:S(2)}, u32[]{:S(2)}) collective-permute-start(bf16[528,512]{1,0:T(8,128)(2,1)S(1)} %collective-permute-done.1.vm), channel_id=1, source_target_pairs={{0,16},{16,0},{1,17},{17,1},{2,18},{18,2},{3,19},{19,3},{4,20},{20... | collective-permute-start | bytes 1622024 | tf_op jit(solution)/shard_map/ppermute | solution.py:260
  21.0 0.2 shift-right-arithmetic_reduce_fusion
  21.2 0.1 and_reduce_fusion.2
  21.3 0.1 pad_add_fusion.entries
  21.4 0.9 %collective-permute-done.3.ut = bf16[528,512]{1,0:T(8,128)(2,1)S(1)} collective-permute-done((bf16[528,512]{1,0:T(8,128)(2,1)S(1)}, bf16[528,512]{1,0:T(8,128)(2,1)S(1)}, u32[]{:S(2)}, u32[]{:S(2)}) %collective-permute-start.3) | collective-permute-done | bytes 540704 | tf_op jit(solution)/shard_map/ppermute | solution.py:260
  22.3 0.8 %collective-permute-done.4.vt = bf16[528,512]{1,0:T(8,128)(2,1)S(1)} collective-permute-done((bf16[528,512]{1,0:T(8,128)(2,1)S(1)}, bf16[528,512]{1,0:T(8,128)(2,1)S(1)}, u32[]{:S(2)}, u32[]{:S(2)}) %collective-permute-start.4) | collective-permute-done | bytes 540704 | tf_op jit(solution)/shard_map/ppermute | solution.py:260
  23.1 3.9 %shard_map.58 = (bf16[8,512,512]{2,1,0:T(8,128)(2,1)S(1)}, f32[4,128,512]{2,1,0:T(8,128)S(1)}, f32[4,128,512]{2,1,0:T(8,128)S(1)}) custom-call(s32[16]{0:T(128)S(1)} %pad_add_fusion.entries, bf16[528,512]{1,0:T(8,128)(2,1)S(1)} %shard_map.55.lm, bf16[528,512]{1,0:T(8,128)(2,1)S(1)} %collective-permute-done.2.lt, ...), custom_call_target="tpu_custom_call" | custom-call | flops 40000000 | bytes 120000 | tf_op jit(solution)/shard_map/pallas_call | solution.py:241
  27.0 2.5 %collective-permute-done.6.g_v.g = bf16[4,128,512]{2,1,0:T(8,128)(2,1)S(1)} collective-permute-done((bf16[4,128,512]{2,1,0:T(8,128)(2,1)S(1)}, bf16[4,128,512]{2,1,0:T(8,128)(2,1)S(1)}, u32[]{:S(2)}, u32[]{:S(2)}) %collective-permute-start.6) | collective-permute-done | bytes 524320 | tf_op jit(solution)/shard_map/ppermute | solution.py:258
  29.5 1.4 %shard_map.60 = bf16[4,128,512]{2,1,0:T(8,128)(2,1)S(1)} custom-call(s32[16]{0:T(128)S(1)} %pad_add_fusion.entries, bf16[8,512,512]{2,1,0:T(8,128)(2,1)S(1)} %get-tuple-element.12.far, f32[4,128,512]{2,1,0:T(8,128)S(1)} %get-tuple-element.14.inc, bf16[4,128,512]{2,1,0:T(8,128)(2,1)S(1)} %collective-permute-done.6.g_v.g), custom_call_target="tpu_custom_call" | custom-call | flops 10000000 | bytes 30000 | tf_op jit(solution)/shard_map/pallas_call | solution.py:241
  30.9 3.0 %collective-permute-start.8 = (bf16[4,128,512]{2,1,0:T(8,128)(2,1)S(1)}, bf16[4,128,512]{2,1,0:T(8,128)(2,1)S(1)}, u32[]{:S(2)}, u32[]{:S(2)}) collective-permute-start(bf16[4,128,512]{2,1,0:T(8,128)(2,1)S(1)} %shard_map.60), channel_id=1, source_target_pairs={{0,1},{1,3},{2,4},{4,5},{5,7},{6,8},{8,9},{9,11},{10,12},{12,13},{... | collective-permute-start | bytes 1572872 | tf_op jit(solution)/shard_map/ppermute | solution.py:258
  34.0 0.0 collective-permute-done.5.g_u.g
  34.0 1.2 %shard_map.59 = bf16[4,128,512]{2,1,0:T(8,128)(2,1)S(1)} custom-call(s32[16]{0:T(128)S(1)} %pad_add_fusion.entries, bf16[8,512,512]{2,1,0:T(8,128)(2,1)S(1)} %get-tuple-element.12.far, f32[4,128,512]{2,1,0:T(8,128)S(1)} %get-tuple-element.13.inc, bf16[4,128,512]{2,1,0:T(8,128)(2,1)S(1)} %collective-permute-done.5.g_u.g), custom_call_target="tpu_custom_call" | custom-call | flops 10000000 | bytes 30000 | tf_op jit(solution)/shard_map/pallas_call | solution.py:241
  35.2 4.6 %collective-permute-start.7 = (bf16[4,128,512]{2,1,0:T(8,128)(2,1)S(1)}, bf16[4,128,512]{2,1,0:T(8,128)(2,1)S(1)}, u32[]{:S(2)}, u32[]{:S(2)}) collective-permute-start(bf16[4,128,512]{2,1,0:T(8,128)(2,1)S(1)} %shard_map.59), channel_id=1, source_target_pairs={{0,2},{1,5},{2,3},{4,6},{5,9},{6,7},{8,10},{9,13},{10,11},{12,14},... | collective-permute-start | bytes 1572872 | tf_op jit(solution)/shard_map/ppermute | solution.py:258
  39.8 6.7 %shard_map.57.total = f32[4,128,512]{2,1,0:T(8,128)S(1)} custom-call(s32[16]{0:T(128)S(1)} %pad_add_fusion.entries, bf16[528,512]{1,0:T(8,128)(2,1)S(1)} %shard_map.55.lm, bf16[528,512]{1,0:T(8,128)(2,1)S(1)} %collective-permute-done.2.lt, bf16[528,512]{1,0:T(8,128)(2,1)S(1)} %collective-permute-done.um, bf16[528,512]{1,0:T(8,128)(2,1)S(1)} %collective-permute-done.3.ut, ...), custom_call_target="tpu_custom_call" | custom-call | flops 100000000 | bytes 300000 | tf_op jit(solution)/shard_map/pallas_call | solution.py:241
  46.5 0.0 collective-permute-done.8.from_v
  46.6 3.6 %collective-permute-done.7.from_u = bf16[4,128,512]{2,1,0:T(8,128)(2,1)S(1)} collective-permute-done((bf16[4,128,512]{2,1,0:T(8,128)(2,1)S(1)}, bf16[4,128,512]{2,1,0:T(8,128)(2,1)S(1)}, u32[]{:S(2)}, u32[]{:S(2)}) %collective-permute-start.7) | collective-permute-done | bytes 524320 | tf_op jit(solution)/shard_map/ppermute | solution.py:258
  50.2 0.9 %shard_map.61 = bf16[4,128,512]{2,1,0:T(8,128)(2,1)} custom-call(f32[4,128,512]{2,1,0:T(8,128)S(1)} %shard_map.57.total, bf16[4,128,512]{2,1,0:T(8,128)(2,1)S(1)} %collective-permute-done.7.from_u, bf16[4,128,512]{2,1,0:T(8,128)(2,1)S(1)} %collective-permute-done.8.from_v), custom_call_target="tpu_custom_call" | custom-call | flops 10000000 | bytes 30000 | tf_op jit(solution)/shard_map/pallas_call | solution.py:241
  (5 shorter events, 0.1 us)
Async XLA Ops:
  1.2 19.3 %collective-permute-start.1 = (bf16[528,512]{1,0:T(8,128)(2,1)S(1)}, bf16[528,512]{1,0:T(8,128)(2,1)S(1)}, u32[]{:S(2)}, u32[]{:S(2)}) collective-permute-start(bf16[528,512]{1,0:T(8,128)(2,1)S(1)} %shard_map.55.lm), channel_id=1, source_target_pairs={{2,0},{5,1},{3,2},{6,4},{9,5},{7,6},{10,8},{13,9},{11,10},{14,12},... | collective-permute-start | bytes 1622024 | tf_op jit(solution)/shard_map/ppermute | solution.py:258
  2.5 17.9 %collective-permute-start = (bf16[528,512]{1,0:T(8,128)(2,1)S(1)}, bf16[528,512]{1,0:T(8,128)(2,1)S(1)}, u32[]{:S(2)}, u32[]{:S(2)}) collective-permute-start(bf16[528,512]{1,0:T(8,128)(2,1)S(1)} %shard_map.55.lm), channel_id=1, source_target_pairs={{1,0},{3,1},{4,2},{5,4},{7,5},{8,6},{9,8},{11,9},{12,10},{13,12},{... | collective-permute-start | bytes 1622024 | tf_op jit(solution)/shard_map/ppermute | solution.py:258
  3.8 2.1 %collective-permute-start.2 = (bf16[528,512]{1,0:T(8,128)(2,1)S(1)}, bf16[528,512]{1,0:T(8,128)(2,1)S(1)}, u32[]{:S(2)}, u32[]{:S(2)}) collective-permute-start(bf16[528,512]{1,0:T(8,128)(2,1)S(1)} %shard_map.55.lm), channel_id=1, source_target_pairs={{0,16},{16,0},{1,17},{17,1},{2,18},{18,2},{3,19},{19,3},{4,20},{20... | collective-permute-start | bytes 1622024 | tf_op jit(solution)/shard_map/ppermute | solution.py:260
  5.8 0.7 %copy-start = (s32[8]{0:T(128)S(1)}, s32[8]{0:T(128)}, u32[]{:S(2)}) copy-start(s32[8]{0:T(128)} %obs) | copy-start | bytes 100
  8.1 21.5 %collective-permute-start.6 = (bf16[4,128,512]{2,1,0:T(8,128)(2,1)S(1)}, bf16[4,128,512]{2,1,0:T(8,128)(2,1)S(1)}, u32[]{:S(2)}, u32[]{:S(2)}) collective-permute-start(bf16[4,128,512]{2,1,0:T(8,128)(2,1)S(1)} %shard_map.56.g_l.g), channel_id=1, source_target_pairs={{2,0},{5,1},{3,2},{6,4},{9,5},{7,6},{10,8},{13,9},{11,10},{14,12},... | collective-permute-start | bytes 1572872 | tf_op jit(solution)/shard_map/ppermute | solution.py:258
  9.4 24.6 %collective-permute-start.5 = (bf16[4,128,512]{2,1,0:T(8,128)(2,1)S(1)}, bf16[4,128,512]{2,1,0:T(8,128)(2,1)S(1)}, u32[]{:S(2)}, u32[]{:S(2)}) collective-permute-start(bf16[4,128,512]{2,1,0:T(8,128)(2,1)S(1)} %shard_map.56.g_l.g), channel_id=1, source_target_pairs={{1,0},{3,1},{4,2},{5,4},{7,5},{8,6},{9,8},{11,9},{12,10},{13,12},{... | collective-permute-start | bytes 1572872 | tf_op jit(solution)/shard_map/ppermute | solution.py:258
  20.4 1.9 %collective-permute-start.3 = (bf16[528,512]{1,0:T(8,128)(2,1)S(1)}, bf16[528,512]{1,0:T(8,128)(2,1)S(1)}, u32[]{:S(2)}, u32[]{:S(2)}) collective-permute-start(bf16[528,512]{1,0:T(8,128)(2,1)S(1)} %collective-permute-done.um), channel_id=1, source_target_pairs={{0,16},{16,0},{1,17},{17,1},{2,18},{18,2},{3,19},{19,3},{4,20},{20... | collective-permute-start | bytes 1622024 | tf_op jit(solution)/shard_map/ppermute | solution.py:260
  20.4 2.7 %collective-permute-start.4 = (bf16[528,512]{1,0:T(8,128)(2,1)S(1)}, bf16[528,512]{1,0:T(8,128)(2,1)S(1)}, u32[]{:S(2)}, u32[]{:S(2)}) collective-permute-start(bf16[528,512]{1,0:T(8,128)(2,1)S(1)} %collective-permute-done.1.vm), channel_id=1, source_target_pairs={{0,16},{16,0},{1,17},{17,1},{2,18},{18,2},{3,19},{19,3},{4,20},{20... | collective-permute-start | bytes 1622024 | tf_op jit(solution)/shard_map/ppermute | solution.py:260
  30.9 15.6 %collective-permute-start.8 = (bf16[4,128,512]{2,1,0:T(8,128)(2,1)S(1)}, bf16[4,128,512]{2,1,0:T(8,128)(2,1)S(1)}, u32[]{:S(2)}, u32[]{:S(2)}) collective-permute-start(bf16[4,128,512]{2,1,0:T(8,128)(2,1)S(1)} %shard_map.60), channel_id=1, source_target_pairs={{0,1},{1,3},{2,4},{4,5},{5,7},{6,8},{8,9},{9,11},{10,12},{12,13},{... | collective-permute-start | bytes 1572872 | tf_op jit(solution)/shard_map/ppermute | solution.py:258
  35.2 15.0 %collective-permute-start.7 = (bf16[4,128,512]{2,1,0:T(8,128)(2,1)S(1)}, bf16[4,128,512]{2,1,0:T(8,128)(2,1)S(1)}, u32[]{:S(2)}, u32[]{:S(2)}) collective-permute-start(bf16[4,128,512]{2,1,0:T(8,128)(2,1)S(1)} %shard_map.59), channel_id=1, source_target_pairs={{0,2},{1,5},{2,3},{4,6},{5,9},{6,7},{8,10},{9,13},{10,11},{12,14},... | collective-permute-start | bytes 1572872 | tf_op jit(solution)/shard_map/ppermute | solution.py:258

commit v5 on v4

--- a/solution.py
+++ b/solution.py
@@ -51,11 +51,18 @@
     entry = (other & 255) + jnp.where(turned, 2 * NBIN, 0)
     entry = entry + (jnp.where(turned, second, first) << 8) + (jnp.where(turned, first, second) << 16)
     far = jnp.where((other > 0) & (r != 3) & (dist == jnp.where(r == 1, 2, 1)), entry, 0)
-    return jnp.concatenate([near, far])
+    return near[None], far[None]
 
 
 def decode(entry):
     return lax.shift_right_logical(entry, 1) & 127, lax.shift_right_logical(entry, 8) & 255, lax.shift_right_logical(entry, 16)
+
+
+def read_slots(entries, ints):
+    row = entries[...]
+    lane = lax.broadcasted_iota(jnp.int32, row.shape, 1)
+    for k in range(row.shape[1]):
+        ints[k] = jnp.max(jnp.where(lane == k, row, 0))
 
 
 def fill_weights(along, across, points):
@@ -150,19 +157,21 @@
 
         return carry
 
-    lax.fori_loop(0, entries.shape[0] // 2, pair, 0)
-
-
-def early_kernel(entries, lm, lt, um, ut, vm, vt, g, far, inc_u, inc_v, c, along, across):
+    lax.fori_loop(0, entries.shape[0], pair, 0)
+
+
+def early_kernel(near, far_slots, lm, lt, um, ut, vm, vt, g, far, inc_u, inc_v, c, along, across, near_s, far_s):
+    read_slots(near, near_s)
+    read_slots(far_slots, far_s)
     fill_weights(along, across, c.shape[1])
     inc_u[...] = jnp.zeros_like(inc_u)
     inc_v[...] = jnp.zeros_like(inc_v)
-    add_near(1, entries, (lm, lt), (um, ut), g, inc_u, c, along, across)
-    add_near(2, entries, (lm, lt), (vm, vt), g, inc_v, c, along, across)
-    slots = entries.shape[0] // 2
+    add_near(1, near_s, (lm, lt), (um, ut), g, inc_u, c, along, across)
+    add_near(2, near_s, (lm, lt), (vm, vt), g, inc_v, c, along, across)
+    slots = far.shape[0]
 
     def pair(k, carry):
-        entry = entries[slots + k]
+        entry = far_s[k]
         bins, first, second = decode(entry)
 
         @pl.when(entry > 0)
@@ -174,12 +183,12 @@
     lax.fori_loop(0, slots, pair, 0)
 
 
-def far_kernel(group, entries, far, inc, g, out, total):
-    slots = entries.shape[0] // 2
+def far_kernel(group, far_slots, far, inc, g, out, total, far_s):
+    read_slots(far_slots, far_s)
     total[...] = inc[...]
 
     def pair(k, carry):
-        entry = entries[slots + k]
+        entry = far_s[k]
         _, first, second = decode(entry)
 
         @pl.when(entry > 0)
@@ -191,11 +200,12 @@
 
         return carry
 
-    lax.fori_loop(0, slots, pair, 0)
+    lax.fori_loop(0, far.shape[0], pair, 0)
     out[...] = total[...].astype(BF16)
 
 
-def late_kernel(entries, lm, lt, um, ut, vm, vt, g_l, g_u, g_v, out, c, along, across):
+def late_kernel(near, lm, lt, um, ut, vm, vt, g_l, g_u, g_v, out, c, along, across, near_s):
+    read_slots(near, near_s)
     tiles, members, points = g_l.shape
     fill_weights(along, across, points)
 
@@ -208,7 +218,7 @@
     lax.fori_loop(0, tiles, own, 0)
 
     def pair(k, carry):
-        entry = entries[k]
+        entry = near_s[k]
         bins, first, second = decode(entry)
 
         for group, (right, g) in enumerate((((lm, lt), g_l), ((um, ut), g_u), ((vm, vt), g_v))):
@@ -223,7 +233,7 @@
 
         return carry
 
-    lax.fori_loop(0, entries.shape[0] // 2, pair, 0)
+    lax.fori_loop(0, near.shape[1], pair, 0)
 
 
 def final_kernel(total, from_u, from_v, out, done, sems):
@@ -285,21 +295,23 @@
     g_v = send(forcing, to_v)
     g_u = send(forcing, to_u)
     other_list = jnp.where(place % 4 != 2, slot_codes(a_u, slots), slot_codes(a_v, slots))
-    entries = entries_for(slot_codes(a_l, slots), other_list, place, tiles)
+    near, far_slots = entries_for(slot_codes(a_l, slots), other_list, place, tiles)
     square = vm((points, points), BF16)
     across = vm((points // WIDTH, points), F32)
     weights = [square, vm((NBIN, WIDTH, points), F32), across]
     weights_far = [square, vm((2 * NBIN, WIDTH, points), F32), across]
+    ints = pltpu.SMEM((slots,), jnp.int32)
 
     a_vt = swap(a_v)
     a_ut = swap(a_u)
     far, inc_u, inc_v = call(
         early_kernel,
         (sds((slots, points, points), BF16), sds(anomalies.shape, F32), sds(anomalies.shape, F32)),
-        "svvvvvvv",
-        weights_far,
+        "vvvvvvvvv",
+        [*weights_far, ints, ints],
         4,
-        entries,
+        near,
+        far_slots,
         a_l,
         a_t,
         a_u,
@@ -311,10 +323,10 @@
     finish = lambda group, inc, g: call(
         functools.partial(far_kernel, group),
         sds(anomalies.shape, BF16),
-        "svvv",
-        [vm(anomalies.shape, F32)],
+        "vvvv",
+        [vm(anomalies.shape, F32), ints],
         1,
-        entries,
+        far_slots,
         far,
         inc,
         g,
@@ -324,10 +336,10 @@
     total = call(
         late_kernel,
         sds(anomalies.shape, F32),
-        "svvvvvvvvv",
-        weights,
+        "vvvvvvvvvv",
+        [*weights, ints],
         10,
-        entries,
+        near,
         a_l,
         a_t,
         a_u,

time: 50.9 us -> 50.3 us (0.988); the launches traced: 51 us -> 49.6 us
  Pallas kernels: 16.7 us -> 15.4 us
    pallas_call x7, Pallas kernels: 16.7 us -> 15.4 us  [call(): pl.pallas_call(kernel, out_shape=outs, in_specs=[spec[p] for p in places]...]
  transfers between devices with their start and end apart: 9 -> 9, of which waited for: 6 -> 6; matrix products, arithmetic and copies ran while one was open for 2% -> 1% of each run, Pallas kernels for 29% -> 27%
where the time goes in v5:
time: 50.3 us; the launch traced here: 49.6 us
  waiting for transfers between devices  19.1 us (38%)
  Pallas kernels  15.4 us (31%)
  starting transfers between devices  13.7 us (27%)
  other arithmetic  0.73 us (1%)
  local copies, waits for them, and re-layouts  0.65 us (1%)
    ppermute x6, waiting for transfers between devices, per_device(): send = lambda x, pairs: lax.ppermute(x, 'tile', pairs)  16.1 us
    pallas_call x7, Pallas kernels, call(): pl.pallas_call(kernel, out_shape=outs, in_specs=[spec[p] for p in places]...  15.4 us
    ppermute x6, starting transfers between devices, per_device(): send = lambda x, pairs: lax.ppermute(x, 'tile', pairs)  12.6 us
    ppermute x3, waiting for transfers between devices, per_device(): swap = lambda x: lax.ppermute(x, 'mem', [(0, 1), (1, 0)])  2.94 us
    ppermute x3, starting transfers between devices, per_device(): swap = lambda x: lax.ppermute(x, 'mem', [(0, 1), (1, 0)])  1.08 us
  transfers between devices with their start and end apart: 9, of which 6 were waited for; matrix products, arithmetic and copies ran while one was open for 1% of the time, Pallas kernels for 27%

profile of v5, /device:TPU:0, one launch (start us, length us, event | category | flops | bytes accessed | tf_op | source)
XLA Modules:
  0.0 49.6 jit_solution(1840753218965646311)
XLA Ops:
  0.0 1.1 %shard_map.55.lm = bf16[528,512]{1,0:T(8,128)(2,1)S(1)} custom-call(s32[2,8]{1,0:T(2,128)} %bitcast.40, s32[8]{0:T(128)} %bins.1, bf16[4,128,512]{2,1,0:T(8,128)(2,1)} %anomalies.1), custom_call_target="tpu_custom_call" | custom-call | flops 10000000 | bytes 30000 | tf_op jit(solution)/shard_map/pallas_call | solution.py:251
  1.2 1.3 %collective-permute-start.3 = (bf16[528,512]{1,0:T(8,128)(2,1)S(1)}, bf16[528,512]{1,0:T(8,128)(2,1)S(1)}, u32[]{:S(2)}, u32[]{:S(2)}) collective-permute-start(bf16[528,512]{1,0:T(8,128)(2,1)S(1)} %shard_map.55.lm), channel_id=1, source_target_pairs={{2,0},{5,1},{3,2},{6,4},{9,5},{7,6},{10,8},{13,9},{11,10},{14,12},... | collective-permute-start | bytes 1622024 | tf_op jit(solution)/shard_map/ppermute | solution.py:268
  2.5 1.3 %collective-permute-start.1 = (bf16[528,512]{1,0:T(8,128)(2,1)S(1)}, bf16[528,512]{1,0:T(8,128)(2,1)S(1)}, u32[]{:S(2)}, u32[]{:S(2)}) collective-permute-start(bf16[528,512]{1,0:T(8,128)(2,1)S(1)} %shard_map.55.lm), channel_id=1, source_target_pairs={{1,0},{3,1},{4,2},{5,4},{7,5},{8,6},{9,8},{11,9},{12,10},{13,12},{... | collective-permute-start | bytes 1622024 | tf_op jit(solution)/shard_map/ppermute | solution.py:268
  3.8 0.5 %collective-permute-start = (bf16[528,512]{1,0:T(8,128)(2,1)S(1)}, bf16[528,512]{1,0:T(8,128)(2,1)S(1)}, u32[]{:S(2)}, u32[]{:S(2)}) collective-permute-start(bf16[528,512]{1,0:T(8,128)(2,1)S(1)} %shard_map.55.lm), channel_id=1, source_target_pairs={{0,16},{16,0},{1,17},{17,1},{2,18},{18,2},{3,19},{19,3},{4,20},{20... | collective-permute-start | bytes 1622024 | tf_op jit(solution)/shard_map/ppermute | solution.py:270
  4.3 0.2 shift-right-arithmetic_reduce_fusion.1
  4.5 0.1 compare_reduce_fusion
  4.6 1.2 %collective-permute-done.lt = bf16[528,512]{1,0:T(8,128)(2,1)S(1)} collective-permute-done((bf16[528,512]{1,0:T(8,128)(2,1)S(1)}, bf16[528,512]{1,0:T(8,128)(2,1)S(1)}, u32[]{:S(2)}, u32[]{:S(2)}) %collective-permute-start) | collective-permute-done | bytes 540704 | tf_op jit(solution)/shard_map/ppermute | solution.py:270
  5.8 0.0 copy-start
  5.8 0.7 %copy-done = s32[8]{0:T(128)S(1)} copy-done((s32[8]{0:T(128)S(1)}, s32[8]{0:T(128)}, u32[]{:S(2)}) %copy-start) | copy-done | bytes 56
  6.5 1.6 %shard_map.56.g_l.g = bf16[4,128,512]{2,1,0:T(8,128)(2,1)S(1)} custom-call(s32[8]{0:T(128)S(1)} %copy-done, bf16[8,128,512]{2,1,0:T(8,128)(2,1)} %innov.1), custom_call_target="tpu_custom_call" | custom-call | flops 10000000 | bytes 30000 | tf_op jit(solution)/shard_map/pallas_call | solution.py:251
  8.1 1.3 %collective-permute-start.6 = (bf16[4,128,512]{2,1,0:T(8,128)(2,1)S(1)}, bf16[4,128,512]{2,1,0:T(8,128)(2,1)S(1)}, u32[]{:S(2)}, u32[]{:S(2)}) collective-permute-start(bf16[4,128,512]{2,1,0:T(8,128)(2,1)S(1)} %shard_map.56.g_l.g), channel_id=1, source_target_pairs={{2,0},{5,1},{3,2},{6,4},{9,5},{7,6},{10,8},{13,9},{11,10},{14,12},... | collective-permute-start | bytes 1572872 | tf_op jit(solution)/shard_map/ppermute | solution.py:268
  9.4 1.3 %collective-permute-start.5 = (bf16[4,128,512]{2,1,0:T(8,128)(2,1)S(1)}, bf16[4,128,512]{2,1,0:T(8,128)(2,1)S(1)}, u32[]{:S(2)}, u32[]{:S(2)}) collective-permute-start(bf16[4,128,512]{2,1,0:T(8,128)(2,1)S(1)} %shard_map.56.g_l.g), channel_id=1, source_target_pairs={{1,0},{3,1},{4,2},{5,4},{7,5},{8,6},{9,8},{11,9},{12,10},{13,12},{... | collective-permute-start | bytes 1572872 | tf_op jit(solution)/shard_map/ppermute | solution.py:268
  10.7 9.7 %collective-permute-done.1.um = bf16[528,512]{1,0:T(8,128)(2,1)S(1)} collective-permute-done((bf16[528,512]{1,0:T(8,128)(2,1)S(1)}, bf16[528,512]{1,0:T(8,128)(2,1)S(1)}, u32[]{:S(2)}, u32[]{:S(2)}) %collective-permute-start.1) | collective-permute-done | bytes 540704 | tf_op jit(solution)/shard_map/ppermute | solution.py:268
  20.4 0.0 collective-permute-start.2
  20.4 0.0 collective-permute-done.3.vm
  20.4 0.6 %collective-permute-start.4 = (bf16[528,512]{1,0:T(8,128)(2,1)S(1)}, bf16[528,512]{1,0:T(8,128)(2,1)S(1)}, u32[]{:S(2)}, u32[]{:S(2)}) collective-permute-start(bf16[528,512]{1,0:T(8,128)(2,1)S(1)} %collective-permute-done.3.vm), channel_id=1, source_target_pairs={{0,16},{16,0},{1,17},{17,1},{2,18},{18,2},{3,19},{19,3},{4,20},{20... | collective-permute-start | bytes 1622024 | tf_op jit(solution)/shard_map/ppermute | solution.py:270
  21.0 0.2 shift-right-arithmetic_reduce_fusion
  21.2 0.1 and_reduce_fusion.2
  21.3 1.0 %collective-permute-done.2.ut = bf16[528,512]{1,0:T(8,128)(2,1)S(1)} collective-permute-done((bf16[528,512]{1,0:T(8,128)(2,1)S(1)}, bf16[528,512]{1,0:T(8,128)(2,1)S(1)}, u32[]{:S(2)}, u32[]{:S(2)}) %collective-permute-start.2) | collective-permute-done | bytes 540704 | tf_op jit(solution)/shard_map/ppermute | solution.py:270
  22.3 0.8 %collective-permute-done.4.vt = bf16[528,512]{1,0:T(8,128)(2,1)S(1)} collective-permute-done((bf16[528,512]{1,0:T(8,128)(2,1)S(1)}, bf16[528,512]{1,0:T(8,128)(2,1)S(1)}, u32[]{:S(2)}, u32[]{:S(2)}) %collective-permute-start.4) | collective-permute-done | bytes 540704 | tf_op jit(solution)/shard_map/ppermute | solution.py:270
  23.1 2.9 %shard_map.58 = (bf16[8,512,512]{2,1,0:T(8,128)(2,1)S(1)}, f32[4,128,512]{2,1,0:T(8,128)S(1)}, f32[4,128,512]{2,1,0:T(8,128)S(1)}) custom-call(s32[1,8]{1,0:T(1,128)S(1)} %fusion.1.near, s32[1,8]{1,0:T(1,128)S(1)} %fusion.far_slots, bf16[528,512]{1,0:T(8,128)(2,1)S(1)} %shard_map.55.lm, bf16[528,512]{1,0:T(8,128)(2,1)S(1)} %collective-permute-done.lt, ...), custom_call_target="tpu_custom_call" | custom-call | flops 40000000 | bytes 120000 | tf_op jit(solution)/shard_map/pallas_call | solution.py:251
  26.0 3.5 %collective-permute-done.6.g_v.g = bf16[4,128,512]{2,1,0:T(8,128)(2,1)S(1)} collective-permute-done((bf16[4,128,512]{2,1,0:T(8,128)(2,1)S(1)}, bf16[4,128,512]{2,1,0:T(8,128)(2,1)S(1)}, u32[]{:S(2)}, u32[]{:S(2)}) %collective-permute-start.6) | collective-permute-done | bytes 524320 | tf_op jit(solution)/shard_map/ppermute | solution.py:268
  29.5 1.0 %shard_map.60 = bf16[4,128,512]{2,1,0:T(8,128)(2,1)S(1)} custom-call(s32[1,8]{1,0:T(1,128)S(1)} %fusion.far_slots, bf16[8,512,512]{2,1,0:T(8,128)(2,1)S(1)} %get-tuple-element.12.far, f32[4,128,512]{2,1,0:T(8,128)S(1)} %get-tuple-element.14.inc, bf16[4,128,512]{2,1,0:T(8,128)(2,1)S(1)} %collective-permute-done.6.g_v.g), custom_call_target="tpu_custom_call" | custom-call | flops 10000000 | bytes 30000 | tf_op jit(solution)/shard_map/pallas_call | solution.py:251
  30.5 3.6 %collective-permute-start.8 = (bf16[4,128,512]{2,1,0:T(8,128)(2,1)S(1)}, bf16[4,128,512]{2,1,0:T(8,128)(2,1)S(1)}, u32[]{:S(2)}, u32[]{:S(2)}) collective-permute-start(bf16[4,128,512]{2,1,0:T(8,128)(2,1)S(1)} %shard_map.60), channel_id=1, source_target_pairs={{0,1},{1,3},{2,4},{4,5},{5,7},{6,8},{8,9},{9,11},{10,12},{12,13},{... | collective-permute-start | bytes 1572872 | tf_op jit(solution)/shard_map/ppermute | solution.py:268
  34.2 0.0 collective-permute-done.5.g_u.g
  34.2 0.8 %shard_map.59 = bf16[4,128,512]{2,1,0:T(8,128)(2,1)S(1)} custom-call(s32[1,8]{1,0:T(1,128)S(1)} %fusion.far_slots, bf16[8,512,512]{2,1,0:T(8,128)(2,1)S(1)} %get-tuple-element.12.far, f32[4,128,512]{2,1,0:T(8,128)S(1)} %get-tuple-element.13.inc, bf16[4,128,512]{2,1,0:T(8,128)(2,1)S(1)} %collective-permute-done.5.g_u.g), custom_call_target="tpu_custom_call" | custom-call | flops 10000000 | bytes 30000 | tf_op jit(solution)/shard_map/pallas_call | solution.py:251
  35.0 3.8 %collective-permute-start.7 = (bf16[4,128,512]{2,1,0:T(8,128)(2,1)S(1)}, bf16[4,128,512]{2,1,0:T(8,128)(2,1)S(1)}, u32[]{:S(2)}, u32[]{:S(2)}) collective-permute-start(bf16[4,128,512]{2,1,0:T(8,128)(2,1)S(1)} %shard_map.59), channel_id=1, source_target_pairs={{0,2},{1,5},{2,3},{4,6},{5,9},{6,7},{8,10},{9,13},{10,11},{12,14},... | collective-permute-start | bytes 1572872 | tf_op jit(solution)/shard_map/ppermute | solution.py:268
  38.8 7.1 %shard_map.57.total = f32[4,128,512]{2,1,0:T(8,128)S(1)} custom-call(s32[1,8]{1,0:T(1,128)S(1)} %fusion.1.near, bf16[528,512]{1,0:T(8,128)(2,1)S(1)} %shard_map.55.lm, bf16[528,512]{1,0:T(8,128)(2,1)S(1)} %collective-permute-done.lt, bf16[528,512]{1,0:T(8,128)(2,1)S(1)} %collective-permute-done.1.um, bf16[528,512]{1,0:T(8,128)(2,1)S(1)} %collective-permute-done.2.ut, ...), custom_call_target="tpu_custom_call" | custom-call | flops 100000000 | bytes 300000 | tf_op jit(solution)/shard_map/pallas_call | solution.py:251
  45.9 0.0 collective-permute-done.8.from_v
  45.9 2.9 %collective-permute-done.7.from_u = bf16[4,128,512]{2,1,0:T(8,128)(2,1)S(1)} collective-permute-done((bf16[4,128,512]{2,1,0:T(8,128)(2,1)S(1)}, bf16[4,128,512]{2,1,0:T(8,128)(2,1)S(1)}, u32[]{:S(2)}, u32[]{:S(2)}) %collective-permute-start.7) | collective-permute-done | bytes 524320 | tf_op jit(solution)/shard_map/ppermute | solution.py:268
  48.8 0.9 %shard_map.61 = bf16[4,128,512]{2,1,0:T(8,128)(2,1)} custom-call(f32[4,128,512]{2,1,0:T(8,128)S(1)} %shard_map.57.total, bf16[4,128,512]{2,1,0:T(8,128)(2,1)S(1)} %collective-permute-done.7.from_u, bf16[4,128,512]{2,1,0:T(8,128)(2,1)S(1)} %collective-permute-done.8.from_v), custom_call_target="tpu_custom_call" | custom-call | flops 10000000 | bytes 30000 | tf_op jit(solution)/shard_map/pallas_call | solution.py:251
  (5 shorter events, 0.1 us)
Async XLA Ops:
  1.2 19.3 %collective-permute-start.3 = (bf16[528,512]{1,0:T(8,128)(2,1)S(1)}, bf16[528,512]{1,0:T(8,128)(2,1)S(1)}, u32[]{:S(2)}, u32[]{:S(2)}) collective-permute-start(bf16[528,512]{1,0:T(8,128)(2,1)S(1)} %shard_map.55.lm), channel_id=1, source_target_pairs={{2,0},{5,1},{3,2},{6,4},{9,5},{7,6},{10,8},{13,9},{11,10},{14,12},... | collective-permute-start | bytes 1622024 | tf_op jit(solution)/shard_map/ppermute | solution.py:268
  2.5 17.9 %collective-permute-start.1 = (bf16[528,512]{1,0:T(8,128)(2,1)S(1)}, bf16[528,512]{1,0:T(8,128)(2,1)S(1)}, u32[]{:S(2)}, u32[]{:S(2)}) collective-permute-start(bf16[528,512]{1,0:T(8,128)(2,1)S(1)} %shard_map.55.lm), channel_id=1, source_target_pairs={{1,0},{3,1},{4,2},{5,4},{7,5},{8,6},{9,8},{11,9},{12,10},{13,12},{... | collective-permute-start | bytes 1622024 | tf_op jit(solution)/shard_map/ppermute | solution.py:268
  3.8 2.1 %collective-permute-start = (bf16[528,512]{1,0:T(8,128)(2,1)S(1)}, bf16[528,512]{1,0:T(8,128)(2,1)S(1)}, u32[]{:S(2)}, u32[]{:S(2)}) collective-permute-start(bf16[528,512]{1,0:T(8,128)(2,1)S(1)} %shard_map.55.lm), channel_id=1, source_target_pairs={{0,16},{16,0},{1,17},{17,1},{2,18},{18,2},{3,19},{19,3},{4,20},{20... | collective-permute-start | bytes 1622024 | tf_op jit(solution)/shard_map/ppermute | solution.py:270
  5.8 0.7 %copy-start = (s32[8]{0:T(128)S(1)}, s32[8]{0:T(128)}, u32[]{:S(2)}) copy-start(s32[8]{0:T(128)} %obs) | copy-start | bytes 100
  8.1 21.5 %collective-permute-start.6 = (bf16[4,128,512]{2,1,0:T(8,128)(2,1)S(1)}, bf16[4,128,512]{2,1,0:T(8,128)(2,1)S(1)}, u32[]{:S(2)}, u32[]{:S(2)}) collective-permute-start(bf16[4,128,512]{2,1,0:T(8,128)(2,1)S(1)} %shard_map.56.g_l.g), channel_id=1, source_target_pairs={{2,0},{5,1},{3,2},{6,4},{9,5},{7,6},{10,8},{13,9},{11,10},{14,12},... | collective-permute-start | bytes 1572872 | tf_op jit(solution)/shard_map/ppermute | solution.py:268
  9.4 24.8 %collective-permute-start.5 = (bf16[4,128,512]{2,1,0:T(8,128)(2,1)S(1)}, bf16[4,128,512]{2,1,0:T(8,128)(2,1)S(1)}, u32[]{:S(2)}, u32[]{:S(2)}) collective-permute-start(bf16[4,128,512]{2,1,0:T(8,128)(2,1)S(1)} %shard_map.56.g_l.g), channel_id=1, source_target_pairs={{1,0},{3,1},{4,2},{5,4},{7,5},{8,6},{9,8},{11,9},{12,10},{13,12},{... | collective-permute-start | bytes 1572872 | tf_op jit(solution)/shard_map/ppermute | solution.py:268
  20.4 1.9 %collective-permute-start.2 = (bf16[528,512]{1,0:T(8,128)(2,1)S(1)}, bf16[528,512]{1,0:T(8,128)(2,1)S(1)}, u32[]{:S(2)}, u32[]{:S(2)}) collective-permute-start(bf16[528,512]{1,0:T(8,128)(2,1)S(1)} %collective-permute-done.1.um), channel_id=1, source_target_pairs={{0,16},{16,0},{1,17},{17,1},{2,18},{18,2},{3,19},{19,3},{4,20},{20... | collective-permute-start | bytes 1622024 | tf_op jit(solution)/shard_map/ppermute | solution.py:270
  20.4 2.7 %collective-permute-start.4 = (bf16[528,512]{1,0:T(8,128)(2,1)S(1)}, bf16[528,512]{1,0:T(8,128)(2,1)S(1)}, u32[]{:S(2)}, u32[]{:S(2)}) collective-permute-start(bf16[528,512]{1,0:T(8,128)(2,1)S(1)} %collective-permute-done.3.vm), channel_id=1, source_target_pairs={{0,16},{16,0},{1,17},{17,1},{2,18},{18,2},{3,19},{19,3},{4,20},{20... | collective-permute-start | bytes 1622024 | tf_op jit(solution)/shard_map/ppermute | solution.py:270
  30.5 15.4 %collective-permute-start.8 = (bf16[4,128,512]{2,1,0:T(8,128)(2,1)S(1)}, bf16[4,128,512]{2,1,0:T(8,128)(2,1)S(1)}, u32[]{:S(2)}, u32[]{:S(2)}) collective-permute-start(bf16[4,128,512]{2,1,0:T(8,128)(2,1)S(1)} %shard_map.60), channel_id=1, source_target_pairs={{0,1},{1,3},{2,4},{4,5},{5,7},{6,8},{8,9},{9,11},{10,12},{12,13},{... | collective-permute-start | bytes 1572872 | tf_op jit(solution)/shard_map/ppermute | solution.py:268
  35.0 13.8 %collective-permute-start.7 = (bf16[4,128,512]{2,1,0:T(8,128)(2,1)S(1)}, bf16[4,128,512]{2,1,0:T(8,128)(2,1)S(1)}, u32[]{:S(2)}, u32[]{:S(2)}) collective-permute-start(bf16[4,128,512]{2,1,0:T(8,128)(2,1)S(1)} %shard_map.59), channel_id=1, source_target_pairs={{0,2},{1,5},{2,3},{4,6},{5,9},{6,7},{8,10},{9,13},{10,11},{12,14},... | collective-permute-start | bytes 1572872 | tf_op jit(solution)/shard_map/ppermute | solution.py:268

commit v6 on v5

--- a/solution.py
+++ b/solution.py
@@ -142,65 +142,79 @@
     out[...] = total[...].astype(BF16)
 
 
-def add_near(group, entries, left, right, g, inc, c, along, across):
+def compact(ints, wanted, kept):
+    count = jnp.int32(0)
+    for k in range(ints.shape[0]):
+        kept[count] = ints[k]
+        count = count + wanted(ints[k]).astype(jnp.int32)
+    return count
+
+
+def in_twos(count, step):
+    def two(k, carry):
+        step([2 * k, 2 * k + 1])
+        return carry
+
+    lax.fori_loop(0, lax.div(count, 2), two, 0)
+
+    @pl.when(lax.rem(count, 2) == 1)
+    def _():
+        step([count - 1])
+
+
+def add_near(group, ints, kept, left, right, g, inc, c, along, across):
     tiles = g.shape[0]
 
-    def pair(k, carry):
-        entry = entries[k]
-        bins, first, second = decode(entry)
-        here = second - group * tiles
-
-        @pl.when((entry > 0) & (here >= 0) & (here < tiles))
-        def _():
-            covariance(left, right, first, here, along[bins], across, c)
-            inc[here] = inc[here] + to_second(g[first], c[...])
-
-        return carry
-
-    lax.fori_loop(0, entries.shape[0], pair, 0)
-
-
-def early_kernel(near, far_slots, lm, lt, um, ut, vm, vt, g, far, inc_u, inc_v, c, along, across, near_s, far_s):
-    read_slots(near, near_s)
-    read_slots(far_slots, far_s)
-    fill_weights(along, across, c.shape[1])
+    def wanted(entry):
+        _, _, second = decode(entry)
+        return (entry > 0) & (second >= group * tiles) & (second < (group + 1) * tiles)
+
+    def step(indices):
+        pairs = [decode(kept[k]) for k in indices]
+        for q, (bins, first, second) in enumerate(pairs):
+            covariance(left, right, first, second - group * tiles, along[bins], across, c.at[q])
+        parts = [to_second(g[first], c[q]) for q, (_, first, _) in enumerate(pairs)]
+        for part, (_, _, second) in zip(parts, pairs):
+            here = second - group * tiles
+            inc[here] = inc[here] + part
+
+    in_twos(compact(ints, wanted, kept), step)
+
+
+def early_kernel(near, far_slots, lm, lt, um, ut, vm, vt, g, far, inc_u, inc_v, c, along, across, ints, kept):
+    points = c.shape[1]
+    read_slots(near, ints)
+    fill_weights(along, across, points)
     inc_u[...] = jnp.zeros_like(inc_u)
     inc_v[...] = jnp.zeros_like(inc_v)
-    add_near(1, near_s, (lm, lt), (um, ut), g, inc_u, c, along, across)
-    add_near(2, near_s, (lm, lt), (vm, vt), g, inc_v, c, along, across)
-    slots = far.shape[0]
-
-    def pair(k, carry):
-        entry = far_s[k]
-        bins, first, second = decode(entry)
-
-        @pl.when(entry > 0)
-        def _():
+    add_near(1, ints, kept, (lm, lt), (um, ut), g, inc_u, c, along, across)
+    add_near(2, ints, kept, (lm, lt), (vm, vt), g, inc_v, c, along, across)
+    read_slots(far_slots, ints)
+
+    def step(indices):
+        for k in indices:
+            bins, first, second = decode(kept[k])
             covariance((um, ut), (vm, vt), first, second, along[bins], across, far.at[k])
 
-        return carry
-
-    lax.fori_loop(0, slots, pair, 0)
-
-
-def far_kernel(group, far_slots, far, inc, g, out, total, far_s):
-    read_slots(far_slots, far_s)
+    in_twos(compact(ints, lambda entry: entry > 0, kept), step)
+
+
+def far_kernel(group, far_slots, far, inc, g, out, total, ints, kept):
+    read_slots(far_slots, ints)
     total[...] = inc[...]
 
-    def pair(k, carry):
-        entry = far_s[k]
-        _, first, second = decode(entry)
-
-        @pl.when(entry > 0)
-        def _():
-            if group == 1:
-                total[first] = total[first] + to_first(g[second], far[k])
-            else:
-                total[second] = total[second] + to_second(g[first], far[k])
-
-        return carry
-
-    lax.fori_loop(0, far.shape[0], pair, 0)
+    def step(indices):
+        pairs = [decode(kept[k])[1:] for k in indices]
+        if group == 1:
+            parts = [to_first(g[second], far[k]) for k, (_, second) in zip(indices, pairs)]
+            places = [first for first, _ in pairs]
+        else:
+            parts = [to_second(g[first], far[k]) for k, (first, _) in zip(indices, pairs)]
+            places = [second for _, second in pairs]
+        for part, here in zip(parts, places):
+            total[here] = total[here] + part
+
+    in_twos(compact(ints, lambda entry: entry > 0, kept), step)
     out[...] = total[...].astype(BF16)
 
 
@@ -299,7 +313,7 @@
     square = vm((points, points), BF16)
     across = vm((points // WIDTH, points), F32)
     weights = [square, vm((NBIN, WIDTH, points), F32), across]
-    weights_far = [square, vm((2 * NBIN, WIDTH, points), F32), across]
+    weights_far = [vm((2, points, points), BF16), vm((2 * NBIN, WIDTH, points), F32), across]
     ints = pltpu.SMEM((slots,), jnp.int32)
 
     a_vt = swap(a_v)
@@ -324,7 +338,7 @@
         functools.partial(far_kernel, group),
         sds(anomalies.shape, BF16),
         "vvvv",
-        [vm(anomalies.shape, F32), ints],
+        [vm(anomalies.shape, F32), ints, ints],
         1,
         far_slots,
         far,

time: 50.3 us -> 49.3 us (0.980)
  Pallas kernels: 15.4 us -> 13.7 us
  waiting for transfers between devices: 19.1 us -> 20 us
    pallas_call x7, Pallas kernels: 15.4 us -> 13.7 us  [call(): pl.pallas_call(kernel, out_shape=outs, in_specs=[spec[p] for p in places]...]
    ppermute x6, waiting for transfers between devices: 16.1 us -> 17.1 us  [per_device(): send = lambda x, pairs: lax.ppermute(x, 'tile', pairs)]
  transfers between devices with their start and end apart: 9 -> 9, of which waited for: 6 -> 6; matrix products, arithmetic and copies ran while one was open for 1% -> 1% of each run, Pallas kernels for 27% -> 24%
where the time goes in v6:
time: 49.3 us; the launch traced here: 49.1 us
  waiting for transfers between devices  20 us (41%)
  starting transfers between devices  13.9 us (28%)
  Pallas kernels  13.7 us (28%)
  other arithmetic  0.73 us (1%)
  local copies, waits for them, and re-layouts  0.65 us (1%)
    ppermute x6, waiting for transfers between devices, per_device(): send = lambda x, pairs: lax.ppermute(x, 'tile', pairs)  17.1 us
    pallas_call x7, Pallas kernels, call(): pl.pallas_call(kernel, out_shape=outs, in_specs=[spec[p] for p in places]...  13.7 us
    ppermute x6, starting transfers between devices, per_device(): send = lambda x, pairs: lax.ppermute(x, 'tile', pairs)  12.8 us
    ppermute x3, waiting for transfers between devices, per_device(): swap = lambda x: lax.ppermute(x, 'mem', [(0, 1), (1, 0)])  2.94 us
    ppermute x3, starting transfers between devices, per_device(): swap = lambda x: lax.ppermute(x, 'mem', [(0, 1), (1, 0)])  1.08 us
  transfers between devices with their start and end apart: 9, of which 6 were waited for; matrix products, arithmetic and copies ran while one was open for 1% of the time, Pallas kernels for 24%

profile of v6, /device:TPU:0, one launch (start us, length us, event | category | flops | bytes accessed | tf_op | source)
XLA Modules:
  0.0 49.1 jit_solution(3361645881641511261)
XLA Ops:
  0.0 1.1 %shard_map.55.lm = bf16[528,512]{1,0:T(8,128)(2,1)S(1)} custom-call(s32[2,8]{1,0:T(2,128)} %bitcast.40, s32[8]{0:T(128)} %bins.1, bf16[4,128,512]{2,1,0:T(8,128)(2,1)} %anomalies.1), custom_call_target="tpu_custom_call" | custom-call | flops 10000000 | bytes 30000 | tf_op jit(solution)/shard_map/pallas_call | solution.py:265
  1.2 1.3 %collective-permute-start.3 = (bf16[528,512]{1,0:T(8,128)(2,1)S(1)}, bf16[528,512]{1,0:T(8,128)(2,1)S(1)}, u32[]{:S(2)}, u32[]{:S(2)}) collective-permute-start(bf16[528,512]{1,0:T(8,128)(2,1)S(1)} %shard_map.55.lm), channel_id=1, source_target_pairs={{2,0},{5,1},{3,2},{6,4},{9,5},{7,6},{10,8},{13,9},{11,10},{14,12},... | collective-permute-start | bytes 1622024 | tf_op jit(solution)/shard_map/ppermute | solution.py:282
  2.5 1.3 %collective-permute-start.1 = (bf16[528,512]{1,0:T(8,128)(2,1)S(1)}, bf16[528,512]{1,0:T(8,128)(2,1)S(1)}, u32[]{:S(2)}, u32[]{:S(2)}) collective-permute-start(bf16[528,512]{1,0:T(8,128)(2,1)S(1)} %shard_map.55.lm), channel_id=1, source_target_pairs={{1,0},{3,1},{4,2},{5,4},{7,5},{8,6},{9,8},{11,9},{12,10},{13,12},{... | collective-permute-start | bytes 1622024 | tf_op jit(solution)/shard_map/ppermute | solution.py:282
  3.8 0.5 %collective-permute-start = (bf16[528,512]{1,0:T(8,128)(2,1)S(1)}, bf16[528,512]{1,0:T(8,128)(2,1)S(1)}, u32[]{:S(2)}, u32[]{:S(2)}) collective-permute-start(bf16[528,512]{1,0:T(8,128)(2,1)S(1)} %shard_map.55.lm), channel_id=1, source_target_pairs={{0,16},{16,0},{1,17},{17,1},{2,18},{18,2},{3,19},{19,3},{4,20},{20... | collective-permute-start | bytes 1622024 | tf_op jit(solution)/shard_map/ppermute | solution.py:284
  4.3 0.2 shift-right-arithmetic_reduce_fusion.1
  4.5 0.1 compare_reduce_fusion
  4.6 1.2 %collective-permute-done.lt = bf16[528,512]{1,0:T(8,128)(2,1)S(1)} collective-permute-done((bf16[528,512]{1,0:T(8,128)(2,1)S(1)}, bf16[528,512]{1,0:T(8,128)(2,1)S(1)}, u32[]{:S(2)}, u32[]{:S(2)}) %collective-permute-start) | collective-permute-done | bytes 540704 | tf_op jit(solution)/shard_map/ppermute | solution.py:284
  5.8 0.0 copy-start
  5.8 0.7 %copy-done = s32[8]{0:T(128)S(1)} copy-done((s32[8]{0:T(128)S(1)}, s32[8]{0:T(128)}, u32[]{:S(2)}) %copy-start) | copy-done | bytes 56
  6.5 1.6 %shard_map.56.g_l.g = bf16[4,128,512]{2,1,0:T(8,128)(2,1)S(1)} custom-call(s32[8]{0:T(128)S(1)} %copy-done, bf16[8,128,512]{2,1,0:T(8,128)(2,1)} %innov.1), custom_call_target="tpu_custom_call" | custom-call | flops 10000000 | bytes 30000 | tf_op jit(solution)/shard_map/pallas_call | solution.py:265
  8.1 1.3 %collective-permute-start.6 = (bf16[4,128,512]{2,1,0:T(8,128)(2,1)S(1)}, bf16[4,128,512]{2,1,0:T(8,128)(2,1)S(1)}, u32[]{:S(2)}, u32[]{:S(2)}) collective-permute-start(bf16[4,128,512]{2,1,0:T(8,128)(2,1)S(1)} %shard_map.56.g_l.g), channel_id=1, source_target_pairs={{2,0},{5,1},{3,2},{6,4},{9,5},{7,6},{10,8},{13,9},{11,10},{14,12},... | collective-permute-start | bytes 1572872 | tf_op jit(solution)/shard_map/ppermute | solution.py:282
  9.4 1.3 %collective-permute-start.5 = (bf16[4,128,512]{2,1,0:T(8,128)(2,1)S(1)}, bf16[4,128,512]{2,1,0:T(8,128)(2,1)S(1)}, u32[]{:S(2)}, u32[]{:S(2)}) collective-permute-start(bf16[4,128,512]{2,1,0:T(8,128)(2,1)S(1)} %shard_map.56.g_l.g), channel_id=1, source_target_pairs={{1,0},{3,1},{4,2},{5,4},{7,5},{8,6},{9,8},{11,9},{12,10},{13,12},{... | collective-permute-start | bytes 1572872 | tf_op jit(solution)/shard_map/ppermute | solution.py:282
  10.7 9.7 %collective-permute-done.1.um = bf16[528,512]{1,0:T(8,128)(2,1)S(1)} collective-permute-done((bf16[528,512]{1,0:T(8,128)(2,1)S(1)}, bf16[528,512]{1,0:T(8,128)(2,1)S(1)}, u32[]{:S(2)}, u32[]{:S(2)}) %collective-permute-start.1) | collective-permute-done | bytes 540704 | tf_op jit(solution)/shard_map/ppermute | solution.py:282
  20.4 0.0 collective-permute-start.2
  20.4 0.0 collective-permute-done.3.vm
  20.4 0.6 %collective-permute-start.4 = (bf16[528,512]{1,0:T(8,128)(2,1)S(1)}, bf16[528,512]{1,0:T(8,128)(2,1)S(1)}, u32[]{:S(2)}, u32[]{:S(2)}) collective-permute-start(bf16[528,512]{1,0:T(8,128)(2,1)S(1)} %collective-permute-done.3.vm), channel_id=1, source_target_pairs={{0,16},{16,0},{1,17},{17,1},{2,18},{18,2},{3,19},{19,3},{4,20},{20... | collective-permute-start | bytes 1622024 | tf_op jit(solution)/shard_map/ppermute | solution.py:284
  21.0 0.2 shift-right-arithmetic_reduce_fusion
  21.2 0.1 and_reduce_fusion.2
  21.3 1.0 %collective-permute-done.2.ut = bf16[528,512]{1,0:T(8,128)(2,1)S(1)} collective-permute-done((bf16[528,512]{1,0:T(8,128)(2,1)S(1)}, bf16[528,512]{1,0:T(8,128)(2,1)S(1)}, u32[]{:S(2)}, u32[]{:S(2)}) %collective-permute-start.2) | collective-permute-done | bytes 540704 | tf_op jit(solution)/shard_map/ppermute | solution.py:284
  22.3 0.8 %collective-permute-done.4.vt = bf16[528,512]{1,0:T(8,128)(2,1)S(1)} collective-permute-done((bf16[528,512]{1,0:T(8,128)(2,1)S(1)}, bf16[528,512]{1,0:T(8,128)(2,1)S(1)}, u32[]{:S(2)}, u32[]{:S(2)}) %collective-permute-start.4) | collective-permute-done | bytes 540704 | tf_op jit(solution)/shard_map/ppermute | solution.py:284
  23.1 2.8 %shard_map.58 = (bf16[8,512,512]{2,1,0:T(8,128)(2,1)S(1)}, f32[4,128,512]{2,1,0:T(8,128)S(1)}, f32[4,128,512]{2,1,0:T(8,128)S(1)}) custom-call(s32[1,8]{1,0:T(1,128)S(1)} %fusion.1.near, s32[1,8]{1,0:T(1,128)S(1)} %fusion.far_slots, bf16[528,512]{1,0:T(8,128)(2,1)S(1)} %shard_map.55.lm, bf16[528,512]{1,0:T(8,128)(2,1)S(1)} %collective-permute-done.lt, ...), custom_call_target="tpu_custom_call" | custom-call | flops 40000000 | bytes 120000 | tf_op jit(solution)/shard_map/pallas_call | solution.py:265
  25.9 3.7 %collective-permute-done.6.g_v.g = bf16[4,128,512]{2,1,0:T(8,128)(2,1)S(1)} collective-permute-done((bf16[4,128,512]{2,1,0:T(8,128)(2,1)S(1)}, bf16[4,128,512]{2,1,0:T(8,128)(2,1)S(1)}, u32[]{:S(2)}, u32[]{:S(2)}) %collective-permute-start.6) | collective-permute-done | bytes 524320 | tf_op jit(solution)/shard_map/ppermute | solution.py:282
  29.5 0.6 %shard_map.60 = bf16[4,128,512]{2,1,0:T(8,128)(2,1)S(1)} custom-call(s32[1,8]{1,0:T(1,128)S(1)} %fusion.far_slots, bf16[8,512,512]{2,1,0:T(8,128)(2,1)S(1)} %get-tuple-element.12.far, f32[4,128,512]{2,1,0:T(8,128)S(1)} %get-tuple-element.14.inc, bf16[4,128,512]{2,1,0:T(8,128)(2,1)S(1)} %collective-permute-done.6.g_v.g), custom_call_target="tpu_custom_call" | custom-call | flops 10000000 | bytes 30000 | tf_op jit(solution)/shard_map/pallas_call | solution.py:265
  30.1 3.6 %collective-permute-start.8 = (bf16[4,128,512]{2,1,0:T(8,128)(2,1)S(1)}, bf16[4,128,512]{2,1,0:T(8,128)(2,1)S(1)}, u32[]{:S(2)}, u32[]{:S(2)}) collective-permute-start(bf16[4,128,512]{2,1,0:T(8,128)(2,1)S(1)} %shard_map.60), channel_id=1, source_target_pairs={{0,1},{1,3},{2,4},{4,5},{5,7},{6,8},{8,9},{9,11},{10,12},{12,13},{... | collective-permute-start | bytes 1572872 | tf_op jit(solution)/shard_map/ppermute | solution.py:282
  33.8 0.0 collective-permute-done.5.g_u.g
  33.8 0.5 %shard_map.59 = bf16[4,128,512]{2,1,0:T(8,128)(2,1)S(1)} custom-call(s32[1,8]{1,0:T(1,128)S(1)} %fusion.far_slots, bf16[8,512,512]{2,1,0:T(8,128)(2,1)S(1)} %get-tuple-element.12.far, f32[4,128,512]{2,1,0:T(8,128)S(1)} %get-tuple-element.13.inc, bf16[4,128,512]{2,1,0:T(8,128)(2,1)S(1)} %collective-permute-done.5.g_u.g), custom_call_target="tpu_custom_call" | custom-call | flops 10000000 | bytes 30000 | tf_op jit(solution)/shard_map/pallas_call | solution.py:265
  34.3 4.0 %collective-permute-start.7 = (bf16[4,128,512]{2,1,0:T(8,128)(2,1)S(1)}, bf16[4,128,512]{2,1,0:T(8,128)(2,1)S(1)}, u32[]{:S(2)}, u32[]{:S(2)}) collective-permute-start(bf16[4,128,512]{2,1,0:T(8,128)(2,1)S(1)} %shard_map.59), channel_id=1, source_target_pairs={{0,2},{1,5},{2,3},{4,6},{5,9},{6,7},{8,10},{9,13},{10,11},{12,14},... | collective-permute-start | bytes 1572872 | tf_op jit(solution)/shard_map/ppermute | solution.py:282
  38.3 6.3 %shard_map.57.total = f32[4,128,512]{2,1,0:T(8,128)S(1)} custom-call(s32[1,8]{1,0:T(1,128)S(1)} %fusion.1.near, bf16[528,512]{1,0:T(8,128)(2,1)S(1)} %shard_map.55.lm, bf16[528,512]{1,0:T(8,128)(2,1)S(1)} %collective-permute-done.lt, bf16[528,512]{1,0:T(8,128)(2,1)S(1)} %collective-permute-done.1.um, bf16[528,512]{1,0:T(8,128)(2,1)S(1)} %collective-permute-done.2.ut, ...), custom_call_target="tpu_custom_call" | custom-call | flops 100000000 | bytes 300000 | tf_op jit(solution)/shard_map/pallas_call | solution.py:265
  44.6 0.0 collective-permute-done.8.from_v
  44.6 3.7 %collective-permute-done.7.from_u = bf16[4,128,512]{2,1,0:T(8,128)(2,1)S(1)} collective-permute-done((bf16[4,128,512]{2,1,0:T(8,128)(2,1)S(1)}, bf16[4,128,512]{2,1,0:T(8,128)(2,1)S(1)}, u32[]{:S(2)}, u32[]{:S(2)}) %collective-permute-start.7) | collective-permute-done | bytes 524320 | tf_op jit(solution)/shard_map/ppermute | solution.py:282
  48.2 0.9 %shard_map.61 = bf16[4,128,512]{2,1,0:T(8,128)(2,1)} custom-call(f32[4,128,512]{2,1,0:T(8,128)S(1)} %shard_map.57.total, bf16[4,128,512]{2,1,0:T(8,128)(2,1)S(1)} %collective-permute-done.7.from_u, bf16[4,128,512]{2,1,0:T(8,128)(2,1)S(1)} %collective-permute-done.8.from_v), custom_call_target="tpu_custom_call" | custom-call | flops 10000000 | bytes 30000 | tf_op jit(solution)/shard_map/pallas_call | solution.py:265
  (5 shorter events, 0.1 us)
Async XLA Ops:
  1.2 19.3 %collective-permute-start.3 = (bf16[528,512]{1,0:T(8,128)(2,1)S(1)}, bf16[528,512]{1,0:T(8,128)(2,1)S(1)}, u32[]{:S(2)}, u32[]{:S(2)}) collective-permute-start(bf16[528,512]{1,0:T(8,128)(2,1)S(1)} %shard_map.55.lm), channel_id=1, source_target_pairs={{2,0},{5,1},{3,2},{6,4},{9,5},{7,6},{10,8},{13,9},{11,10},{14,12},... | collective-permute-start | bytes 1622024 | tf_op jit(solution)/shard_map/ppermute | solution.py:282
  2.5 17.9 %collective-permute-start.1 = (bf16[528,512]{1,0:T(8,128)(2,1)S(1)}, bf16[528,512]{1,0:T(8,128)(2,1)S(1)}, u32[]{:S(2)}, u32[]{:S(2)}) collective-permute-start(bf16[528,512]{1,0:T(8,128)(2,1)S(1)} %shard_map.55.lm), channel_id=1, source_target_pairs={{1,0},{3,1},{4,2},{5,4},{7,5},{8,6},{9,8},{11,9},{12,10},{13,12},{... | collective-permute-start | bytes 1622024 | tf_op jit(solution)/shard_map/ppermute | solution.py:282
  3.8 2.1 %collective-permute-start = (bf16[528,512]{1,0:T(8,128)(2,1)S(1)}, bf16[528,512]{1,0:T(8,128)(2,1)S(1)}, u32[]{:S(2)}, u32[]{:S(2)}) collective-permute-start(bf16[528,512]{1,0:T(8,128)(2,1)S(1)} %shard_map.55.lm), channel_id=1, source_target_pairs={{0,16},{16,0},{1,17},{17,1},{2,18},{18,2},{3,19},{19,3},{4,20},{20... | collective-permute-start | bytes 1622024 | tf_op jit(solution)/shard_map/ppermute | solution.py:284
  5.8 0.7 %copy-start = (s32[8]{0:T(128)S(1)}, s32[8]{0:T(128)}, u32[]{:S(2)}) copy-start(s32[8]{0:T(128)} %obs) | copy-start | bytes 100
  8.1 21.5 %collective-permute-start.6 = (bf16[4,128,512]{2,1,0:T(8,128)(2,1)S(1)}, bf16[4,128,512]{2,1,0:T(8,128)(2,1)S(1)}, u32[]{:S(2)}, u32[]{:S(2)}) collective-permute-start(bf16[4,128,512]{2,1,0:T(8,128)(2,1)S(1)} %shard_map.56.g_l.g), channel_id=1, source_target_pairs={{2,0},{5,1},{3,2},{6,4},{9,5},{7,6},{10,8},{13,9},{11,10},{14,12},... | collective-permute-start | bytes 1572872 | tf_op jit(solution)/shard_map/ppermute | solution.py:282
  9.4 24.4 %collective-permute-start.5 = (bf16[4,128,512]{2,1,0:T(8,128)(2,1)S(1)}, bf16[4,128,512]{2,1,0:T(8,128)(2,1)S(1)}, u32[]{:S(2)}, u32[]{:S(2)}) collective-permute-start(bf16[4,128,512]{2,1,0:T(8,128)(2,1)S(1)} %shard_map.56.g_l.g), channel_id=1, source_target_pairs={{1,0},{3,1},{4,2},{5,4},{7,5},{8,6},{9,8},{11,9},{12,10},{13,12},{... | collective-permute-start | bytes 1572872 | tf_op jit(solution)/shard_map/ppermute | solution.py:282
  20.4 1.9 %collective-permute-start.2 = (bf16[528,512]{1,0:T(8,128)(2,1)S(1)}, bf16[528,512]{1,0:T(8,128)(2,1)S(1)}, u32[]{:S(2)}, u32[]{:S(2)}) collective-permute-start(bf16[528,512]{1,0:T(8,128)(2,1)S(1)} %collective-permute-done.1.um), channel_id=1, source_target_pairs={{0,16},{16,0},{1,17},{17,1},{2,18},{18,2},{3,19},{19,3},{4,20},{20... | collective-permute-start | bytes 1622024 | tf_op jit(solution)/shard_map/ppermute | solution.py:284
  20.4 2.7 %collective-permute-start.4 = (bf16[528,512]{1,0:T(8,128)(2,1)S(1)}, bf16[528,512]{1,0:T(8,128)(2,1)S(1)}, u32[]{:S(2)}, u32[]{:S(2)}) collective-permute-start(bf16[528,512]{1,0:T(8,128)(2,1)S(1)} %collective-permute-done.3.vm), channel_id=1, source_target_pairs={{0,16},{16,0},{1,17},{17,1},{2,18},{18,2},{3,19},{19,3},{4,20},{20... | collective-permute-start | bytes 1622024 | tf_op jit(solution)/shard_map/ppermute | solution.py:284
  30.1 14.4 %collective-permute-start.8 = (bf16[4,128,512]{2,1,0:T(8,128)(2,1)S(1)}, bf16[4,128,512]{2,1,0:T(8,128)(2,1)S(1)}, u32[]{:S(2)}, u32[]{:S(2)}) collective-permute-start(bf16[4,128,512]{2,1,0:T(8,128)(2,1)S(1)} %shard_map.60), channel_id=1, source_target_pairs={{0,1},{1,3},{2,4},{4,5},{5,7},{6,8},{8,9},{9,11},{10,12},{12,13},{... | collective-permute-start | bytes 1572872 | tf_op jit(solution)/shard_map/ppermute | solution.py:282
  34.3 13.9 %collective-permute-start.7 = (bf16[4,128,512]{2,1,0:T(8,128)(2,1)S(1)}, bf16[4,128,512]{2,1,0:T(8,128)(2,1)S(1)}, u32[]{:S(2)}, u32[]{:S(2)}) collective-permute-start(bf16[4,128,512]{2,1,0:T(8,128)(2,1)S(1)} %shard_map.59), channel_id=1, source_target_pairs={{0,2},{1,5},{2,3},{4,6},{5,9},{6,7},{8,10},{9,13},{10,11},{12,14},... | collective-permute-start | bytes 1572872 | tf_op jit(solution)/shard_map/ppermute | solution.py:282

commit v7 on v6

--- a/solution.py
+++ b/solution.py
@@ -36,18 +36,20 @@
     return parts[:, 0] + (parts[:, 1] << 8) + (parts[:, 2] << 16)
 
 
-def entries_for(own, other, place, tiles):
+def entries_for(own, other, place, core, tiles):
     r = place % 4
     first, second = (own >> 8) & 255, own >> 16
     dist = second // tiles
-    group = jnp.where(r == 0, dist, jnp.where(r == 2, 3 - dist, jnp.where((r == 1) & (dist == 2), 1, -1)))
+    group = jnp.where(r == 0, dist, jnp.where(r == 2, 3 - dist, 1))
+    group = jnp.where(core == 1, 3 - group, group)
     group = jnp.where(dist == 0, 0, group)
     entry = (own & 65535) + ((second % tiles + tiles * group) << 16)
-    near = jnp.where((own > 0) & (group >= 0), entry, 0)
+    here = (dist == 0) | (r == 0) | (r == 2) | ((r == 1) & (dist == 2))
+    near = jnp.where((own > 0) & here, entry, 0)
     first, second = (other >> 8) & 255, other >> 16
     dist = second // tiles
     second = second % tiles
-    turned = r == 2
+    turned = (r == 2) != (core == 1)
     entry = (other & 255) + jnp.where(turned, 2 * NBIN, 0)
     entry = entry + (jnp.where(turned, second, first) << 8) + (jnp.where(turned, first, second) << 16)
     far = jnp.where((other > 0) & (r != 3) & (dist == jnp.where(r == 1, 2, 1)), entry, 0)
@@ -278,8 +280,11 @@
     slots = loc_bin.shape[0]
     size = lax.axis_size("tile")
     place = lax.axis_index("tile")
-    to_u, to_v = routes(size, FROM_U), routes(size, FROM_V)
-    send = lambda x, pairs: lax.ppermute(x, "tile", pairs)
+    core = lax.axis_index("mem")
+    routes_u, routes_v = routes(size, FROM_U), routes(size, FROM_V)
+    to_u = routes_u + [(size + a, size + b) for a, b in routes_v]
+    to_v = routes_v + [(size + a, size + b) for a, b in routes_u]
+    send = lambda x, pairs: lax.ppermute(x, ("mem", "tile"), pairs)
     stay = lambda x: pltpu.with_memory_space_constraint(x, pltpu.HBM)
     swap = lambda x: lax.ppermute(x, "mem", [(0, 1), (1, 0)])
 
@@ -308,16 +313,16 @@
     )
     g_v = send(forcing, to_v)
     g_u = send(forcing, to_u)
-    other_list = jnp.where(place % 4 != 2, slot_codes(a_u, slots), slot_codes(a_v, slots))
-    near, far_slots = entries_for(slot_codes(a_l, slots), other_list, place, tiles)
+    other_list = jnp.where((place % 4 != 2) == (core == 0), slot_codes(a_u, slots), slot_codes(a_v, slots))
+    near, far_slots = entries_for(slot_codes(a_l, slots), other_list, place, core, tiles)
     square = vm((points, points), BF16)
     across = vm((points // WIDTH, points), F32)
     weights = [square, vm((NBIN, WIDTH, points), F32), across]
     weights_far = [vm((2, points, points), BF16), vm((2 * NBIN, WIDTH, points), F32), across]
     ints = pltpu.SMEM((slots,), jnp.int32)
 
-    a_vt = swap(a_v)
-    a_ut = swap(a_u)
+    a_vt = swap(a_u)
+    a_ut = swap(a_v)
     far, inc_u, inc_v = call(
         early_kernel,
         (sds((slots, points, points), BF16), sds(anomalies.shape, F32), sds(anomalies.shape, F32)),

time: 49.3 us -> 47.9 us (0.972)
  starting transfers between devices: 13.9 us -> 11.9 us
    ppermute x6, starting transfers between devices: 12.8 us -> 11.4 us  [per_device(): send = lambda x, pairs: lax.ppermute(x, ('mem', 'tile'), pairs)]
    ppermute x3, starting transfers between devices: 1.08 us -> 0.52 us  [per_device(): swap = lambda x: lax.ppermute(x, 'mem', [(0, 1), (1, 0)])]
  transfers between devices with their start and end apart: 9 -> 9, of which waited for: 6 -> 6; matrix products, arithmetic and copies ran while one was open for 1% -> 2% of each run, Pallas kernels for 24% -> 25%
where the time goes in v7:
time: 47.9 us; the launch traced here: 47.4 us
  waiting for transfers between devices  19.8 us (41%)
  Pallas kernels  14.1 us (29%)
  starting transfers between devices  11.9 us (25%)
  other arithmetic  0.73 us (2%)
  local copies, waits for them, and re-layouts  0.65 us (1%)
    ppermute x6, waiting for transfers between devices, per_device(): send = lambda x, pairs: lax.ppermute(x, ('mem', 'tile'), pairs)  17.1 us
    pallas_call x7, Pallas kernels, call(): pl.pallas_call(kernel, out_shape=outs, in_specs=[spec[p] for p in places]...  14.1 us
    ppermute x6, starting transfers between devices, per_device(): send = lambda x, pairs: lax.ppermute(x, ('mem', 'tile'), pairs)  11.4 us
    ppermute x3, waiting for transfers between devices, per_device(): swap = lambda x: lax.ppermute(x, 'mem', [(0, 1), (1, 0)])  2.75 us
  transfers between devices with their start and end apart: 9, of which 6 were waited for; matrix products, arithmetic and copies ran while one was open for 2% of the time, Pallas kernels for 25%

profile of v7, /device:TPU:0, one launch (start us, length us, event | category | flops | bytes accessed | tf_op | source)
XLA Modules:
  0.0 47.4 jit_solution(5972185466224644355)
XLA Ops:
  0.0 1.1 %shard_map.55.lm = bf16[528,512]{1,0:T(8,128)(2,1)S(1)} custom-call(s32[2,8]{1,0:T(2,128)} %bitcast.38, s32[8]{0:T(128)} %bins.1, bf16[4,128,512]{2,1,0:T(8,128)(2,1)} %anomalies.1), custom_call_target="tpu_custom_call" | custom-call | flops 10000000 | bytes 30000 | tf_op jit(solution)/shard_map/pallas_call | solution.py:267
  1.2 1.3 %collective-permute-start.2 = (bf16[528,512]{1,0:T(8,128)(2,1)S(1)}, bf16[528,512]{1,0:T(8,128)(2,1)S(1)}, u32[]{:S(2)}, u32[]{:S(2)}) collective-permute-start(bf16[528,512]{1,0:T(8,128)(2,1)S(1)} %shard_map.55.lm), channel_id=1, source_target_pairs={{2,0},{5,1},{3,2},{6,4},{9,5},{7,6},{10,8},{13,9},{11,10},{14,12},... | collective-permute-start | bytes 1622024 | tf_op jit(solution)/shard_map/ppermute | solution.py:287
  2.5 1.3 %collective-permute-start.1 = (bf16[528,512]{1,0:T(8,128)(2,1)S(1)}, bf16[528,512]{1,0:T(8,128)(2,1)S(1)}, u32[]{:S(2)}, u32[]{:S(2)}) collective-permute-start(bf16[528,512]{1,0:T(8,128)(2,1)S(1)} %shard_map.55.lm), channel_id=1, source_target_pairs={{1,0},{3,1},{4,2},{5,4},{7,5},{8,6},{9,8},{11,9},{12,10},{13,12},{... | collective-permute-start | bytes 1622024 | tf_op jit(solution)/shard_map/ppermute | solution.py:287
  3.8 0.5 %collective-permute-start = (bf16[528,512]{1,0:T(8,128)(2,1)S(1)}, bf16[528,512]{1,0:T(8,128)(2,1)S(1)}, u32[]{:S(2)}, u32[]{:S(2)}) collective-permute-start(bf16[528,512]{1,0:T(8,128)(2,1)S(1)} %shard_map.55.lm), channel_id=1, source_target_pairs={{0,16},{16,0},{1,17},{17,1},{2,18},{18,2},{3,19},{19,3},{4,20},{20... | collective-permute-start | bytes 1622024 | tf_op jit(solution)/shard_map/ppermute | solution.py:289
  4.3 0.2 shift-right-arithmetic_reduce_fusion.1
  4.5 0.1 compare_reduce_fusion
  4.6 1.2 %collective-permute-done.lt = bf16[528,512]{1,0:T(8,128)(2,1)S(1)} collective-permute-done((bf16[528,512]{1,0:T(8,128)(2,1)S(1)}, bf16[528,512]{1,0:T(8,128)(2,1)S(1)}, u32[]{:S(2)}, u32[]{:S(2)}) %collective-permute-start) | collective-permute-done | bytes 540704 | tf_op jit(solution)/shard_map/ppermute | solution.py:289
  5.8 0.0 copy-start
  5.8 0.7 %copy-done = s32[8]{0:T(128)S(1)} copy-done((s32[8]{0:T(128)S(1)}, s32[8]{0:T(128)}, u32[]{:S(2)}) %copy-start) | copy-done | bytes 56
  6.5 1.6 %shard_map.56.g_l.g = bf16[4,128,512]{2,1,0:T(8,128)(2,1)S(1)} custom-call(s32[8]{0:T(128)S(1)} %copy-done, bf16[8,128,512]{2,1,0:T(8,128)(2,1)} %innov.1), custom_call_target="tpu_custom_call" | custom-call | flops 10000000 | bytes 30000 | tf_op jit(solution)/shard_map/pallas_call | solution.py:267
  8.1 1.3 %collective-permute-start.6 = (bf16[4,128,512]{2,1,0:T(8,128)(2,1)S(1)}, bf16[4,128,512]{2,1,0:T(8,128)(2,1)S(1)}, u32[]{:S(2)}, u32[]{:S(2)}) collective-permute-start(bf16[4,128,512]{2,1,0:T(8,128)(2,1)S(1)} %shard_map.56.g_l.g), channel_id=1, source_target_pairs={{2,0},{5,1},{3,2},{6,4},{9,5},{7,6},{10,8},{13,9},{11,10},{14,12},... | collective-permute-start | bytes 1572872 | tf_op jit(solution)/shard_map/ppermute | solution.py:287
  9.4 1.3 %collective-permute-start.5 = (bf16[4,128,512]{2,1,0:T(8,128)(2,1)S(1)}, bf16[4,128,512]{2,1,0:T(8,128)(2,1)S(1)}, u32[]{:S(2)}, u32[]{:S(2)}) collective-permute-start(bf16[4,128,512]{2,1,0:T(8,128)(2,1)S(1)} %shard_map.56.g_l.g), channel_id=1, source_target_pairs={{1,0},{3,1},{4,2},{5,4},{7,5},{8,6},{9,8},{11,9},{12,10},{13,12},{... | collective-permute-start | bytes 1572872 | tf_op jit(solution)/shard_map/ppermute | solution.py:287
  10.7 8.1 %collective-permute-done.2.vm = bf16[528,512]{1,0:T(8,128)(2,1)S(1)} collective-permute-done((bf16[528,512]{1,0:T(8,128)(2,1)S(1)}, bf16[528,512]{1,0:T(8,128)(2,1)S(1)}, u32[]{:S(2)}, u32[]{:S(2)}) %collective-permute-start.2) | collective-permute-done | bytes 540704 | tf_op jit(solution)/shard_map/ppermute | solution.py:287
  18.8 0.0 collective-permute-start.3
  18.8 1.7 %collective-permute-done.1.um = bf16[528,512]{1,0:T(8,128)(2,1)S(1)} collective-permute-done((bf16[528,512]{1,0:T(8,128)(2,1)S(1)}, bf16[528,512]{1,0:T(8,128)(2,1)S(1)}, u32[]{:S(2)}, u32[]{:S(2)}) %collective-permute-start.1) | collective-permute-done | bytes 540704 | tf_op jit(solution)/shard_map/ppermute | solution.py:287
  20.5 0.0 collective-permute-start.4
  20.5 0.2 shift-right-arithmetic_reduce_fusion
  20.7 0.1 and_reduce_fusion.2
  20.9 0.0 collective-permute-done.3.ut
  20.9 1.6 %collective-permute-done.4.vt = bf16[528,512]{1,0:T(8,128)(2,1)S(1)} collective-permute-done((bf16[528,512]{1,0:T(8,128)(2,1)S(1)}, bf16[528,512]{1,0:T(8,128)(2,1)S(1)}, u32[]{:S(2)}, u32[]{:S(2)}) %collective-permute-start.4) | collective-permute-done | bytes 540704 | tf_op jit(solution)/shard_map/ppermute | solution.py:289
  22.4 2.3 %shard_map.58 = (bf16[8,512,512]{2,1,0:T(8,128)(2,1)S(1)}, f32[4,128,512]{2,1,0:T(8,128)S(1)}, f32[4,128,512]{2,1,0:T(8,128)S(1)}) custom-call(s32[1,8]{1,0:T(1,128)S(1)} %fusion.1.near, s32[1,8]{1,0:T(1,128)S(1)} %fusion.far_slots, bf16[528,512]{1,0:T(8,128)(2,1)S(1)} %shard_map.55.lm, bf16[528,512]{1,0:T(8,128)(2,1)S(1)} %collective-permute-done.lt, ...), custom_call_target="tpu_custom_call" | custom-call | flops 40000000 | bytes 120000 | tf_op jit(solution)/shard_map/pallas_call | solution.py:267
  24.7 5.3 %collective-permute-done.6.g_v.g = bf16[4,128,512]{2,1,0:T(8,128)(2,1)S(1)} collective-permute-done((bf16[4,128,512]{2,1,0:T(8,128)(2,1)S(1)}, bf16[4,128,512]{2,1,0:T(8,128)(2,1)S(1)}, u32[]{:S(2)}, u32[]{:S(2)}) %collective-permute-start.6) | collective-permute-done | bytes 524320 | tf_op jit(solution)/shard_map/ppermute | solution.py:287
  30.0 0.3 shard_map.60
  30.3 4.7 %collective-permute-start.8 = (bf16[4,128,512]{2,1,0:T(8,128)(2,1)S(1)}, bf16[4,128,512]{2,1,0:T(8,128)(2,1)S(1)}, u32[]{:S(2)}, u32[]{:S(2)}) collective-permute-start(bf16[4,128,512]{2,1,0:T(8,128)(2,1)S(1)} %shard_map.60), channel_id=1, source_target_pairs={{0,1},{1,3},{2,4},{4,5},{5,7},{6,8},{8,9},{9,11},{10,12},{12,13},{... | collective-permute-start | bytes 1572872 | tf_op jit(solution)/shard_map/ppermute | solution.py:287
  35.0 0.0 collective-permute-done.5.g_u.g
  35.0 0.3 shard_map.59
  35.3 1.6 %collective-permute-start.7 = (bf16[4,128,512]{2,1,0:T(8,128)(2,1)S(1)}, bf16[4,128,512]{2,1,0:T(8,128)(2,1)S(1)}, u32[]{:S(2)}, u32[]{:S(2)}) collective-permute-start(bf16[4,128,512]{2,1,0:T(8,128)(2,1)S(1)} %shard_map.59), channel_id=1, source_target_pairs={{0,2},{1,5},{2,3},{4,6},{5,9},{6,7},{8,10},{9,13},{10,11},{12,14},... | collective-permute-start | bytes 1572872 | tf_op jit(solution)/shard_map/ppermute | solution.py:287
  36.9 7.6 %shard_map.57.total = f32[4,128,512]{2,1,0:T(8,128)S(1)} custom-call(s32[1,8]{1,0:T(1,128)S(1)} %fusion.1.near, bf16[528,512]{1,0:T(8,128)(2,1)S(1)} %shard_map.55.lm, bf16[528,512]{1,0:T(8,128)(2,1)S(1)} %collective-permute-done.lt, bf16[528,512]{1,0:T(8,128)(2,1)S(1)} %collective-permute-done.1.um, bf16[528,512]{1,0:T(8,128)(2,1)S(1)} %collective-permute-done.3.ut, ...), custom_call_target="tpu_custom_call" | custom-call | flops 100000000 | bytes 300000 | tf_op jit(solution)/shard_map/pallas_call | solution.py:267
  44.5 2.0 %collective-permute-done.8.from_v = bf16[4,128,512]{2,1,0:T(8,128)(2,1)S(1)} collective-permute-done((bf16[4,128,512]{2,1,0:T(8,128)(2,1)S(1)}, bf16[4,128,512]{2,1,0:T(8,128)(2,1)S(1)}, u32[]{:S(2)}, u32[]{:S(2)}) %collective-permute-start.8) | collective-permute-done | bytes 524320 | tf_op jit(solution)/shard_map/ppermute | solution.py:287
  46.5 0.0 collective-permute-done.7.from_u
  46.5 0.9 %shard_map.61 = bf16[4,128,512]{2,1,0:T(8,128)(2,1)} custom-call(f32[4,128,512]{2,1,0:T(8,128)S(1)} %shard_map.57.total, bf16[4,128,512]{2,1,0:T(8,128)(2,1)S(1)} %collective-permute-done.7.from_u, bf16[4,128,512]{2,1,0:T(8,128)(2,1)S(1)} %collective-permute-done.8.from_v), custom_call_target="tpu_custom_call" | custom-call | flops 10000000 | bytes 30000 | tf_op jit(solution)/shard_map/pallas_call | solution.py:267
  (5 shorter events, 0.1 us)
Async XLA Ops:
  1.2 17.6 %collective-permute-start.2 = (bf16[528,512]{1,0:T(8,128)(2,1)S(1)}, bf16[528,512]{1,0:T(8,128)(2,1)S(1)}, u32[]{:S(2)}, u32[]{:S(2)}) collective-permute-start(bf16[528,512]{1,0:T(8,128)(2,1)S(1)} %shard_map.55.lm), channel_id=1, source_target_pairs={{2,0},{5,1},{3,2},{6,4},{9,5},{7,6},{10,8},{13,9},{11,10},{14,12},... | collective-permute-start | bytes 1622024 | tf_op jit(solution)/shard_map/ppermute | solution.py:287
  2.5 18.0 %collective-permute-start.1 = (bf16[528,512]{1,0:T(8,128)(2,1)S(1)}, bf16[528,512]{1,0:T(8,128)(2,1)S(1)}, u32[]{:S(2)}, u32[]{:S(2)}) collective-permute-start(bf16[528,512]{1,0:T(8,128)(2,1)S(1)} %shard_map.55.lm), channel_id=1, source_target_pairs={{1,0},{3,1},{4,2},{5,4},{7,5},{8,6},{9,8},{11,9},{12,10},{13,12},{... | collective-permute-start | bytes 1622024 | tf_op jit(solution)/shard_map/ppermute | solution.py:287
  3.8 2.1 %collective-permute-start = (bf16[528,512]{1,0:T(8,128)(2,1)S(1)}, bf16[528,512]{1,0:T(8,128)(2,1)S(1)}, u32[]{:S(2)}, u32[]{:S(2)}) collective-permute-start(bf16[528,512]{1,0:T(8,128)(2,1)S(1)} %shard_map.55.lm), channel_id=1, source_target_pairs={{0,16},{16,0},{1,17},{17,1},{2,18},{18,2},{3,19},{19,3},{4,20},{20... | collective-permute-start | bytes 1622024 | tf_op jit(solution)/shard_map/ppermute | solution.py:289
  5.8 0.7 %copy-start = (s32[8]{0:T(128)S(1)}, s32[8]{0:T(128)}, u32[]{:S(2)}) copy-start(s32[8]{0:T(128)} %obs) | copy-start | bytes 100
  8.1 22.0 %collective-permute-start.6 = (bf16[4,128,512]{2,1,0:T(8,128)(2,1)S(1)}, bf16[4,128,512]{2,1,0:T(8,128)(2,1)S(1)}, u32[]{:S(2)}, u32[]{:S(2)}) collective-permute-start(bf16[4,128,512]{2,1,0:T(8,128)(2,1)S(1)} %shard_map.56.g_l.g), channel_id=1, source_target_pairs={{2,0},{5,1},{3,2},{6,4},{9,5},{7,6},{10,8},{13,9},{11,10},{14,12},... | collective-permute-start | bytes 1572872 | tf_op jit(solution)/shard_map/ppermute | solution.py:287
  9.4 25.6 %collective-permute-start.5 = (bf16[4,128,512]{2,1,0:T(8,128)(2,1)S(1)}, bf16[4,128,512]{2,1,0:T(8,128)(2,1)S(1)}, u32[]{:S(2)}, u32[]{:S(2)}) collective-permute-start(bf16[4,128,512]{2,1,0:T(8,128)(2,1)S(1)} %shard_map.56.g_l.g), channel_id=1, source_target_pairs={{1,0},{3,1},{4,2},{5,4},{7,5},{8,6},{9,8},{11,9},{12,10},{13,12},{... | collective-permute-start | bytes 1572872 | tf_op jit(solution)/shard_map/ppermute | solution.py:287
  18.8 2.1 %collective-permute-start.3 = (bf16[528,512]{1,0:T(8,128)(2,1)S(1)}, bf16[528,512]{1,0:T(8,128)(2,1)S(1)}, u32[]{:S(2)}, u32[]{:S(2)}) collective-permute-start(bf16[528,512]{1,0:T(8,128)(2,1)S(1)} %collective-permute-done.2.vm), channel_id=1, source_target_pairs={{0,16},{16,0},{1,17},{17,1},{2,18},{18,2},{3,19},{19,3},{4,20},{20... | collective-permute-start | bytes 1622024 | tf_op jit(solution)/shard_map/ppermute | solution.py:289
  20.5 1.9 %collective-permute-start.4 = (bf16[528,512]{1,0:T(8,128)(2,1)S(1)}, bf16[528,512]{1,0:T(8,128)(2,1)S(1)}, u32[]{:S(2)}, u32[]{:S(2)}) collective-permute-start(bf16[528,512]{1,0:T(8,128)(2,1)S(1)} %collective-permute-done.1.um), channel_id=1, source_target_pairs={{0,16},{16,0},{1,17},{17,1},{2,18},{18,2},{3,19},{19,3},{4,20},{20... | collective-permute-start | bytes 1622024 | tf_op jit(solution)/shard_map/ppermute | solution.py:289
  30.3 16.2 %collective-permute-start.8 = (bf16[4,128,512]{2,1,0:T(8,128)(2,1)S(1)}, bf16[4,128,512]{2,1,0:T(8,128)(2,1)S(1)}, u32[]{:S(2)}, u32[]{:S(2)}) collective-permute-start(bf16[4,128,512]{2,1,0:T(8,128)(2,1)S(1)} %shard_map.60), channel_id=1, source_target_pairs={{0,1},{1,3},{2,4},{4,5},{5,7},{6,8},{8,9},{9,11},{10,12},{12,13},{... | collective-permute-start | bytes 1572872 | tf_op jit(solution)/shard_map/ppermute | solution.py:287
  35.3 11.2 %collective-permute-start.7 = (bf16[4,128,512]{2,1,0:T(8,128)(2,1)S(1)}, bf16[4,128,512]{2,1,0:T(8,128)(2,1)S(1)}, u32[]{:S(2)}, u32[]{:S(2)}) collective-permute-start(bf16[4,128,512]{2,1,0:T(8,128)(2,1)S(1)} %shard_map.59), channel_id=1, source_target_pairs={{0,2},{1,5},{2,3},{4,6},{5,9},{6,7},{8,10},{9,13},{10,11},{12,14},... | collective-permute-start | bytes 1572872 | tf_op jit(solution)/shard_map/ppermute | solution.py:287

commit v8 on v7

--- a/solution.py
+++ b/solution.py
@@ -312,7 +312,8 @@
         forcing_kernel, sds(anomalies.shape, BF16), "sv", [vm(anomalies.shape, F32)], 1, obs_tile, stay(innovations)
     )
     g_v = send(forcing, to_v)
-    g_u = send(forcing, to_u)
+    late_forcing, a_v = lax.optimization_barrier((forcing, a_v))
+    g_u = send(late_forcing, to_u)
     other_list = jnp.where((place % 4 != 2) == (core == 0), slot_codes(a_u, slots), slot_codes(a_v, slots))
     near, far_slots = entries_for(slot_codes(a_l, slots), other_list, place, core, tiles)
     square = vm((points, points), BF16)

time: 47.9 us -> 45.8 us (0.956)
  the two profiles are of different devices: /device:TPU:0 before, /device:TPU:25 now
where the time goes in v8:
time: 45.8 us; the launch traced here: 45 us
  waiting for transfers between devices  15.7 us (34%)
  starting transfers between devices  14.5 us (32%)
  Pallas kernels  13.2 us (29%)
  other arithmetic  0.73 us (2%)
  local copies, waits for them, and re-layouts  0.65 us (1%)
    ppermute x6, waiting for transfers between devices, per_device(): send = lambda x, pairs: lax.ppermute(x, ('mem', 'tile'), pairs)  14.5 us
    pallas_call x7, Pallas kernels, call(): pl.pallas_call(kernel, out_shape=outs, in_specs=[spec[p] for p in places]...  13.2 us
    ppermute x6, starting transfers between devices, per_device(): send = lambda x, pairs: lax.ppermute(x, ('mem', 'tile'), pairs)  12.7 us
    ppermute x3, starting transfers between devices, per_device(): swap = lambda x: lax.ppermute(x, 'mem', [(0, 1), (1, 0)])  1.81 us
    ppermute x3, waiting for transfers between devices, per_device(): swap = lambda x: lax.ppermute(x, 'mem', [(0, 1), (1, 0)])  1.19 us
  transfers between devices with their start and end apart: 9, of which 6 were waited for; matrix products, arithmetic and copies ran while one was open for 2% of the time, Pallas kernels for 25%

profile of v8, /device:TPU:25, one launch (start us, length us, event | category | flops | bytes accessed | tf_op | source)
XLA Modules:
  0.0 45.0 jit_solution(16205336448083725964)
XLA Ops:
  0.0 1.1 %shard_map.55.lm = bf16[528,512]{1,0:T(8,128)(2,1)S(1)} custom-call(s32[2,8]{1,0:T(2,128)} %bitcast.38, s32[8]{0:T(128)} %bins.1, bf16[4,128,512]{2,1,0:T(8,128)(2,1)} %anomalies.1), custom_call_target="tpu_custom_call" | custom-call | flops 10000000 | bytes 30000 | tf_op jit(solution)/shard_map/pallas_call | solution.py:267
  1.2 0.7 %collective-permute-start = (bf16[528,512]{1,0:T(8,128)(2,1)S(1)}, bf16[528,512]{1,0:T(8,128)(2,1)S(1)}, u32[]{:S(2)}, u32[]{:S(2)}) collective-permute-start(bf16[528,512]{1,0:T(8,128)(2,1)S(1)} %shard_map.55.lm), channel_id=1, source_target_pairs={{0,16},{16,0},{1,17},{17,1},{2,18},{18,2},{3,19},{19,3},{4,20},{20... | collective-permute-start | bytes 1622024 | tf_op jit(solution)/shard_map/ppermute | solution.py:289
  1.9 3.0 %collective-permute-start.2 = (bf16[528,512]{1,0:T(8,128)(2,1)S(1)}, bf16[528,512]{1,0:T(8,128)(2,1)S(1)}, u32[]{:S(2)}, u32[]{:S(2)}) collective-permute-start(bf16[528,512]{1,0:T(8,128)(2,1)S(1)} %shard_map.55.lm), channel_id=1, source_target_pairs={{2,0},{5,1},{3,2},{6,4},{9,5},{7,6},{10,8},{13,9},{11,10},{14,12},... | collective-permute-start | bytes 1622024 | tf_op jit(solution)/shard_map/ppermute | solution.py:287
  4.9 1.3 %collective-permute-start.1 = (bf16[528,512]{1,0:T(8,128)(2,1)S(1)}, bf16[528,512]{1,0:T(8,128)(2,1)S(1)}, u32[]{:S(2)}, u32[]{:S(2)}) collective-permute-start(bf16[528,512]{1,0:T(8,128)(2,1)S(1)} %shard_map.55.lm), channel_id=1, source_target_pairs={{1,0},{3,1},{4,2},{5,4},{7,5},{8,6},{9,8},{11,9},{12,10},{13,12},{... | collective-permute-start | bytes 1622024 | tf_op jit(solution)/shard_map/ppermute | solution.py:287
  6.3 0.2 shift-right-arithmetic_reduce_fusion.1
  6.5 0.1 compare_reduce_fusion
  6.6 0.0 collective-permute-done.lt
  6.7 0.0 copy-start
  6.7 0.6 %copy-done = s32[8]{0:T(128)S(1)} copy-done((s32[8]{0:T(128)S(1)}, s32[8]{0:T(128)}, u32[]{:S(2)}) %copy-start) | copy-done | bytes 56
  7.3 1.6 %shard_map.56.g_l.g = bf16[4,128,512]{2,1,0:T(8,128)(2,1)S(1)} custom-call(s32[8]{0:T(128)S(1)} %copy-done, bf16[8,128,512]{2,1,0:T(8,128)(2,1)} %innov.1), custom_call_target="tpu_custom_call" | custom-call | flops 10000000 | bytes 30000 | tf_op jit(solution)/shard_map/pallas_call | solution.py:267
  8.9 3.9 %collective-permute-start.6 = (bf16[4,128,512]{2,1,0:T(8,128)(2,1)S(1)}, bf16[4,128,512]{2,1,0:T(8,128)(2,1)S(1)}, u32[]{:S(2)}, u32[]{:S(2)}) collective-permute-start(bf16[4,128,512]{2,1,0:T(8,128)(2,1)S(1)} %shard_map.56.g_l.g), channel_id=1, source_target_pairs={{2,0},{5,1},{3,2},{6,4},{9,5},{7,6},{10,8},{13,9},{11,10},{14,12},... | collective-permute-start | bytes 1572872 | tf_op jit(solution)/shard_map/ppermute | solution.py:287
  12.8 2.9 %collective-permute-done.2.vm = bf16[528,512]{1,0:T(8,128)(2,1)S(1)} collective-permute-done((bf16[528,512]{1,0:T(8,128)(2,1)S(1)}, bf16[528,512]{1,0:T(8,128)(2,1)S(1)}, u32[]{:S(2)}, u32[]{:S(2)}) %collective-permute-start.2) | collective-permute-done | bytes 540704 | tf_op jit(solution)/shard_map/ppermute | solution.py:287
  15.6 0.7 %collective-permute-start.3 = (bf16[528,512]{1,0:T(8,128)(2,1)S(1)}, bf16[528,512]{1,0:T(8,128)(2,1)S(1)}, u32[]{:S(2)}, u32[]{:S(2)}) collective-permute-start(bf16[528,512]{1,0:T(8,128)(2,1)S(1)} %collective-permute-done.2.vm), channel_id=1, source_target_pairs={{0,16},{16,0},{1,17},{17,1},{2,18},{18,2},{3,19},{19,3},{4,20},{20... | collective-permute-start | bytes 1622024 | tf_op jit(solution)/shard_map/ppermute | solution.py:289
  16.3 1.3 %collective-permute-start.5 = (bf16[4,128,512]{2,1,0:T(8,128)(2,1)S(1)}, bf16[4,128,512]{2,1,0:T(8,128)(2,1)S(1)}, u32[]{:S(2)}, u32[]{:S(2)}) collective-permute-start(bf16[4,128,512]{2,1,0:T(8,128)(2,1)S(1)} %shard_map.56.g_l.g), channel_id=1, source_target_pairs={{1,0},{3,1},{4,2},{5,4},{7,5},{8,6},{9,8},{11,9},{12,10},{13,12},{... | collective-permute-start | bytes 1572872 | tf_op jit(solution)/shard_map/ppermute | solution.py:287
  17.6 3.5 %collective-permute-done.1.um = bf16[528,512]{1,0:T(8,128)(2,1)S(1)} collective-permute-done((bf16[528,512]{1,0:T(8,128)(2,1)S(1)}, bf16[528,512]{1,0:T(8,128)(2,1)S(1)}, u32[]{:S(2)}, u32[]{:S(2)}) %collective-permute-start.1) | collective-permute-done | bytes 540704 | tf_op jit(solution)/shard_map/ppermute | solution.py:287
  21.2 0.4 collective-permute-start.4
  21.6 0.2 shift-right-arithmetic_reduce_fusion
  21.8 0.1 and_reduce_fusion.2
  21.9 0.0 collective-permute-done.3.ut
  21.9 1.2 %collective-permute-done.4.vt = bf16[528,512]{1,0:T(8,128)(2,1)S(1)} collective-permute-done((bf16[528,512]{1,0:T(8,128)(2,1)S(1)}, bf16[528,512]{1,0:T(8,128)(2,1)S(1)}, u32[]{:S(2)}, u32[]{:S(2)}) %collective-permute-start.4) | collective-permute-done | bytes 540704 | tf_op jit(solution)/shard_map/ppermute | solution.py:289
  23.1 2.6 %shard_map.58 = (bf16[8,512,512]{2,1,0:T(8,128)(2,1)S(1)}, f32[4,128,512]{2,1,0:T(8,128)S(1)}, f32[4,128,512]{2,1,0:T(8,128)S(1)}) custom-call(s32[1,8]{1,0:T(1,128)S(1)} %fusion.1.near, s32[1,8]{1,0:T(1,128)S(1)} %fusion.far_slots, bf16[528,512]{1,0:T(8,128)(2,1)S(1)} %shard_map.55.lm, bf16[528,512]{1,0:T(8,128)(2,1)S(1)} %collective-permute-done.lt, ...), custom_call_target="tpu_custom_call" | custom-call | flops 40000000 | bytes 120000 | tf_op jit(solution)/shard_map/pallas_call | solution.py:267
  25.7 0.2 collective-permute-done.6.g_v.g
  25.9 1.1 %shard_map.60 = bf16[4,128,512]{2,1,0:T(8,128)(2,1)S(1)} custom-call(s32[1,8]{1,0:T(1,128)S(1)} %fusion.far_slots, bf16[8,512,512]{2,1,0:T(8,128)(2,1)S(1)} %get-tuple-element.16.far, f32[4,128,512]{2,1,0:T(8,128)S(1)} %get-tuple-element.18.inc, bf16[4,128,512]{2,1,0:T(8,128)(2,1)S(1)} %collective-permute-done.6.g_v.g), custom_call_target="tpu_custom_call" | custom-call | flops 10000000 | bytes 30000 | tf_op jit(solution)/shard_map/pallas_call | solution.py:267
  27.0 1.3 %collective-permute-start.8 = (bf16[4,128,512]{2,1,0:T(8,128)(2,1)S(1)}, bf16[4,128,512]{2,1,0:T(8,128)(2,1)S(1)}, u32[]{:S(2)}, u32[]{:S(2)}) collective-permute-start(bf16[4,128,512]{2,1,0:T(8,128)(2,1)S(1)} %shard_map.60), channel_id=1, source_target_pairs={{0,1},{1,3},{2,4},{4,5},{5,7},{6,8},{8,9},{9,11},{10,12},{12,13},{... | collective-permute-start | bytes 1572872 | tf_op jit(solution)/shard_map/ppermute | solution.py:287
  28.3 1.2 %collective-permute-done.5.g_u.g = bf16[4,128,512]{2,1,0:T(8,128)(2,1)S(1)} collective-permute-done((bf16[4,128,512]{2,1,0:T(8,128)(2,1)S(1)}, bf16[4,128,512]{2,1,0:T(8,128)(2,1)S(1)}, u32[]{:S(2)}, u32[]{:S(2)}) %collective-permute-start.5) | collective-permute-done | bytes 524320 | tf_op jit(solution)/shard_map/ppermute | solution.py:287
  29.5 0.8 %shard_map.59 = bf16[4,128,512]{2,1,0:T(8,128)(2,1)S(1)} custom-call(s32[1,8]{1,0:T(1,128)S(1)} %fusion.far_slots, bf16[8,512,512]{2,1,0:T(8,128)(2,1)S(1)} %get-tuple-element.16.far, f32[4,128,512]{2,1,0:T(8,128)S(1)} %get-tuple-element.17.inc, bf16[4,128,512]{2,1,0:T(8,128)(2,1)S(1)} %collective-permute-done.5.g_u.g), custom_call_target="tpu_custom_call" | custom-call | flops 10000000 | bytes 30000 | tf_op jit(solution)/shard_map/pallas_call | solution.py:267
  30.3 1.9 %collective-permute-start.7 = (bf16[4,128,512]{2,1,0:T(8,128)(2,1)S(1)}, bf16[4,128,512]{2,1,0:T(8,128)(2,1)S(1)}, u32[]{:S(2)}, u32[]{:S(2)}) collective-permute-start(bf16[4,128,512]{2,1,0:T(8,128)(2,1)S(1)} %shard_map.59), channel_id=1, source_target_pairs={{0,2},{1,5},{2,3},{4,6},{5,9},{6,7},{8,10},{9,13},{10,11},{12,14},... | collective-permute-start | bytes 1572872 | tf_op jit(solution)/shard_map/ppermute | solution.py:287
  32.2 5.1 %shard_map.57.total = f32[4,128,512]{2,1,0:T(8,128)S(1)} custom-call(s32[1,8]{1,0:T(1,128)S(1)} %fusion.1.near, bf16[528,512]{1,0:T(8,128)(2,1)S(1)} %shard_map.55.lm, bf16[528,512]{1,0:T(8,128)(2,1)S(1)} %collective-permute-done.lt, bf16[528,512]{1,0:T(8,128)(2,1)S(1)} %collective-permute-done.1.um, bf16[528,512]{1,0:T(8,128)(2,1)S(1)} %collective-permute-done.3.ut, ...), custom_call_target="tpu_custom_call" | custom-call | flops 100000000 | bytes 300000 | tf_op jit(solution)/shard_map/pallas_call | solution.py:267
  37.4 0.0 collective-permute-done.8.from_v
  37.4 6.7 %collective-permute-done.7.from_u = bf16[4,128,512]{2,1,0:T(8,128)(2,1)S(1)} collective-permute-done((bf16[4,128,512]{2,1,0:T(8,128)(2,1)S(1)}, bf16[4,128,512]{2,1,0:T(8,128)(2,1)S(1)}, u32[]{:S(2)}, u32[]{:S(2)}) %collective-permute-start.7) | collective-permute-done | bytes 524320 | tf_op jit(solution)/shard_map/ppermute | solution.py:287
  44.1 0.9 %shard_map.61 = bf16[4,128,512]{2,1,0:T(8,128)(2,1)} custom-call(f32[4,128,512]{2,1,0:T(8,128)S(1)} %shard_map.57.total, bf16[4,128,512]{2,1,0:T(8,128)(2,1)S(1)} %collective-permute-done.7.from_u, bf16[4,128,512]{2,1,0:T(8,128)(2,1)S(1)} %collective-permute-done.8.from_v), custom_call_target="tpu_custom_call" | custom-call | flops 10000000 | bytes 30000 | tf_op jit(solution)/shard_map/pallas_call | solution.py:267
  (5 shorter events, 0.1 us)
Async XLA Ops:
  1.2 5.5 %collective-permute-start = (bf16[528,512]{1,0:T(8,128)(2,1)S(1)}, bf16[528,512]{1,0:T(8,128)(2,1)S(1)}, u32[]{:S(2)}, u32[]{:S(2)}) collective-permute-start(bf16[528,512]{1,0:T(8,128)(2,1)S(1)} %shard_map.55.lm), channel_id=1, source_target_pairs={{0,16},{16,0},{1,17},{17,1},{2,18},{18,2},{3,19},{19,3},{4,20},{20... | collective-permute-start | bytes 1622024 | tf_op jit(solution)/shard_map/ppermute | solution.py:289
  1.9 13.8 %collective-permute-start.2 = (bf16[528,512]{1,0:T(8,128)(2,1)S(1)}, bf16[528,512]{1,0:T(8,128)(2,1)S(1)}, u32[]{:S(2)}, u32[]{:S(2)}) collective-permute-start(bf16[528,512]{1,0:T(8,128)(2,1)S(1)} %shard_map.55.lm), channel_id=1, source_target_pairs={{2,0},{5,1},{3,2},{6,4},{9,5},{7,6},{10,8},{13,9},{11,10},{14,12},... | collective-permute-start | bytes 1622024 | tf_op jit(solution)/shard_map/ppermute | solution.py:287
  4.9 16.2 %collective-permute-start.1 = (bf16[528,512]{1,0:T(8,128)(2,1)S(1)}, bf16[528,512]{1,0:T(8,128)(2,1)S(1)}, u32[]{:S(2)}, u32[]{:S(2)}) collective-permute-start(bf16[528,512]{1,0:T(8,128)(2,1)S(1)} %shard_map.55.lm), channel_id=1, source_target_pairs={{1,0},{3,1},{4,2},{5,4},{7,5},{8,6},{9,8},{11,9},{12,10},{13,12},{... | collective-permute-start | bytes 1622024 | tf_op jit(solution)/shard_map/ppermute | solution.py:287
  6.7 0.7 %copy-start = (s32[8]{0:T(128)S(1)}, s32[8]{0:T(128)}, u32[]{:S(2)}) copy-start(s32[8]{0:T(128)} %obs) | copy-start | bytes 100
  8.9 17.0 %collective-permute-start.6 = (bf16[4,128,512]{2,1,0:T(8,128)(2,1)S(1)}, bf16[4,128,512]{2,1,0:T(8,128)(2,1)S(1)}, u32[]{:S(2)}, u32[]{:S(2)}) collective-permute-start(bf16[4,128,512]{2,1,0:T(8,128)(2,1)S(1)} %shard_map.56.g_l.g), channel_id=1, source_target_pairs={{2,0},{5,1},{3,2},{6,4},{9,5},{7,6},{10,8},{13,9},{11,10},{14,12},... | collective-permute-start | bytes 1572872 | tf_op jit(solution)/shard_map/ppermute | solution.py:287
  15.6 6.3 %collective-permute-start.3 = (bf16[528,512]{1,0:T(8,128)(2,1)S(1)}, bf16[528,512]{1,0:T(8,128)(2,1)S(1)}, u32[]{:S(2)}, u32[]{:S(2)}) collective-permute-start(bf16[528,512]{1,0:T(8,128)(2,1)S(1)} %collective-permute-done.2.vm), channel_id=1, source_target_pairs={{0,16},{16,0},{1,17},{17,1},{2,18},{18,2},{3,19},{19,3},{4,20},{20... | collective-permute-start | bytes 1622024 | tf_op jit(solution)/shard_map/ppermute | solution.py:289
  16.3 13.2 %collective-permute-start.5 = (bf16[4,128,512]{2,1,0:T(8,128)(2,1)S(1)}, bf16[4,128,512]{2,1,0:T(8,128)(2,1)S(1)}, u32[]{:S(2)}, u32[]{:S(2)}) collective-permute-start(bf16[4,128,512]{2,1,0:T(8,128)(2,1)S(1)} %shard_map.56.g_l.g), channel_id=1, source_target_pairs={{1,0},{3,1},{4,2},{5,4},{7,5},{8,6},{9,8},{11,9},{12,10},{13,12},{... | collective-permute-start | bytes 1572872 | tf_op jit(solution)/shard_map/ppermute | solution.py:287
  21.2 2.0 %collective-permute-start.4 = (bf16[528,512]{1,0:T(8,128)(2,1)S(1)}, bf16[528,512]{1,0:T(8,128)(2,1)S(1)}, u32[]{:S(2)}, u32[]{:S(2)}) collective-permute-start(bf16[528,512]{1,0:T(8,128)(2,1)S(1)} %collective-permute-done.1.um), channel_id=1, source_target_pairs={{0,16},{16,0},{1,17},{17,1},{2,18},{18,2},{3,19},{19,3},{4,20},{20... | collective-permute-start | bytes 1622024 | tf_op jit(solution)/shard_map/ppermute | solution.py:289
  27.0 10.4 %collective-permute-start.8 = (bf16[4,128,512]{2,1,0:T(8,128)(2,1)S(1)}, bf16[4,128,512]{2,1,0:T(8,128)(2,1)S(1)}, u32[]{:S(2)}, u32[]{:S(2)}) collective-permute-start(bf16[4,128,512]{2,1,0:T(8,128)(2,1)S(1)} %shard_map.60), channel_id=1, source_target_pairs={{0,1},{1,3},{2,4},{4,5},{5,7},{6,8},{8,9},{9,11},{10,12},{12,13},{... | collective-permute-start | bytes 1572872 | tf_op jit(solution)/shard_map/ppermute | solution.py:287
  30.3 13.8 %collective-permute-start.7 = (bf16[4,128,512]{2,1,0:T(8,128)(2,1)S(1)}, bf16[4,128,512]{2,1,0:T(8,128)(2,1)S(1)}, u32[]{:S(2)}, u32[]{:S(2)}) collective-permute-start(bf16[4,128,512]{2,1,0:T(8,128)(2,1)S(1)} %shard_map.59), channel_id=1, source_target_pairs={{0,2},{1,5},{2,3},{4,6},{5,9},{6,7},{8,10},{9,13},{10,11},{12,14},... | collective-permute-start | bytes 1572872 | tf_op jit(solution)/shard_map/ppermute | solution.py:287

commit v9 on v8

--- a/solution.py
+++ b/solution.py
@@ -220,36 +220,41 @@
     out[...] = total[...].astype(BF16)
 
 
-def late_kernel(near, lm, lt, um, ut, vm, vt, g_l, g_u, g_v, out, c, along, across, near_s):
-    read_slots(near, near_s)
+def late_kernel(near, lm, lt, um, ut, vm, vt, g_l, g_u, g_v, out, c, along, across, ints, kept):
     tiles, members, points = g_l.shape
+    read_slots(near, ints)
     fill_weights(along, across, points)
 
-    def own(t, carry):
-        covariance((lm, lt), (lm, lt), t, t, along[0], across, c)
-        rows = pl.ds(pl.multiple_of(t * members, members), members)
-        out[t] = lm[rows, :].astype(F32) + to_first(g_l[t], c[...])
+    def own(k, carry):
+        for q in range(2):
+            covariance((lm, lt), (lm, lt), 2 * k + q, 2 * k + q, along[0], across, c.at[q])
+        for q in range(2):
+            t = 2 * k + q
+            rows = pl.ds(pl.multiple_of(t * members, members), members)
+            out[t] = lm[rows, :].astype(F32) + to_first(g_l[t], c[q])
         return carry
 
-    lax.fori_loop(0, tiles, own, 0)
-
-    def pair(k, carry):
-        entry = near_s[k]
-        bins, first, second = decode(entry)
-
-        for group, (right, g) in enumerate((((lm, lt), g_l), ((um, ut), g_u), ((vm, vt), g_v))):
-            here = second - group * tiles
-
-            @pl.when((entry > 0) & (here >= 0) & (here < tiles))
-            def _():
-                covariance((lm, lt), right, first, here, along[bins], across, c)
-                out[first] = out[first] + to_first(g[here], c[...])
-                if group == 0:
-                    out[here] = out[here] + to_second(g_l[first], c[...])
-
-        return carry
-
-    lax.fori_loop(0, near.shape[1], pair, 0)
+    lax.fori_loop(0, tiles // 2, own, 0)
+
+    for group, right, g in ((0, (lm, lt), g_l), (1, (um, ut), g_u), (2, (vm, vt), g_v)):
+
+        def wanted(entry):
+            _, _, second = decode(entry)
+            return (entry > 0) & (second >= group * tiles) & (second < (group + 1) * tiles)
+
+        def step(indices):
+            pairs = [decode(kept[k]) for k in indices]
+            for q, (bins, first, second) in enumerate(pairs):
+                covariance((lm, lt), right, first, second - group * tiles, along[bins], across, c.at[q])
+            parts = [to_first(g[second - group * tiles], c[q]) for q, (_, _, second) in enumerate(pairs)]
+            places = [first for _, first, _ in pairs]
+            if group == 0:
+                parts += [to_second(g_l[first], c[q]) for q, (_, first, _) in enumerate(pairs)]
+                places += [second for _, _, second in pairs]
+            for part, here in zip(parts, places):
+                out[here] = out[here] + part
+
+        in_twos(compact(ints, wanted, kept), step)
 
 
 def final_kernel(total, from_u, from_v, out, done, sems):
@@ -357,7 +362,7 @@
         late_kernel,
         sds(anomalies.shape, F32),
         "vvvvvvvvvv",
-        [*weights, ints],
+        [vm((2, points, points), BF16), *weights[1:], ints, ints],
         10,
         near,
         a_l,

time: 45.8 us -> 45.5 us (level)
  the two profiles are of different devices: /device:TPU:25 before, /device:TPU:11 now
where the time goes in v9:
time: 45.5 us
  starting transfers between devices  16.9 us (37%)
  waiting for transfers between devices  14 us (31%)
  Pallas kernels  13 us (29%)
  other arithmetic  0.73 us (2%)
  local copies, waits for them, and re-layouts  0.65 us (1%)
    ppermute x6, starting transfers between devices, per_device(): send = lambda x, pairs: lax.ppermute(x, ('mem', 'tile'), pairs)  13.1 us
    pallas_call x7, Pallas kernels, call(): pl.pallas_call(kernel, out_shape=outs, in_specs=[spec[p] for p in places]...  13 us
    ppermute x6, waiting for transfers between devices, per_device(): send = lambda x, pairs: lax.ppermute(x, ('mem', 'tile'), pairs)  12.8 us
    ppermute x3, starting transfers between devices, per_device(): swap = lambda x: lax.ppermute(x, 'mem', [(0, 1), (1, 0)])  3.86 us
    ppermute x3, waiting for transfers between devices, per_device(): swap = lambda x: lax.ppermute(x, 'mem', [(0, 1), (1, 0)])  1.19 us
  transfers between devices with their start and end apart: 9, of which 5 were waited for; matrix products, arithmetic and copies ran while one was open for 2% of the time, Pallas kernels for 24%

profile of v9, /device:TPU:11, one launch (start us, length us, event | category | flops | bytes accessed | tf_op | source)
XLA Modules:
  0.0 45.5 jit_solution(14368318021685289877)
XLA Ops:
  0.0 1.1 %shard_map.55.lm = bf16[528,512]{1,0:T(8,128)(2,1)S(1)} custom-call(s32[2,8]{1,0:T(2,128)} %bitcast.38, s32[8]{0:T(128)} %bins.1, bf16[4,128,512]{2,1,0:T(8,128)(2,1)} %anomalies.1), custom_call_target="tpu_custom_call" | custom-call | flops 10000000 | bytes 30000 | tf_op jit(solution)/shard_map/pallas_call | solution.py:272
  1.2 0.7 %collective-permute-start = (bf16[528,512]{1,0:T(8,128)(2,1)S(1)}, bf16[528,512]{1,0:T(8,128)(2,1)S(1)}, u32[]{:S(2)}, u32[]{:S(2)}) collective-permute-start(bf16[528,512]{1,0:T(8,128)(2,1)S(1)} %shard_map.55.lm), channel_id=1, source_target_pairs={{0,16},{16,0},{1,17},{17,1},{2,18},{18,2},{3,19},{19,3},{4,20},{20... | collective-permute-start | bytes 1622024 | tf_op jit(solution)/shard_map/ppermute | solution.py:294
  1.9 2.2 %collective-permute-start.2 = (bf16[528,512]{1,0:T(8,128)(2,1)S(1)}, bf16[528,512]{1,0:T(8,128)(2,1)S(1)}, u32[]{:S(2)}, u32[]{:S(2)}) collective-permute-start(bf16[528,512]{1,0:T(8,128)(2,1)S(1)} %shard_map.55.lm), channel_id=1, source_target_pairs={{2,0},{5,1},{3,2},{6,4},{9,5},{7,6},{10,8},{13,9},{11,10},{14,12},... | collective-permute-start | bytes 1622024 | tf_op jit(solution)/shard_map/ppermute | solution.py:292
  4.1 1.9 %collective-permute-start.1 = (bf16[528,512]{1,0:T(8,128)(2,1)S(1)}, bf16[528,512]{1,0:T(8,128)(2,1)S(1)}, u32[]{:S(2)}, u32[]{:S(2)}) collective-permute-start(bf16[528,512]{1,0:T(8,128)(2,1)S(1)} %shard_map.55.lm), channel_id=1, source_target_pairs={{1,0},{3,1},{4,2},{5,4},{7,5},{8,6},{9,8},{11,9},{12,10},{13,12},{... | collective-permute-start | bytes 1622024 | tf_op jit(solution)/shard_map/ppermute | solution.py:292
  6.0 0.2 shift-right-arithmetic_reduce_fusion.1
  6.3 0.1 compare_reduce_fusion
  6.4 0.0 collective-permute-done.lt
  6.4 0.0 copy-start
  6.4 0.6 %copy-done = s32[8]{0:T(128)S(1)} copy-done((s32[8]{0:T(128)S(1)}, s32[8]{0:T(128)}, u32[]{:S(2)}) %copy-start) | copy-done | bytes 56
  7.1 1.6 %shard_map.56.g_l.g = bf16[4,128,512]{2,1,0:T(8,128)(2,1)S(1)} custom-call(s32[8]{0:T(128)S(1)} %copy-done, bf16[8,128,512]{2,1,0:T(8,128)(2,1)} %innov.1), custom_call_target="tpu_custom_call" | custom-call | flops 10000000 | bytes 30000 | tf_op jit(solution)/shard_map/pallas_call | solution.py:272
  8.6 2.4 %collective-permute-start.6 = (bf16[4,128,512]{2,1,0:T(8,128)(2,1)S(1)}, bf16[4,128,512]{2,1,0:T(8,128)(2,1)S(1)}, u32[]{:S(2)}, u32[]{:S(2)}) collective-permute-start(bf16[4,128,512]{2,1,0:T(8,128)(2,1)S(1)} %shard_map.56.g_l.g), channel_id=1, source_target_pairs={{2,0},{5,1},{3,2},{6,4},{9,5},{7,6},{10,8},{13,9},{11,10},{14,12},... | collective-permute-start | bytes 1572872 | tf_op jit(solution)/shard_map/ppermute | solution.py:292
  11.1 4.1 %collective-permute-done.2.vm = bf16[528,512]{1,0:T(8,128)(2,1)S(1)} collective-permute-done((bf16[528,512]{1,0:T(8,128)(2,1)S(1)}, bf16[528,512]{1,0:T(8,128)(2,1)S(1)}, u32[]{:S(2)}, u32[]{:S(2)}) %collective-permute-start.2) | collective-permute-done | bytes 540704 | tf_op jit(solution)/shard_map/ppermute | solution.py:292
  15.2 2.0 %collective-permute-start.3 = (bf16[528,512]{1,0:T(8,128)(2,1)S(1)}, bf16[528,512]{1,0:T(8,128)(2,1)S(1)}, u32[]{:S(2)}, u32[]{:S(2)}) collective-permute-start(bf16[528,512]{1,0:T(8,128)(2,1)S(1)} %collective-permute-done.2.vm), channel_id=1, source_target_pairs={{0,16},{16,0},{1,17},{17,1},{2,18},{18,2},{3,19},{19,3},{4,20},{20... | collective-permute-start | bytes 1622024 | tf_op jit(solution)/shard_map/ppermute | solution.py:294
  17.2 2.2 %collective-permute-start.5 = (bf16[4,128,512]{2,1,0:T(8,128)(2,1)S(1)}, bf16[4,128,512]{2,1,0:T(8,128)(2,1)S(1)}, u32[]{:S(2)}, u32[]{:S(2)}) collective-permute-start(bf16[4,128,512]{2,1,0:T(8,128)(2,1)S(1)} %shard_map.56.g_l.g), channel_id=1, source_target_pairs={{1,0},{3,1},{4,2},{5,4},{7,5},{8,6},{9,8},{11,9},{12,10},{13,12},{... | collective-permute-start | bytes 1572872 | tf_op jit(solution)/shard_map/ppermute | solution.py:292
  19.4 0.9 %collective-permute-done.1.um = bf16[528,512]{1,0:T(8,128)(2,1)S(1)} collective-permute-done((bf16[528,512]{1,0:T(8,128)(2,1)S(1)}, bf16[528,512]{1,0:T(8,128)(2,1)S(1)}, u32[]{:S(2)}, u32[]{:S(2)}) %collective-permute-start.1) | collective-permute-done | bytes 540704 | tf_op jit(solution)/shard_map/ppermute | solution.py:292
  20.3 1.1 %collective-permute-start.4 = (bf16[528,512]{1,0:T(8,128)(2,1)S(1)}, bf16[528,512]{1,0:T(8,128)(2,1)S(1)}, u32[]{:S(2)}, u32[]{:S(2)}) collective-permute-start(bf16[528,512]{1,0:T(8,128)(2,1)S(1)} %collective-permute-done.1.um), channel_id=1, source_target_pairs={{0,16},{16,0},{1,17},{17,1},{2,18},{18,2},{3,19},{19,3},{4,20},{20... | collective-permute-start | bytes 1622024 | tf_op jit(solution)/shard_map/ppermute | solution.py:294
  21.4 0.2 shift-right-arithmetic_reduce_fusion
  21.6 0.1 and_reduce_fusion.2
  21.7 0.0 collective-permute-done.3.ut
  21.8 1.2 %collective-permute-done.4.vt = bf16[528,512]{1,0:T(8,128)(2,1)S(1)} collective-permute-done((bf16[528,512]{1,0:T(8,128)(2,1)S(1)}, bf16[528,512]{1,0:T(8,128)(2,1)S(1)}, u32[]{:S(2)}, u32[]{:S(2)}) %collective-permute-start.4) | collective-permute-done | bytes 540704 | tf_op jit(solution)/shard_map/ppermute | solution.py:294
  22.9 2.7 %shard_map.58 = (bf16[8,512,512]{2,1,0:T(8,128)(2,1)S(1)}, f32[4,128,512]{2,1,0:T(8,128)S(1)}, f32[4,128,512]{2,1,0:T(8,128)S(1)}) custom-call(s32[1,8]{1,0:T(1,128)S(1)} %fusion.1.near, s32[1,8]{1,0:T(1,128)S(1)} %fusion.far_slots, bf16[528,512]{1,0:T(8,128)(2,1)S(1)} %shard_map.55.lm, bf16[528,512]{1,0:T(8,128)(2,1)S(1)} %collective-permute-done.lt, ...), custom_call_target="tpu_custom_call" | custom-call | flops 40000000 | bytes 120000 | tf_op jit(solution)/shard_map/pallas_call | solution.py:272
  25.7 0.0 collective-permute-done.6.g_v.g
  25.7 1.7 %shard_map.60 = bf16[4,128,512]{2,1,0:T(8,128)(2,1)S(1)} custom-call(s32[1,8]{1,0:T(1,128)S(1)} %fusion.far_slots, bf16[8,512,512]{2,1,0:T(8,128)(2,1)S(1)} %get-tuple-element.16.far, f32[4,128,512]{2,1,0:T(8,128)S(1)} %get-tuple-element.18.inc, bf16[4,128,512]{2,1,0:T(8,128)(2,1)S(1)} %collective-permute-done.6.g_v.g), custom_call_target="tpu_custom_call" | custom-call | flops 10000000 | bytes 30000 | tf_op jit(solution)/shard_map/pallas_call | solution.py:272
  27.4 2.4 %collective-permute-start.8 = (bf16[4,128,512]{2,1,0:T(8,128)(2,1)S(1)}, bf16[4,128,512]{2,1,0:T(8,128)(2,1)S(1)}, u32[]{:S(2)}, u32[]{:S(2)}) collective-permute-start(bf16[4,128,512]{2,1,0:T(8,128)(2,1)S(1)} %shard_map.60), channel_id=1, source_target_pairs={{0,1},{1,3},{2,4},{4,5},{5,7},{6,8},{8,9},{9,11},{10,12},{12,13},{... | collective-permute-start | bytes 1572872 | tf_op jit(solution)/shard_map/ppermute | solution.py:292
  29.9 0.0 collective-permute-done.5.g_u.g
  29.9 1.2 %shard_map.59 = bf16[4,128,512]{2,1,0:T(8,128)(2,1)S(1)} custom-call(s32[1,8]{1,0:T(1,128)S(1)} %fusion.far_slots, bf16[8,512,512]{2,1,0:T(8,128)(2,1)S(1)} %get-tuple-element.16.far, f32[4,128,512]{2,1,0:T(8,128)S(1)} %get-tuple-element.17.inc, bf16[4,128,512]{2,1,0:T(8,128)(2,1)S(1)} %collective-permute-done.5.g_u.g), custom_call_target="tpu_custom_call" | custom-call | flops 10000000 | bytes 30000 | tf_op jit(solution)/shard_map/pallas_call | solution.py:272
  31.1 1.9 %collective-permute-start.7 = (bf16[4,128,512]{2,1,0:T(8,128)(2,1)S(1)}, bf16[4,128,512]{2,1,0:T(8,128)(2,1)S(1)}, u32[]{:S(2)}, u32[]{:S(2)}) collective-permute-start(bf16[4,128,512]{2,1,0:T(8,128)(2,1)S(1)} %shard_map.59), channel_id=1, source_target_pairs={{0,2},{1,5},{2,3},{4,6},{5,9},{6,7},{8,10},{9,13},{10,11},{12,14},... | collective-permute-start | bytes 1572872 | tf_op jit(solution)/shard_map/ppermute | solution.py:292
  33.0 3.8 %shard_map.57.total = f32[4,128,512]{2,1,0:T(8,128)S(1)} custom-call(s32[1,8]{1,0:T(1,128)S(1)} %fusion.1.near, bf16[528,512]{1,0:T(8,128)(2,1)S(1)} %shard_map.55.lm, bf16[528,512]{1,0:T(8,128)(2,1)S(1)} %collective-permute-done.lt, bf16[528,512]{1,0:T(8,128)(2,1)S(1)} %collective-permute-done.1.um, bf16[528,512]{1,0:T(8,128)(2,1)S(1)} %collective-permute-done.3.ut, ...), custom_call_target="tpu_custom_call" | custom-call | flops 100000000 | bytes 300000 | tf_op jit(solution)/shard_map/pallas_call | solution.py:272
  36.8 1.6 %collective-permute-done.8.from_v = bf16[4,128,512]{2,1,0:T(8,128)(2,1)S(1)} collective-permute-done((bf16[4,128,512]{2,1,0:T(8,128)(2,1)S(1)}, bf16[4,128,512]{2,1,0:T(8,128)(2,1)S(1)}, u32[]{:S(2)}, u32[]{:S(2)}) %collective-permute-start.8) | collective-permute-done | bytes 524320 | tf_op jit(solution)/shard_map/ppermute | solution.py:292
  38.4 6.2 %collective-permute-done.7.from_u = bf16[4,128,512]{2,1,0:T(8,128)(2,1)S(1)} collective-permute-done((bf16[4,128,512]{2,1,0:T(8,128)(2,1)S(1)}, bf16[4,128,512]{2,1,0:T(8,128)(2,1)S(1)}, u32[]{:S(2)}, u32[]{:S(2)}) %collective-permute-start.7) | collective-permute-done | bytes 524320 | tf_op jit(solution)/shard_map/ppermute | solution.py:292
  44.6 0.9 %shard_map.61 = bf16[4,128,512]{2,1,0:T(8,128)(2,1)} custom-call(f32[4,128,512]{2,1,0:T(8,128)S(1)} %shard_map.57.total, bf16[4,128,512]{2,1,0:T(8,128)(2,1)S(1)} %collective-permute-done.7.from_u, bf16[4,128,512]{2,1,0:T(8,128)(2,1)S(1)} %collective-permute-done.8.from_v), custom_call_target="tpu_custom_call" | custom-call | flops 10000000 | bytes 30000 | tf_op jit(solution)/shard_map/pallas_call | solution.py:272
  (5 shorter events, 0.1 us)
Async XLA Ops:
  1.2 5.3 %collective-permute-start = (bf16[528,512]{1,0:T(8,128)(2,1)S(1)}, bf16[528,512]{1,0:T(8,128)(2,1)S(1)}, u32[]{:S(2)}, u32[]{:S(2)}) collective-permute-start(bf16[528,512]{1,0:T(8,128)(2,1)S(1)} %shard_map.55.lm), channel_id=1, source_target_pairs={{0,16},{16,0},{1,17},{17,1},{2,18},{18,2},{3,19},{19,3},{4,20},{20... | collective-permute-start | bytes 1622024 | tf_op jit(solution)/shard_map/ppermute | solution.py:294
  1.9 13.3 %collective-permute-start.2 = (bf16[528,512]{1,0:T(8,128)(2,1)S(1)}, bf16[528,512]{1,0:T(8,128)(2,1)S(1)}, u32[]{:S(2)}, u32[]{:S(2)}) collective-permute-start(bf16[528,512]{1,0:T(8,128)(2,1)S(1)} %shard_map.55.lm), channel_id=1, source_target_pairs={{2,0},{5,1},{3,2},{6,4},{9,5},{7,6},{10,8},{13,9},{11,10},{14,12},... | collective-permute-start | bytes 1622024 | tf_op jit(solution)/shard_map/ppermute | solution.py:292
  4.1 16.3 %collective-permute-start.1 = (bf16[528,512]{1,0:T(8,128)(2,1)S(1)}, bf16[528,512]{1,0:T(8,128)(2,1)S(1)}, u32[]{:S(2)}, u32[]{:S(2)}) collective-permute-start(bf16[528,512]{1,0:T(8,128)(2,1)S(1)} %shard_map.55.lm), channel_id=1, source_target_pairs={{1,0},{3,1},{4,2},{5,4},{7,5},{8,6},{9,8},{11,9},{12,10},{13,12},{... | collective-permute-start | bytes 1622024 | tf_op jit(solution)/shard_map/ppermute | solution.py:292
  6.4 0.7 %copy-start = (s32[8]{0:T(128)S(1)}, s32[8]{0:T(128)}, u32[]{:S(2)}) copy-start(s32[8]{0:T(128)} %obs) | copy-start | bytes 100
  8.6 17.0 %collective-permute-start.6 = (bf16[4,128,512]{2,1,0:T(8,128)(2,1)S(1)}, bf16[4,128,512]{2,1,0:T(8,128)(2,1)S(1)}, u32[]{:S(2)}, u32[]{:S(2)}) collective-permute-start(bf16[4,128,512]{2,1,0:T(8,128)(2,1)S(1)} %shard_map.56.g_l.g), channel_id=1, source_target_pairs={{2,0},{5,1},{3,2},{6,4},{9,5},{7,6},{10,8},{13,9},{11,10},{14,12},... | collective-permute-start | bytes 1572872 | tf_op jit(solution)/shard_map/ppermute | solution.py:292
  15.2 6.6 %collective-permute-start.3 = (bf16[528,512]{1,0:T(8,128)(2,1)S(1)}, bf16[528,512]{1,0:T(8,128)(2,1)S(1)}, u32[]{:S(2)}, u32[]{:S(2)}) collective-permute-start(bf16[528,512]{1,0:T(8,128)(2,1)S(1)} %collective-permute-done.2.vm), channel_id=1, source_target_pairs={{0,16},{16,0},{1,17},{17,1},{2,18},{18,2},{3,19},{19,3},{4,20},{20... | collective-permute-start | bytes 1622024 | tf_op jit(solution)/shard_map/ppermute | solution.py:294
  17.2 12.7 %collective-permute-start.5 = (bf16[4,128,512]{2,1,0:T(8,128)(2,1)S(1)}, bf16[4,128,512]{2,1,0:T(8,128)(2,1)S(1)}, u32[]{:S(2)}, u32[]{:S(2)}) collective-permute-start(bf16[4,128,512]{2,1,0:T(8,128)(2,1)S(1)} %shard_map.56.g_l.g), channel_id=1, source_target_pairs={{1,0},{3,1},{4,2},{5,4},{7,5},{8,6},{9,8},{11,9},{12,10},{13,12},{... | collective-permute-start | bytes 1572872 | tf_op jit(solution)/shard_map/ppermute | solution.py:292
  20.3 2.6 %collective-permute-start.4 = (bf16[528,512]{1,0:T(8,128)(2,1)S(1)}, bf16[528,512]{1,0:T(8,128)(2,1)S(1)}, u32[]{:S(2)}, u32[]{:S(2)}) collective-permute-start(bf16[528,512]{1,0:T(8,128)(2,1)S(1)} %collective-permute-done.1.um), channel_id=1, source_target_pairs={{0,16},{16,0},{1,17},{17,1},{2,18},{18,2},{3,19},{19,3},{4,20},{20... | collective-permute-start | bytes 1622024 | tf_op jit(solution)/shard_map/ppermute | solution.py:294
  27.4 11.0 %collective-permute-start.8 = (bf16[4,128,512]{2,1,0:T(8,128)(2,1)S(1)}, bf16[4,128,512]{2,1,0:T(8,128)(2,1)S(1)}, u32[]{:S(2)}, u32[]{:S(2)}) collective-permute-start(bf16[4,128,512]{2,1,0:T(8,128)(2,1)S(1)} %shard_map.60), channel_id=1, source_target_pairs={{0,1},{1,3},{2,4},{4,5},{5,7},{6,8},{8,9},{9,11},{10,12},{12,13},{... | collective-permute-start | bytes 1572872 | tf_op jit(solution)/shard_map/ppermute | solution.py:292
  31.1 13.5 %collective-permute-start.7 = (bf16[4,128,512]{2,1,0:T(8,128)(2,1)S(1)}, bf16[4,128,512]{2,1,0:T(8,128)(2,1)S(1)}, u32[]{:S(2)}, u32[]{:S(2)}) collective-permute-start(bf16[4,128,512]{2,1,0:T(8,128)(2,1)S(1)} %shard_map.59), channel_id=1, source_target_pairs={{0,2},{1,5},{2,3},{4,6},{5,9},{6,7},{8,10},{9,13},{10,11},{12,14},... | collective-permute-start | bytes 1572872 | tf_op jit(solution)/shard_map/ppermute | solution.py:292
